TPU v7x, 32 devices: a whole 2x2x4 slice. The times are simulated.
32 devices in a mesh: gx: 4 (over z), gy: 4 (over x, core), ha: 2 (over y).
Axes of the slice: x: 2, y: 2, z: 4, core: 2. Of those that a mesh axis runs over, the one named last changes fastest.
Arguments:
- offsets: float32 [3, 8, 8, 4, 128], P(None, 'gx', 'gy', 'ha'), may hold values from 0 to 1
- forces: float32 [3, 8, 8, 4, 128], P(None, 'gx', 'gy', 'ha'), may hold values from -6 to 6
- counts: int32 [8, 8, 4], P('gx', 'gy', 'ha'), may hold values from 16 to 128, as said below
Outputs:
- velocity: float32 [3, 8, 8, 4, 128], P(None, 'gx', 'gy', 'ha')
Inputs may be any that keep to these rules, and one draw needn't show every extreme that they name: `counts`: A bin is heavy when its count exceeds 64. The 16 bins that two devices differing only in their ha index hold together include at most 8 heavy bins; in every draw some such pair holds exactly 8, all on one device; some bin holds exactly 128.
All inputs are finite; a program needn't handle non-finite values.
Results may differ from a plain program's by a relative error of at most 0.0003.
Values sent between devices are 32-bit elements; how exact they have to be, the bound alone decides.
No kernel may reach another device: no remote copies, remote signals or barrier semaphores. Data moves between devices by JAX's collectives and lax.ppermute only.
A program may use at most 64 MiB of HBM per device.

v0:
```python
import functools
import math

import jax
import jax.numpy as jnp
from jax import lax
from jax.experimental import pallas as pl
from jax.experimental.pallas import tpu as pltpu
from jax.sharding import PartitionSpec as P

SPLIT_XI = 2.0
SOFT_SQ = 0.01
GAUSS_COEF = 2.0 * SPLIT_XI / math.sqrt(math.pi)
STOKES_NORM = 1.0 / (8.0 * math.pi)

SOFT_U = SPLIT_XI * SPLIT_XI * SOFT_SQ
LOG2_E = math.log2(math.e)
LOG2_G = math.log2(GAUSS_COEF)
SELF_C = math.erfc(math.sqrt(SOFT_U)) / math.sqrt(SOFT_SQ) + GAUSS_COEF * (
    2.0 * SOFT_U - 3.0
) * math.exp(-SOFT_U)

LANES = 128
ROWS = 8
CHUNK = 32
UNITS = 8
COUNT_ROW = 3
FULL = 640
EARLY = 3
FIRST = (3, 4)
SECOND = (5, 6, 7, 3, 4, 0, 1, 2)
LIST_Z, LIST_X, LIST_Y = 5, 7, 10
FORCE_ROW = 4


def rows_and_lanes(shape=(ROWS, LANES)):
    return lax.broadcasted_iota(jnp.int32, shape, 0), lax.broadcasted_iota(jnp.int32, shape, 1)


def bins_of(cells):
    return [(i, j, k) for i in range(cells[0]) for j in range(cells[1]) for k in range(cells[2])]


def shift_tile(cells, at):
    row, _ = rows_and_lanes()
    moved = jnp.zeros((ROWS, LANES), jnp.float32)
    for i in range(3):
        moved = jnp.where(row == i, SPLIT_XI * (at[i] - 0.5 * (cells[i] - 1)), moved)
    return moved


def compact(listed, base, sources):
    _, lane = rows_and_lanes()
    filled = jnp.int32(0)
    moved = []
    for tile, count in sources:
        at = lax.bitwise_and(filled, LANES - 1)
        tile_id = base + lax.shift_right_logical(filled, 7)
        moved.append((pltpu.roll(tile, at, 1), lane >= at, tile_id, at + count >= LANES))
        filled = filled + count
    current = jnp.zeros((ROWS, LANES), jnp.float32)
    for tile, behind, tile_id, full in moved:
        current = jnp.where(behind, tile, current)
        spill = jnp.where(behind, 0.0, tile)
        listed[tile_id] = current
        listed[tile_id + 1] = spill
        current = jnp.where(full, spill, current)
    return filled


def up_to(count, size):
    return lax.shift_right_logical(count + (size - 1), size.bit_length() - 1)


def parts_of(value, n):
    parts = []
    for _ in range(n):
        part = value.astype(jnp.bfloat16)
        value = value - part.astype(jnp.float32)
        parts.append(part)
    return parts


def spread_targets(spread, first, tile):
    parts = [p.astype(jnp.float32) for p in parts_of(tile, 3)] + [jnp.zeros_like(tile)]
    row, lane = rows_and_lanes((4 * ROWS, 3 * LANES))
    pick = jnp.where(lax.bitwise_and(row, ROWS - 1) == lax.shift_right_logical(lane, 7), 1.0, 0.0)
    wide = lax.dot_general(
        jnp.concatenate(parts, axis=0).astype(jnp.bfloat16),
        pick.astype(jnp.bfloat16),
        (((0,), (0,)), ((), ())),
        preferred_element_type=jnp.float32,
    )
    for i in range(3):
        spread[i, first : first + LANES, :] = wide[:, i * LANES : (i + 1) * LANES]


def coefficients(target, source, force):
    delta = [t - s for t, s in zip(target, source)]
    u = (delta[0] * delta[0] + SOFT_U) + delta[1] * delta[1] + delta[2] * delta[2]
    inv = lax.rsqrt(u)
    tail = (1.0 - lax.erf(u * inv)) * inv
    gauss = jnp.exp2(LOG2_G - u * LOG2_E)
    rest = gauss * (u - 1.5)
    coef_d = ((tail - rest) - gauss) * (inv * inv)
    along = coef_d * (delta[0] * force[0] + delta[1] * force[1] + delta[2] * force[2])
    return tail + rest, along


class Groups:
    def __init__(self, tables):
        self.tables = tables
        self.size = 0
        self.total = jnp.int32(0)

    def add(self, n_chunks, n_tiles, first_tile, spread_row, acc_row):
        for table, value in zip(self.tables, (n_chunks, n_tiles, first_tile, spread_row, acc_row)):
            table[self.size] = jnp.int32(value)
        self.size += 1
        self.total = self.total + n_chunks * n_tiles

    def run(self, listed, spread, coefs, acc):
        chunks_of, tiles_of, list_of, spread_of, acc_of = self.tables
        trash = acc.shape[1] - CHUNK
        coefs[...] = jnp.zeros_like(coefs)

        def rows(tile_id, at):
            return [listed[tile_id, i : i + 1, :] for i in at]

        def advance(group, chunk, tile):
            end_tile = tile + 1 == tiles_of[group]
            next_chunk = jnp.where(end_tile, chunk + CHUNK, chunk)
            end_chunk = next_chunk == chunks_of[group] * CHUNK
            next_group = jnp.where(end_chunk, jnp.minimum(group + 1, self.size - 1), group)
            return next_group, jnp.where(end_chunk, 0, next_chunk), jnp.where(end_tile, 0, tile + 1)

        def some_units(step, state):
            place, olds = state[:3], state[3:]
            news, targets, sources = [], [], []
            for n in range(UNITS):
                group, chunk, tile = place
                valid = step * UNITS + n < self.total
                news += [jnp.where(valid, acc_of[group] + chunk, trash), list_of[group] + tile]
                at = pl.ds(pl.multiple_of(spread_of[group] + chunk, CHUNK), CHUNK)
                targets.append([spread[i, at, :] for i in range(3)])
                sources.append((rows(news[-1], (0, 1, 2)), rows(news[-1], (4, 5, 6))))
                place = advance(*place)
            old_coefs = [(coefs[n, 0], coefs[n, 1]) for n in range(UNITS)]
            old_sources = [(rows(tile, (0, 1, 2)), rows(tile, (4, 5, 6))) for tile in olds[1::2]]

            new_coefs = [coefficients(target, *source) for target, source in zip(targets, sources)]
            terms = []
            for (source, force), (coef_c, along) in zip(old_sources, old_coefs):
                terms.append([coef_c * force[i] - along * source[i] for i in range(3)] + [along])

            for first, unit in zip(olds[::2], terms):
                at = pl.ds(pl.multiple_of(first, CHUNK), CHUNK)
                for i in range(4):
                    acc[i, at, :] = acc[i, at, :] + unit[i]
            for n in range(UNITS):
                coefs[n, 0], coefs[n, 1] = new_coefs[n]
            return place + tuple(news)

        zero = jnp.int32(0)
        start = (zero, zero, zero) + (jnp.int32(trash), list_of[0]) * UNITS
        lax.fori_loop(0, lax.div(self.total + UNITS - 1, UNITS) + 1, some_units, start)


def is_full(cells, count_ref):
    filled = jnp.int32(0)
    for at in bins_of(cells):
        filled = filled + count_ref[at]
    return filled, filled > FULL


def list_own(cells, count_ref, own_ref, listed):
    sources = [(own_ref[at] + shift_tile(cells, at), count_ref[at]) for at in bins_of(cells)]
    compact(listed, 0, sources)


def velocity_rows(cells, group, by_row, tile):
    position = tile + shift_tile(cells, bins_of(cells)[group])
    return (2.0 * STOKES_NORM) * (by_row + position * jnp.broadcast_to(by_row[3:4], (ROWS, LANES)))


def lane_sums(totals):
    _, lane = rows_and_lanes((2 * LANES, LANES))
    merged = jnp.zeros(totals[0].shape, jnp.float32)
    for i, total in enumerate(totals):
        merged = merged + jnp.dot(
            jnp.concatenate(parts_of(total, 2), axis=1),
            jnp.where(lane == i, 1.0, 0.0).astype(jnp.bfloat16),
            preferred_element_type=jnp.float32,
        )
    return merged


def pack_kernel(cells, count_ref, offset_v, force_v, own_ref, early_ref, listed, spread, coefs, acc, *tables):
    slot = lax.broadcasted_iota(jnp.int32, (1, LANES), 1)
    for at in bins_of(cells):
        ix, iy, iz = at
        count = count_ref[at]
        wide = jnp.full((1, LANES), count, jnp.int32).astype(jnp.float32)
        for i in range(3):
            position = offset_v[i, ix, iy, iz : iz + 1, :]
            own_ref[ix, iy, iz, i : i + 1, :] = position * SPLIT_XI - 0.5 * SPLIT_XI
            force = force_v[i, ix, iy, iz : iz + 1, :]
            own_ref[ix, iy, iz, 4 + i : 5 + i, :] = jnp.where(slot < count, force, 0.0)
        own_ref[ix, iy, iz, 3:4, :] = wide
        own_ref[ix, iy, iz, 7:8, :] = wide
    early_ref[...] = jnp.zeros_like(early_ref)
    filled, full = is_full(cells, count_ref)

    @pl.when(full)
    def _():
        list_own(cells, count_ref, own_ref, listed)
        acc[...] = jnp.zeros_like(acc)
        groups = range(EARLY)
        tiles = [own_ref[bins_of(cells)[n]] for n in groups]
        work = Groups(tables)
        for n in groups:
            at = bins_of(cells)[n]
            spread_targets(spread, n * LANES, tiles[n] + shift_tile(cells, at))
            work.add(up_to(count_ref[at], CHUNK), up_to(filled, LANES), 0, n * LANES, n * LANES)
        work.run(listed, spread, coefs, acc)
        merged = lane_sums([acc[i, : EARLY * LANES, :] for i in range(4)])
        for n in groups:
            by_row = jnp.transpose(merged[n * LANES : (n + 1) * LANES])[:ROWS]
            early_ref[n] = velocity_rows(cells, n, by_row, tiles[n])


def counts_of(tiles, count_v, count_s, sem):
    _, lane = rows_and_lanes()
    held = jnp.zeros((ROWS, LANES), jnp.float32)
    for cell, tile in enumerate(tiles):
        held = jnp.where(lane == cell, tile, held)
    count_v[...] = held.astype(jnp.int32)
    copy = pltpu.make_async_copy(count_v, count_s, sem)
    copy.start()
    return copy


def first_kernel(cells, sent_ref, own_ref, listed, spread, acc, coefs, *refs):
    tables, (count_v, count_s, sem) = refs[:5], refs[5:]
    bins = bins_of(cells)
    copy = counts_of([sent_ref[at] for at in bins], count_v, count_s, sem)
    own_ref[...] = sent_ref[...]
    for n, at in enumerate(bins):
        spread_targets(spread, n * LANES, own_ref[at] + shift_tile(cells, at))
    acc[...] = jnp.zeros_like(acc)
    copy.wait()
    count_ref = {at: count_s[COUNT_ROW, n] for n, at in enumerate(bins)}
    list_own(cells, count_ref, own_ref, listed)
    filled, full = is_full(cells, count_ref)
    work = Groups(tables)
    for m, n in enumerate(FIRST):
        n_chunks = jnp.where(full, up_to(count_ref[bins[n]], CHUNK), 0)
        work.add(n_chunks, up_to(filled, LANES), 0, n * LANES, m * LANES)
    work.run(listed, spread, coefs, acc)


def second_kernel(cells, count_ref, other, own_list, spread, first, acc, listed, coefs, *refs):
    tables, (count_v, count_s, sem) = refs[:5], refs[5:]
    bins = bins_of(cells)
    size_x, size_y, size_z = cells
    copy = counts_of([other[at] for at in bins], count_v, count_s, sem)
    for n in range(len(bins)):
        here = slice(n * LANES, (n + 1) * LANES)
        if n in FIRST:
            m = FIRST.index(n)
            acc[:, here, :] = first[:, m * LANES : (m + 1) * LANES, :]
        else:
            acc[:, here, :] = jnp.zeros((4, LANES, LANES), jnp.float32)
    n_own = own_list.shape[0]
    for n in range(n_own):
        listed[n] = own_list[n]
    filled, full = is_full(cells, count_ref)
    copy.wait()
    work = Groups(tables)
    for bz in range(size_z):
        z = (-1, size_z)[bz]
        sources = []
        for x in range(size_x):
            for y in range(size_y):
                place = (x, y, z % size_z)
                tile = other[place] + shift_tile(cells, (x, y, z))
                sources.append((tile, count_s[COUNT_ROW, bins.index(place)]))
        first_tile = n_own + bz * LIST_Z
        n_tiles = up_to(compact(listed, first_tile, sources), LANES)
        for n, at in enumerate(bins):
            if at[2] == bz:
                work.add(up_to(count_ref[at], CHUNK), n_tiles, first_tile, n * LANES, n * LANES)
    for n in SECOND:
        n_chunks = up_to(count_ref[bins[n]], CHUNK)
        n_chunks = jnp.where(full, 0, n_chunks) if n < EARLY or n in FIRST else n_chunks
        work.add(n_chunks, up_to(filled, LANES), 0, n * LANES, n * LANES)
    work.run(listed, spread, coefs, acc)


def middle_kernel(cells, count_ref, wide, spread, second, acc, listed, coefs, *refs):
    tables, (count_v, count_s, sem) = refs[:5], refs[5:]
    size_x, size_y, size_z = cells
    n_z = 2 * size_z
    bins = bins_of(cells)
    places = [(i, j, k) for i in (0, size_x + 1) for j in range(size_y) for k in range(n_z)]
    copy = counts_of([wide[at] for at in places], count_v, count_s, sem)
    acc[...] = second[...]
    copy.wait()
    work = Groups(tables)
    for bx in range(size_x):
        for bz in range(size_z):
            x = (-1, size_x)[bx]
            sources = []
            for y in range(size_y):
                for z in (bz - 1, bz, bz + 1):
                    place = (x + 1, y, z % n_z)
                    tile = wide[place] + shift_tile(cells, (x, y, z))
                    sources.append((tile, count_s[COUNT_ROW, places.index(place)]))
            first_tile = (bx * size_z + bz) * LIST_X
            n_tiles = up_to(compact(listed, first_tile, sources), LANES)
            for n, at in enumerate(bins):
                if (at[0], at[2]) == (bx, bz):
                    work.add(up_to(count_ref[at], CHUNK), n_tiles, first_tile, n * LANES, n * LANES)
    work.run(listed, spread, coefs, acc)


def last_kernel(cells, count_ref, own_ref, y_lo, y_hi, spread, *refs):
    (middle, early, out_ref, acc, listed, coefs), refs = refs[:6], refs[6:]
    tables, (count_v, count_s, sem) = refs[:5], refs[5:]
    size_x, size_y, size_z = cells
    n_z = 2 * size_z
    bins = bins_of(cells)
    places = [(i, j, k) for i in range(size_x + 2) for j in range(2) for k in range(n_z)]
    tiles = [(y_lo, y_hi)[j][i, 0, k] for i, j, k in places]
    copy = counts_of(tiles, count_v, count_s, sem)
    acc[...] = middle[...]
    copy.wait()
    work = Groups(tables)
    for n, (bx, by, bz) in enumerate(bins):
        sources = []
        for x in (bx - 1, bx, bx + 1):
            for z in (bz - 1, bz, bz + 1):
                cell = places.index((x + 1, by, z % n_z))
                tile = tiles[cell] + shift_tile(cells, (x, (-1, size_y)[by], z))
                sources.append((tile, count_s[COUNT_ROW, cell]))
        n_tiles = up_to(compact(listed, n * LIST_Y, sources), LANES)
        work.add(up_to(count_ref[bx, by, bz], CHUNK), n_tiles, n * LIST_Y, n * LANES, n * LANES)
    work.run(listed, spread, coefs, acc)

    slot = lax.broadcasted_iota(jnp.int32, (1, LANES), 1)
    merged = lane_sums([acc[i, : len(bins) * LANES, :] for i in range(4)])
    for n, at in enumerate(bins):
        by_row = jnp.transpose(merged[n * LANES : (n + 1) * LANES])[:ROWS]
        tile = own_ref[at]
        total = velocity_rows(cells, n, by_row, tile)
        total = total - (STOKES_NORM * SELF_C) * pltpu.roll(tile, ROWS - FORCE_ROW, 0)
        if n < EARLY:
            total = total + early[n]
        total = jnp.where(slot < count_ref[at], total, 0.0)
        for i in range(3):
            out_ref[i, at[0], at[1], at[2] : at[2] + 1, :] = total[i : i + 1]


def shifted(array, axis, dim):
    size, length = lax.axis_size(axis), array.shape[dim]
    up = [(i, (i + 1) % size) for i in range(size)]
    down = [(j, i) for i, j in up]
    after = lax.ppermute(lax.slice_in_dim(array, 0, 1, axis=dim), axis, down)
    before = lax.ppermute(lax.slice_in_dim(array, length - 1, length, axis=dim), axis, up)
    return before, after


def on_device(offsets, forces, counts):
    cells = offsets.shape[1:4]
    slots = offsets.shape[4]
    n_bins = cells[0] * cells[1] * cells[2]
    n_targets = n_bins * slots
    whole = pl.BlockSpec(memory_space=pltpu.VMEM)
    scalars = pl.BlockSpec(memory_space=pltpu.SMEM)

    def floats(*shape):
        return jax.ShapeDtypeStruct(shape, jnp.float32)

    def params(mib):
        return pltpu.CompilerParams(vmem_limit_bytes=mib << 20)

    loop_scratch = [pltpu.VMEM((UNITS, 2, CHUNK, LANES), jnp.float32)]
    loop_scratch += [pltpu.SMEM((2 * n_bins,), jnp.int32)] * 5
    count_scratch = [
        pltpu.VMEM((ROWS, LANES), jnp.int32),
        pltpu.SMEM((ROWS, LANES), jnp.int32),
        pltpu.SemaphoreType.DMA,
    ]
    cost = pl.CostEstimate(flops=1 << 28, bytes_accessed=1 << 16, transcendentals=1 << 20)

    def list_scratch(n_tiles):
        return [pltpu.VMEM((n_tiles, ROWS, LANES), jnp.float32)]

    own_list, all_targets = floats(n_bins + 1, ROWS, slots), floats(3, n_targets, slots)
    sent, early = pl.pallas_call(
        functools.partial(pack_kernel, cells),
        out_shape=[floats(*cells, ROWS, slots), floats(EARLY, ROWS, slots)],
        in_specs=[scalars, whole, whole],
        out_specs=[whole, whole],
        scratch_shapes=[
            pltpu.VMEM(own_list.shape, jnp.float32),
            pltpu.VMEM((3, EARLY * slots, slots), jnp.float32),
            loop_scratch[0],
            pltpu.VMEM((4, EARLY * slots + CHUNK, slots), jnp.float32),
        ]
        + loop_scratch[1:],
        name="pack",
    )(counts, offsets, forces)

    together = lax.optimization_barrier
    size = lax.axis_size("ha")
    other = lax.ppermute(sent, "ha", [(i, (i + 1) % size) for i in range(size)])
    own, listed, spread, first = pl.pallas_call(
        functools.partial(first_kernel, cells),
        out_shape=[sent, own_list, all_targets, floats(4, len(FIRST) * slots + CHUNK, slots)],
        in_specs=[whole],
        out_specs=[whole] * 4,
        scratch_shapes=loop_scratch + count_scratch,
        compiler_params=params(8),
        cost_estimate=cost,
        name="first",
    )(sent)
    other, own, listed, first = together((other, own, listed, first))
    column = jnp.concatenate([own, other], axis=2)
    x_lo, x_hi = shifted(column, "gx", 0)
    second = pl.pallas_call(
        functools.partial(second_kernel, cells),
        out_shape=floats(4, n_targets + CHUNK, slots),
        in_specs=[scalars] + [whole] * 4,
        out_specs=whole,
        scratch_shapes=[
            pltpu.VMEM((own_list.shape[0] + cells[2] * LIST_Z, ROWS, LANES), jnp.float32)
        ]
        + loop_scratch
        + count_scratch,
        compiler_params=params(8),
        cost_estimate=cost,
        name="second",
    )(counts, other, listed, spread, first)
    x_lo, x_hi, second = together((x_lo, x_hi, second))
    wide = jnp.concatenate([x_lo, column, x_hi], axis=0)
    y_lo, y_hi = shifted(wide, "gy", 1)
    middle = pl.pallas_call(
        functools.partial(middle_kernel, cells),
        out_shape=floats(4, n_targets + CHUNK, slots),
        in_specs=[scalars] + [whole] * 3,
        out_specs=whole,
        scratch_shapes=list_scratch(cells[0] * cells[2] * LIST_X) + loop_scratch + count_scratch,
        compiler_params=params(8),
        cost_estimate=cost,
        name="middle",
    )(counts, wide, spread, second)
    y_lo, y_hi, middle = together((y_lo, y_hi, middle))
    return pl.pallas_call(
        functools.partial(last_kernel, cells),
        out_shape=floats(3, *cells, slots),
        in_specs=[scalars] + [whole] * 6,
        out_specs=whole,
        scratch_shapes=[pltpu.VMEM((4, n_targets + CHUNK, slots), jnp.float32)]
        + list_scratch(n_bins * LIST_Y)
        + loop_scratch
        + count_scratch,
        compiler_params=params(12),
        cost_estimate=cost,
        name="last",
    )(counts, own, y_lo, y_hi, spread, middle, early)


def solution(mesh):
    in_specs = (
        P(None, "gx", "gy", "ha", None),
        P(None, "gx", "gy", "ha", None),
        P("gx", "gy", "ha"),
    )
    out_specs = P(None, "gx", "gy", "ha", None)
    return jax.shard_map(on_device, mesh=mesh, in_specs=in_specs, out_specs=out_specs, check_vma=False)
```

profile of v0, /device:TPU:0, one launch (start us, length us, event | category | flops | bytes accessed | tf_op | source)
XLA Modules:
  0.0 28.5 jit_solution(12536800525317523945)
XLA Ops:
  0.0 0.0 copy-start
  0.0 4.7 %pack.1 = (f32[2,2,2,8,128]{4,3,2,1,0:T(8,128)}, f32[3,8,128]{2,1,0:T(8,128)}) custom-call(s32[2,2,2]{2,1,0:T(2,128)} %count_ref.7, f32[3,2,2,2,128]{4,3,2,1,0:T(2,128)} %offset_v.1, f32[3,2,2,2,128]{4,3,2,1,0:T(2,128)} %force_v.1), custom_call_target="tpu_custom_call" | custom-call | tf_op jit(solution)/shard_map/pack/pallas_call | solution.py:400
  4.7 0.0 collective-permute-start
  4.7 0.0 copy-start.2
  4.7 0.8 %copy-done.2 = f32[2,2,2,8,128]{4,3,2,1,0:T(8,128)S(1)} copy-done((f32[2,2,2,8,128]{4,3,2,1,0:T(8,128)S(1)}, f32[2,2,2,8,128]{4,3,2,1,0:T(8,128)}, u32[]{:S(2)}) %copy-start.2) | copy-done | bytes 32792
  5.5 2.6 %first.1 = (f32[2,2,2,8,128]{4,3,2,1,0:T(8,128)S(1)}, f32[9,8,128]{2,1,0:T(8,128)S(1)}, f32[3,1024,128]{2,1,0:T(8,128)S(1)}, f32[4,288,128]{2,1,0:T(8,128)S(1)}) custom-call(f32[2,2,2,8,128]{4,3,2,1,0:T(8,128)S(1)} %copy-done.2), custom_call_target="tpu_custom_call" | custom-call | flops 268435456 | bytes 65536 | tf_op jit(solution)/shard_map/first/pallas_call | solution.py:418
  8.1 0.7 %collective-permute-done.other = f32[2,2,2,8,128]{4,3,2,1,0:T(8,128)S(1)} collective-permute-done((f32[2,2,2,8,128]{4,3,2,1,0:T(8,128)}, f32[2,2,2,8,128]{4,3,2,1,0:T(8,128)S(1)}, u32[]{:S(2)}, u32[]{:S(2)}) %collective-permute-start) | collective-permute-done | bytes 32800 | tf_op jit(solution)/shard_map/ppermute | solution.py:417
  8.9 1.9 %collective-permute-start.2 = (f32[1,2,4,8,128]{4,3,2,1,0:T(8,128)S(1)}, f32[1,2,4,8,128]{4,3,2,1,0:T(8,128)S(1)}, u32[]{:S(2)}, u32[]{:S(2)}) collective-permute-start(f32[1,2,4,8,128]{4,3,2,1,0:T(8,128)S(1)} %get-tuple-element.39), channel_id=1, source_target_pairs={{8,0},{16,8},{24,16},{0,24},{9,1},{17,9},{25,17},{1,25},{10,2},{18... | collective-permute-start | bytes 98312 | tf_op jit(solution)/shard_map/ppermute | solution.py:368
  10.7 0.2 collective-permute-start.1
  10.9 0.0 copy-done
  10.9 5.7 %second.1 = f32[4,1056,128]{2,1,0:T(8,128)S(1)} custom-call(s32[2,2,2]{2,1,0:T(2,128)S(1)} %copy-done, f32[2,2,2,8,128]{4,3,2,1,0:T(8,128)S(1)} %collective-permute-done.other, f32[9,8,128]{2,1,0:T(8,128)S(1)} %get-tuple-element.27.own_list, f32[3,1024,128]{2,1,0:T(8,128)S(1)} %get-tuple-element.28.spread, f32[4,288,128]{2,1,0:T(8,128)S(1)} %get-tuple-element.29.first), custom_call_target="tpu_custom_call" | custom-call | flops 268435456 | bytes 65536 | tf_op jit(solution)/shard_map/second/pallas_call | solution.py:431
  16.6 0.0 collective-permute-done.2
  16.7 0.0 collective-permute-done.1
  16.7 0.1 collective-permute-start.4
  16.8 0.0 copy-start.1
  16.8 0.5 %collective-permute-start.3 = (f32[4,1,4,8,128]{4,3,2,1,0:T(8,128)S(1)}, f32[4,1,4,8,128]{4,3,2,1,0:T(8,128)S(1)}, u32[]{:S(2)}, u32[]{:S(2)}) collective-permute-start(f32[4,1,4,8,128]{4,3,2,1,0:T(8,128)S(1)} %get-tuple-element.38), channel_id=1, source_target_pairs={{0,2},{2,4},{4,6},{6,0},{1,3},{3,5},{5,7},{7,1},{8,10},{10,12},{12... | collective-permute-start | bytes 196616 | tf_op jit(solution)/shard_map/ppermute | solution.py:369
  17.3 4.0 %middle.1.refs_0_ = f32[4,1056,128]{2,1,0:T(8,128)S(1)} custom-call(s32[2,2,2]{2,1,0:T(2,128)S(1)} %copy-done, f32[4,2,4,8,128]{4,3,2,1,0:T(8,128)S(1)} %pad_maximum_fusion.wide, f32[3,1024,128]{2,1,0:T(8,128)S(1)} %get-tuple-element.28.spread, f32[4,1056,128]{2,1,0:T(8,128)S(1)} %second.1), custom_call_target="tpu_custom_call" | custom-call | flops 268435456 | bytes 65536 | tf_op jit(solution)/shard_map/middle/pallas_call | solution.py:448
  21.2 0.0 collective-permute-done.4.y_hi
  21.2 0.0 collective-permute-done.3.y_lo
  21.3 0.0 copy-done.1
  21.3 7.2 %last.1 = f32[3,2,2,2,128]{4,3,2,1,0:T(2,128)} custom-call(s32[2,2,2]{2,1,0:T(2,128)S(1)} %copy-done, f32[2,2,2,8,128]{4,3,2,1,0:T(8,128)S(1)} %get-tuple-element.25.own_ref, f32[4,1,4,8,128]{4,3,2,1,0:T(8,128)S(1)} %collective-permute-done.3.y_lo, f32[4,1,4,8,128]{4,3,2,1,0:T(8,128)S(1)} %collective-permute-done.4.y_hi, ...), custom_call_target="tpu_custom_call" | custom-call | flops 268435456 | bytes 65536 | tf_op jit(solution)/shard_map/last/pallas_call | solution.py:459
  (5 shorter events, 0.0 us)
Async XLA Ops:
  0.0 10.9 %copy-start = (s32[2,2,2]{2,1,0:T(2,128)S(1)}, s32[2,2,2]{2,1,0:T(2,128)}, u32[]{:S(2)}) copy-start(s32[2,2,2]{2,1,0:T(2,128)} %count_ref.7) | copy-start | bytes 100
  4.7 4.1 %collective-permute-start = (f32[2,2,2,8,128]{4,3,2,1,0:T(8,128)}, f32[2,2,2,8,128]{4,3,2,1,0:T(8,128)S(1)}, u32[]{:S(2)}, u32[]{:S(2)}) collective-permute-start(f32[2,2,2,8,128]{4,3,2,1,0:T(8,128)} %get-tuple-element.21.sent_ref), channel_id=1, source_target_pairs={{0,1},{1,0},{2,3},{3,2},{4,5},{5,4},{6,7},{7,6},{8,9},{9,8},{10,11... | collective-permute-start | bytes 98312 | tf_op jit(solution)/shard_map/ppermute | solution.py:417
  4.7 0.8 %copy-start.2 = (f32[2,2,2,8,128]{4,3,2,1,0:T(8,128)S(1)}, f32[2,2,2,8,128]{4,3,2,1,0:T(8,128)}, u32[]{:S(2)}) copy-start(f32[2,2,2,8,128]{4,3,2,1,0:T(8,128)} %get-tuple-element.21.sent_ref) | copy-start | bytes 98308
  8.9 7.8 %collective-permute-start.2 = (f32[1,2,4,8,128]{4,3,2,1,0:T(8,128)S(1)}, f32[1,2,4,8,128]{4,3,2,1,0:T(8,128)S(1)}, u32[]{:S(2)}, u32[]{:S(2)}) collective-permute-start(f32[1,2,4,8,128]{4,3,2,1,0:T(8,128)S(1)} %get-tuple-element.39), channel_id=1, source_target_pairs={{8,0},{16,8},{24,16},{0,24},{9,1},{17,9},{25,17},{1,25},{10,2},{18... | collective-permute-start | bytes 98312 | tf_op jit(solution)/shard_map/ppermute | solution.py:368
  10.7 5.9 %collective-permute-start.1 = (f32[1,2,4,8,128]{4,3,2,1,0:T(8,128)S(1)}, f32[1,2,4,8,128]{4,3,2,1,0:T(8,128)S(1)}, u32[]{:S(2)}, u32[]{:S(2)}) collective-permute-start(f32[1,2,4,8,128]{4,3,2,1,0:T(8,128)S(1)} %get-tuple-element.40), channel_id=1, source_target_pairs={{0,8},{8,16},{16,24},{24,0},{1,9},{9,17},{17,25},{25,1},{2,10},{10... | collective-permute-start | bytes 98312 | tf_op jit(solution)/shard_map/ppermute | solution.py:369
  16.7 4.5 %collective-permute-start.4 = (f32[4,1,4,8,128]{4,3,2,1,0:T(8,128)S(1)}, f32[4,1,4,8,128]{4,3,2,1,0:T(8,128)S(1)}, u32[]{:S(2)}, u32[]{:S(2)}) collective-permute-start(f32[4,1,4,8,128]{4,3,2,1,0:T(8,128)S(1)} %get-tuple-element.37), channel_id=1, source_target_pairs={{2,0},{4,2},{6,4},{0,6},{3,1},{5,3},{7,5},{1,7},{10,8},{12,10},{14... | collective-permute-start | bytes 196616 | tf_op jit(solution)/shard_map/ppermute | solution.py:368
  16.8 4.5 %copy-start.1 = (f32[3,8,128]{2,1,0:T(8,128)S(1)}, f32[3,8,128]{2,1,0:T(8,128)}, u32[]{:S(2)}) copy-start(f32[3,8,128]{2,1,0:T(8,128)} %get-tuple-element.36.refs_1_) | copy-start | bytes 36868
  16.8 4.5 %collective-permute-start.3 = (f32[4,1,4,8,128]{4,3,2,1,0:T(8,128)S(1)}, f32[4,1,4,8,128]{4,3,2,1,0:T(8,128)S(1)}, u32[]{:S(2)}, u32[]{:S(2)}) collective-permute-start(f32[4,1,4,8,128]{4,3,2,1,0:T(8,128)S(1)} %get-tuple-element.38), channel_id=1, source_target_pairs={{0,2},{2,4},{4,6},{6,0},{1,3},{3,5},{5,7},{7,1},{8,10},{10,12},{12... | collective-permute-start | bytes 196616 | tf_op jit(solution)/shard_map/ppermute | solution.py:369
where the time goes:
time: 28.4 us; the launch traced here: 28.5 us
  Pallas kernels  24.2 us (85%)
  starting transfers between devices  2.62 us (9%)
  local copies, waits for them, and re-layouts  0.83 us (3%)
  waiting for transfers between devices  0.73 us (3%)
    pallas_call x1, Pallas kernels, on_device(): pl.pallas_call(functools.partial(last_kernel, cells), out_shape=floats(3,...  7.23 us
    pallas_call x1, Pallas kernels, on_device(): pl.pallas_call(functools.partial(second_kernel, cells), out_shape=floats(...  5.7 us
    pallas_call x1, Pallas kernels, on_device(): pl.pallas_call(functools.partial(pack_kernel, cells), out_shape=[floats(*...  4.7 us
    pallas_call x1, Pallas kernels, on_device(): pl.pallas_call(functools.partial(middle_kernel, cells), out_shape=floats(...  3.96 us
    pallas_call x1, Pallas kernels, on_device(): pl.pallas_call(functools.partial(first_kernel, cells), out_shape=[sent, o...  2.61 us
    ppermute x2, starting transfers between devices, shifted(): after = lax.ppermute(lax.slice_in_dim(array, 0, 1, axis=dim), axis, down)  1.93 us
    unnamed x7, local copies, waits for them, and re-layouts  0.8 us
    ppermute x1, waiting for transfers between devices, on_device(): other = lax.ppermute(sent, 'ha', [(i, (i + 1) % size) for i in range(size)])  0.72 us
  transfers between devices with their start and end apart: 5, of which 1 were waited for; matrix products, arithmetic and copies ran while one was open for 0% of the time, Pallas kernels for 43%

commit v1 on v0

--- a/solution.py
+++ b/solution.py
@@ -26,9 +26,10 @@
 UNITS = 8
 COUNT_ROW = 3
 FULL = 640
+MANY = 440
 EARLY = 3
 FIRST = (3, 4)
-SECOND = (5, 6, 7, 3, 4, 0, 1, 2)
+SECOND = (5, 6, 7, 0, 1, 2, 3, 4)
 LIST_Z, LIST_X, LIST_Y = 5, 7, 10
 FORCE_ROW = 4
 
@@ -170,7 +171,7 @@
     filled = jnp.int32(0)
     for at in bins_of(cells):
         filled = filled + count_ref[at]
-    return filled, filled > FULL
+    return filled, filled > FULL, filled > MANY
 
 
 def list_own(cells, count_ref, own_ref, listed):
@@ -195,7 +196,18 @@
     return merged
 
 
-def pack_kernel(cells, count_ref, offset_v, force_v, own_ref, early_ref, listed, spread, coefs, acc, *tables):
+def pack_kernel(cells, count_hbm, offset_hbm, force_hbm, own_ref, early_ref, *refs):
+    (count_ref, offset_v, force_v, sems, listed, spread, coefs, acc), tables = refs[:8], refs[8:]
+    copies = [
+        pltpu.make_async_copy(source, target, sems.at[n])
+        for n, (source, target) in enumerate(
+            ((count_hbm, count_ref), (offset_hbm, offset_v), (force_hbm, force_v))
+        )
+    ]
+    for copy in copies:
+        copy.start()
+    for copy in copies:
+        copy.wait()
     slot = lax.broadcasted_iota(jnp.int32, (1, LANES), 1)
     for at in bins_of(cells):
         ix, iy, iz = at
@@ -209,7 +221,7 @@
         own_ref[ix, iy, iz, 3:4, :] = wide
         own_ref[ix, iy, iz, 7:8, :] = wide
     early_ref[...] = jnp.zeros_like(early_ref)
-    filled, full = is_full(cells, count_ref)
+    filled, full, _ = is_full(cells, count_ref)
 
     @pl.when(full)
     def _():
@@ -251,10 +263,10 @@
     copy.wait()
     count_ref = {at: count_s[COUNT_ROW, n] for n, at in enumerate(bins)}
     list_own(cells, count_ref, own_ref, listed)
-    filled, full = is_full(cells, count_ref)
+    filled, _, many = is_full(cells, count_ref)
     work = Groups(tables)
     for m, n in enumerate(FIRST):
-        n_chunks = jnp.where(full, up_to(count_ref[bins[n]], CHUNK), 0)
+        n_chunks = jnp.where(many, up_to(count_ref[bins[n]], CHUNK), 0)
         work.add(n_chunks, up_to(filled, LANES), 0, n * LANES, m * LANES)
     work.run(listed, spread, coefs, acc)
 
@@ -274,7 +286,7 @@
     n_own = own_list.shape[0]
     for n in range(n_own):
         listed[n] = own_list[n]
-    filled, full = is_full(cells, count_ref)
+    filled, full, many = is_full(cells, count_ref)
     copy.wait()
     work = Groups(tables)
     for bz in range(size_z):
@@ -292,7 +304,8 @@
                 work.add(up_to(count_ref[at], CHUNK), n_tiles, first_tile, n * LANES, n * LANES)
     for n in SECOND:
         n_chunks = up_to(count_ref[bins[n]], CHUNK)
-        n_chunks = jnp.where(full, 0, n_chunks) if n < EARLY or n in FIRST else n_chunks
+        if n < EARLY or n in FIRST:
+            n_chunks = jnp.where(full if n < EARLY else many, 0, n_chunks)
         work.add(n_chunks, up_to(filled, LANES), 0, n * LANES, n * LANES)
     work.run(listed, spread, coefs, acc)
 
@@ -397,20 +410,26 @@
         return [pltpu.VMEM((n_tiles, ROWS, LANES), jnp.float32)]
 
     own_list, all_targets = floats(n_bins + 1, ROWS, slots), floats(3, n_targets, slots)
+    arguments = [pltpu.with_memory_space_constraint(x, pltpu.HBM) for x in (counts, offsets, forces)]
     sent, early = pl.pallas_call(
         functools.partial(pack_kernel, cells),
         out_shape=[floats(*cells, ROWS, slots), floats(EARLY, ROWS, slots)],
-        in_specs=[scalars, whole, whole],
+        in_specs=[pl.BlockSpec(memory_space=pltpu.HBM)] * 3,
         out_specs=[whole, whole],
         scratch_shapes=[
+            pltpu.SMEM(counts.shape, jnp.int32),
+            pltpu.VMEM(offsets.shape, jnp.float32),
+            pltpu.VMEM(forces.shape, jnp.float32),
+            pltpu.SemaphoreType.DMA((3,)),
             pltpu.VMEM(own_list.shape, jnp.float32),
             pltpu.VMEM((3, EARLY * slots, slots), jnp.float32),
             loop_scratch[0],
             pltpu.VMEM((4, EARLY * slots + CHUNK, slots), jnp.float32),
         ]
         + loop_scratch[1:],
+        compiler_params=params(8),
         name="pack",
-    )(counts, offsets, forces)
+    )(*arguments)
 
     together = lax.optimization_barrier
     size = lax.axis_size("ha")

time: 28.4 us -> 27 us (0.951)
  Pallas kernels: 24.2 us -> 22 us
  waiting for transfers between devices: 0.73 us -> 1.58 us
  local copies, waits for them, and re-layouts: 0.83 us -> 0.03 us
  starting transfers between devices: 2.62 us -> 3.15 us
    pallas_call x1, Pallas kernels: 4.7 us -> 3.65 us  [on_device(): pl.pallas_call(functools.partial(pack_kernel, cells), out_shape=[floats(*...]
    pallas_call x1, Pallas kernels: 7.23 us -> 6.32 us  [on_device(): pl.pallas_call(functools.partial(last_kernel, cells), out_shape=floats(3,...]
    unnamed x7 -> x3, local copies, waits for them, and re-layouts: 0.8 us -> 0.01 us
    pallas_call x1, Pallas kernels: 5.7 us -> 5.22 us  [on_device(): pl.pallas_call(functools.partial(second_kernel, cells), out_shape=floats(...]
    ppermute x2, waiting for transfers between devices: 0.01 us -> 0.47 us  [shifted(): lax.ppermute(lax.slice_in_dim(array, length - 1, length, axis=dim), axis,...]
    ppermute x2, starting transfers between devices: 1.93 us -> 2.39 us  [shifted(): after = lax.ppermute(lax.slice_in_dim(array, 0, 1, axis=dim), axis, down)]
    ppermute x1, waiting for transfers between devices: 0.72 us -> 1.11 us  [on_device(): other = lax.ppermute(sent, 'ha', [(i, (i + 1) % size) for i in range(size)])]
  transfers between devices with their start and end apart: 5 -> 5, of which waited for: 1 -> 2; matrix products, arithmetic and copies ran while one was open for 0% -> 0% of each run, Pallas kernels for 43% -> 45%
where the time goes in v1:
time: 27 us; the launch traced here: 26.8 us
  Pallas kernels  22 us (81%)
  starting transfers between devices  3.15 us (12%)
  waiting for transfers between devices  1.58 us (6%)
    pallas_call x1, Pallas kernels, on_device(): pl.pallas_call(functools.partial(last_kernel, cells), out_shape=floats(3,...  6.32 us
    pallas_call x1, Pallas kernels, on_device(): pl.pallas_call(functools.partial(second_kernel, cells), out_shape=floats(...  5.22 us
    pallas_call x1, Pallas kernels, on_device(): pl.pallas_call(functools.partial(middle_kernel, cells), out_shape=floats(...  4.19 us
    pallas_call x1, Pallas kernels, on_device(): pl.pallas_call(functools.partial(pack_kernel, cells), out_shape=[floats(*...  3.65 us
    pallas_call x1, Pallas kernels, on_device(): pl.pallas_call(functools.partial(first_kernel, cells), out_shape=[sent, o...  2.6 us
    ppermute x2, starting transfers between devices, shifted(): after = lax.ppermute(lax.slice_in_dim(array, 0, 1, axis=dim), axis, down)  2.39 us
    ppermute x1, waiting for transfers between devices, on_device(): other = lax.ppermute(sent, 'ha', [(i, (i + 1) % size) for i in range(size)])  1.11 us
  transfers between devices with their start and end apart: 5, of which 2 were waited for; matrix products, arithmetic and copies ran while one was open for 0% of the time, Pallas kernels for 45%

profile of v1, /device:TPU:0, one launch (start us, length us, event | category | flops | bytes accessed | tf_op | source)
XLA Modules:
  0.0 26.8 jit_solution(8477594325366612407)
XLA Ops:
  0.0 0.0 copy-start
  0.0 3.6 %pack.1 = (f32[2,2,2,8,128]{4,3,2,1,0:T(8,128)S(1)}, f32[3,8,128]{2,1,0:T(8,128)S(1)}) custom-call(s32[2,2,2]{2,1,0:T(2,128)} %count_ref.5, f32[3,2,2,2,128]{4,3,2,1,0:T(2,128)} %offset_hbm.1, f32[3,2,2,2,128]{4,3,2,1,0:T(2,128)} %force_hbm.1), custom_call_target="tpu_custom_call" | custom-call | tf_op jit(solution)/shard_map/pack/pallas_call | solution.py:414
  3.7 0.3 collective-permute-start
  3.9 2.6 %first.1 = (f32[2,2,2,8,128]{4,3,2,1,0:T(8,128)S(1)}, f32[9,8,128]{2,1,0:T(8,128)S(1)}, f32[3,1024,128]{2,1,0:T(8,128)S(1)}, f32[4,288,128]{2,1,0:T(8,128)S(1)}) custom-call(f32[2,2,2,8,128]{4,3,2,1,0:T(8,128)S(1)} %get-tuple-element.21.sent_ref), custom_call_target="tpu_custom_call" | custom-call | flops 268435456 | bytes 65536 | tf_op jit(solution)/shard_map/first/pallas_call | solution.py:437
  6.5 1.1 %collective-permute-done.other = f32[2,2,2,8,128]{4,3,2,1,0:T(8,128)S(1)} collective-permute-done((f32[2,2,2,8,128]{4,3,2,1,0:T(8,128)S(1)}, f32[2,2,2,8,128]{4,3,2,1,0:T(8,128)S(1)}, u32[]{:S(2)}, u32[]{:S(2)}) %collective-permute-start) | collective-permute-done | bytes 32800 | tf_op jit(solution)/shard_map/ppermute | solution.py:436
  7.7 2.3 %collective-permute-start.2 = (f32[1,2,4,8,128]{4,3,2,1,0:T(8,128)S(1)}, f32[1,2,4,8,128]{4,3,2,1,0:T(8,128)S(1)}, u32[]{:S(2)}, u32[]{:S(2)}) collective-permute-start(f32[1,2,4,8,128]{4,3,2,1,0:T(8,128)S(1)} %get-tuple-element.39), channel_id=1, source_target_pairs={{8,0},{16,8},{24,16},{0,24},{9,1},{17,9},{25,17},{1,25},{10,2},{18... | collective-permute-start | bytes 98312 | tf_op jit(solution)/shard_map/ppermute | solution.py:381
  10.0 0.0 collective-permute-start.1
  10.0 0.0 copy-done
  10.0 5.2 %second.1 = f32[4,1056,128]{2,1,0:T(8,128)S(1)} custom-call(s32[2,2,2]{2,1,0:T(2,128)S(1)} %copy-done, f32[2,2,2,8,128]{4,3,2,1,0:T(8,128)S(1)} %collective-permute-done.other, f32[9,8,128]{2,1,0:T(8,128)S(1)} %get-tuple-element.27.own_list, f32[3,1024,128]{2,1,0:T(8,128)S(1)} %get-tuple-element.28.spread, f32[4,288,128]{2,1,0:T(8,128)S(1)} %get-tuple-element.29.first), custom_call_target="tpu_custom_call" | custom-call | flops 268435456 | bytes 65536 | tf_op jit(solution)/shard_map/second/pallas_call | solution.py:450
  15.2 0.0 collective-permute-done.2
  15.2 0.5 %collective-permute-done.1 = f32[1,2,4,8,128]{4,3,2,1,0:T(8,128)S(1)} collective-permute-done((f32[1,2,4,8,128]{4,3,2,1,0:T(8,128)S(1)}, f32[1,2,4,8,128]{4,3,2,1,0:T(8,128)S(1)}, u32[]{:S(2)}, u32[]{:S(2)}) %collective-permute-start.1) | collective-permute-done | bytes 32800 | tf_op jit(solution)/shard_map/ppermute | solution.py:382
  15.7 0.1 collective-permute-start.4
  15.8 0.5 %collective-permute-start.3 = (f32[4,1,4,8,128]{4,3,2,1,0:T(8,128)S(1)}, f32[4,1,4,8,128]{4,3,2,1,0:T(8,128)S(1)}, u32[]{:S(2)}, u32[]{:S(2)}) collective-permute-start(f32[4,1,4,8,128]{4,3,2,1,0:T(8,128)S(1)} %get-tuple-element.38), channel_id=1, source_target_pairs={{0,2},{2,4},{4,6},{6,0},{1,3},{3,5},{5,7},{7,1},{8,10},{10,12},{12... | collective-permute-start | bytes 196616 | tf_op jit(solution)/shard_map/ppermute | solution.py:382
  16.3 4.2 %middle.1.refs_0_ = f32[4,1056,128]{2,1,0:T(8,128)S(1)} custom-call(s32[2,2,2]{2,1,0:T(2,128)S(1)} %copy-done, f32[4,2,4,8,128]{4,3,2,1,0:T(8,128)S(1)} %pad_maximum_fusion.wide, f32[3,1024,128]{2,1,0:T(8,128)S(1)} %get-tuple-element.28.spread, f32[4,1056,128]{2,1,0:T(8,128)S(1)} %second.1), custom_call_target="tpu_custom_call" | custom-call | flops 268435456 | bytes 65536 | tf_op jit(solution)/shard_map/middle/pallas_call | solution.py:467
  20.5 0.0 collective-permute-done.4.y_hi
  20.5 0.0 collective-permute-done.3.y_lo
  20.5 6.3 %last.1 = f32[3,2,2,2,128]{4,3,2,1,0:T(2,128)} custom-call(s32[2,2,2]{2,1,0:T(2,128)S(1)} %copy-done, f32[2,2,2,8,128]{4,3,2,1,0:T(8,128)S(1)} %get-tuple-element.25.own_ref, f32[4,1,4,8,128]{4,3,2,1,0:T(8,128)S(1)} %collective-permute-done.3.y_lo, f32[4,1,4,8,128]{4,3,2,1,0:T(8,128)S(1)} %collective-permute-done.4.y_hi, ...), custom_call_target="tpu_custom_call" | custom-call | flops 268435456 | bytes 65536 | tf_op jit(solution)/shard_map/last/pallas_call | solution.py:478
  (5 shorter events, 0.0 us)
Async XLA Ops:
  0.0 10.0 %copy-start = (s32[2,2,2]{2,1,0:T(2,128)S(1)}, s32[2,2,2]{2,1,0:T(2,128)}, u32[]{:S(2)}) copy-start(s32[2,2,2]{2,1,0:T(2,128)} %count_ref.5) | copy-start | bytes 100
  3.7 4.0 %collective-permute-start = (f32[2,2,2,8,128]{4,3,2,1,0:T(8,128)S(1)}, f32[2,2,2,8,128]{4,3,2,1,0:T(8,128)S(1)}, u32[]{:S(2)}, u32[]{:S(2)}) collective-permute-start(f32[2,2,2,8,128]{4,3,2,1,0:T(8,128)S(1)} %get-tuple-element.21.sent_ref), channel_id=1, source_target_pairs={{0,1},{1,0},{2,3},{3,2},{4,5},{5,4},{6,7},{7,6},{8,9},{9,8},{10,11... | collective-permute-start | bytes 98312 | tf_op jit(solution)/shard_map/ppermute | solution.py:436
  7.7 7.6 %collective-permute-start.2 = (f32[1,2,4,8,128]{4,3,2,1,0:T(8,128)S(1)}, f32[1,2,4,8,128]{4,3,2,1,0:T(8,128)S(1)}, u32[]{:S(2)}, u32[]{:S(2)}) collective-permute-start(f32[1,2,4,8,128]{4,3,2,1,0:T(8,128)S(1)} %get-tuple-element.39), channel_id=1, source_target_pairs={{8,0},{16,8},{24,16},{0,24},{9,1},{17,9},{25,17},{1,25},{10,2},{18... | collective-permute-start | bytes 98312 | tf_op jit(solution)/shard_map/ppermute | solution.py:381
  10.0 5.7 %collective-permute-start.1 = (f32[1,2,4,8,128]{4,3,2,1,0:T(8,128)S(1)}, f32[1,2,4,8,128]{4,3,2,1,0:T(8,128)S(1)}, u32[]{:S(2)}, u32[]{:S(2)}) collective-permute-start(f32[1,2,4,8,128]{4,3,2,1,0:T(8,128)S(1)} %get-tuple-element.40), channel_id=1, source_target_pairs={{0,8},{8,16},{16,24},{24,0},{1,9},{9,17},{17,25},{25,1},{2,10},{10... | collective-permute-start | bytes 98312 | tf_op jit(solution)/shard_map/ppermute | solution.py:382
  15.7 4.8 %collective-permute-start.4 = (f32[4,1,4,8,128]{4,3,2,1,0:T(8,128)S(1)}, f32[4,1,4,8,128]{4,3,2,1,0:T(8,128)S(1)}, u32[]{:S(2)}, u32[]{:S(2)}) collective-permute-start(f32[4,1,4,8,128]{4,3,2,1,0:T(8,128)S(1)} %get-tuple-element.37), channel_id=1, source_target_pairs={{2,0},{4,2},{6,4},{0,6},{3,1},{5,3},{7,5},{1,7},{10,8},{12,10},{14... | collective-permute-start | bytes 196616 | tf_op jit(solution)/shard_map/ppermute | solution.py:381
  15.8 4.7 %collective-permute-start.3 = (f32[4,1,4,8,128]{4,3,2,1,0:T(8,128)S(1)}, f32[4,1,4,8,128]{4,3,2,1,0:T(8,128)S(1)}, u32[]{:S(2)}, u32[]{:S(2)}) collective-permute-start(f32[4,1,4,8,128]{4,3,2,1,0:T(8,128)S(1)} %get-tuple-element.38), channel_id=1, source_target_pairs={{0,2},{2,4},{4,6},{6,0},{1,3},{3,5},{5,7},{7,1},{8,10},{10,12},{12... | collective-permute-start | bytes 196616 | tf_op jit(solution)/shard_map/ppermute | solution.py:382

commit v2 on v1

--- a/solution.py
+++ b/solution.py
@@ -69,6 +69,20 @@
     return filled
 
 
+def spread_rows(lists, to, listed, base, n_tiles, most):
+    def some(tiles):
+        for n in tiles:
+            for i, row in enumerate((0, 1, 2, 4, 5, 6)):
+                lists[to + n, i] = jnp.broadcast_to(listed[base + n, row : row + 1, :], (ROWS, LANES))
+
+    likely = min(5, most)
+    some(range(likely))
+
+    @pl.when(n_tiles > likely)
+    def _():
+        some(range(likely, most))
+
+
 def up_to(count, size):
     return lax.shift_right_logical(count + (size - 1), size.bit_length() - 1)
 
@@ -120,13 +134,13 @@
         self.size += 1
         self.total = self.total + n_chunks * n_tiles
 
-    def run(self, listed, spread, coefs, acc):
+    def run(self, lists, spread, coefs, acc):
         chunks_of, tiles_of, list_of, spread_of, acc_of = self.tables
         trash = acc.shape[1] - CHUNK
-        coefs[...] = jnp.zeros_like(coefs)
-
-        def rows(tile_id, at):
-            return [listed[tile_id, i : i + 1, :] for i in at]
+
+        def rows(tile_id):
+            wide = [jnp.concatenate([lists[tile_id, i]] * (CHUNK // ROWS), axis=0) for i in range(6)]
+            return wide[:3], wide[3:]
 
         def advance(group, chunk, tile):
             end_tile = tile + 1 == tiles_of[group]
@@ -135,36 +149,49 @@
             next_group = jnp.where(end_chunk, jnp.minimum(group + 1, self.size - 1), group)
             return next_group, jnp.where(end_chunk, 0, next_chunk), jnp.where(end_tile, 0, tile + 1)
 
-        def some_units(step, state):
-            place, olds = state[:3], state[3:]
-            news, targets, sources = [], [], []
+        def find(step, place):
+            units, found = [], []
             for n in range(UNITS):
                 group, chunk, tile = place
                 valid = step * UNITS + n < self.total
-                news += [jnp.where(valid, acc_of[group] + chunk, trash), list_of[group] + tile]
+                units += [jnp.where(valid, acc_of[group] + chunk, trash), list_of[group] + tile]
                 at = pl.ds(pl.multiple_of(spread_of[group] + chunk, CHUNK), CHUNK)
-                targets.append([spread[i, at, :] for i in range(3)])
-                sources.append((rows(news[-1], (0, 1, 2)), rows(news[-1], (4, 5, 6))))
+                target = [spread[i, at, :] for i in range(3)]
+                found.append(coefficients(target, *rows(units[-1])))
                 place = advance(*place)
-            old_coefs = [(coefs[n, 0], coefs[n, 1]) for n in range(UNITS)]
-            old_sources = [(rows(tile, (0, 1, 2)), rows(tile, (4, 5, 6))) for tile in olds[1::2]]
-
-            new_coefs = [coefficients(target, *source) for target, source in zip(targets, sources)]
+            return found, tuple(units), place
+
+        def use(units):
             terms = []
-            for (source, force), (coef_c, along) in zip(old_sources, old_coefs):
+            for n, tile in enumerate(units[1::2]):
+                coef_c, along = coefs[n, 0], coefs[n, 1]
+                source, force = rows(tile)
                 terms.append([coef_c * force[i] - along * source[i] for i in range(3)] + [along])
-
-            for first, unit in zip(olds[::2], terms):
+            return terms
+
+        def keep(found):
+            for n, pair in enumerate(found):
+                coefs[n, 0], coefs[n, 1] = pair
+
+        def add(units, terms):
+            for first, unit in zip(units[::2], terms):
                 at = pl.ds(pl.multiple_of(first, CHUNK), CHUNK)
                 for i in range(4):
                     acc[i, at, :] = acc[i, at, :] + unit[i]
-            for n in range(UNITS):
-                coefs[n, 0], coefs[n, 1] = new_coefs[n]
-            return place + tuple(news)
+
+        def body(step, state):
+            place, olds = state[:3], state[3:]
+            terms = use(olds)
+            found, news, place = find(step, place)
+            add(olds, terms)
+            keep(found)
+            return place + news
 
         zero = jnp.int32(0)
-        start = (zero, zero, zero) + (jnp.int32(trash), list_of[0]) * UNITS
-        lax.fori_loop(0, lax.div(self.total + UNITS - 1, UNITS) + 1, some_units, start)
+        found, units, place = find(0, (zero, zero, zero))
+        keep(found)
+        state = lax.fori_loop(1, lax.div(self.total + UNITS - 1, UNITS), body, place + units)
+        add(state[3:], use(state[3:]))
 
 
 def is_full(cells, count_ref):
@@ -197,7 +224,7 @@
 
 
 def pack_kernel(cells, count_hbm, offset_hbm, force_hbm, own_ref, early_ref, *refs):
-    (count_ref, offset_v, force_v, sems, listed, spread, coefs, acc), tables = refs[:8], refs[8:]
+    (count_ref, offset_v, force_v, sems, listed, lists, spread, coefs, acc), tables = refs[:9], refs[9:]
     copies = [
         pltpu.make_async_copy(source, target, sems.at[n])
         for n, (source, target) in enumerate(
@@ -226,6 +253,7 @@
     @pl.when(full)
     def _():
         list_own(cells, count_ref, own_ref, listed)
+        spread_rows(lists, 0, listed, 0, up_to(filled, LANES), len(bins_of(cells)))
         acc[...] = jnp.zeros_like(acc)
         groups = range(EARLY)
         tiles = [own_ref[bins_of(cells)[n]] for n in groups]
@@ -234,7 +262,7 @@
             at = bins_of(cells)[n]
             spread_targets(spread, n * LANES, tiles[n] + shift_tile(cells, at))
             work.add(up_to(count_ref[at], CHUNK), up_to(filled, LANES), 0, n * LANES, n * LANES)
-        work.run(listed, spread, coefs, acc)
+        work.run(lists, spread, coefs, acc)
         merged = lane_sums([acc[i, : EARLY * LANES, :] for i in range(4)])
         for n in groups:
             by_row = jnp.transpose(merged[n * LANES : (n + 1) * LANES])[:ROWS]
@@ -252,7 +280,7 @@
     return copy
 
 
-def first_kernel(cells, sent_ref, own_ref, listed, spread, acc, coefs, *refs):
+def first_kernel(cells, sent_ref, own_ref, lists, spread, acc, listed, coefs, *refs):
     tables, (count_v, count_s, sem) = refs[:5], refs[5:]
     bins = bins_of(cells)
     copy = counts_of([sent_ref[at] for at in bins], count_v, count_s, sem)
@@ -264,14 +292,15 @@
     count_ref = {at: count_s[COUNT_ROW, n] for n, at in enumerate(bins)}
     list_own(cells, count_ref, own_ref, listed)
     filled, _, many = is_full(cells, count_ref)
+    spread_rows(lists, 0, listed, 0, up_to(filled, LANES), len(bins))
     work = Groups(tables)
     for m, n in enumerate(FIRST):
         n_chunks = jnp.where(many, up_to(count_ref[bins[n]], CHUNK), 0)
         work.add(n_chunks, up_to(filled, LANES), 0, n * LANES, m * LANES)
-    work.run(listed, spread, coefs, acc)
-
-
-def second_kernel(cells, count_ref, other, own_list, spread, first, acc, listed, coefs, *refs):
+    work.run(lists, spread, coefs, acc)
+
+
+def second_kernel(cells, count_ref, other, own_lists, spread, first, acc, listed, lists, coefs, *refs):
     tables, (count_v, count_s, sem) = refs[:5], refs[5:]
     bins = bins_of(cells)
     size_x, size_y, size_z = cells
@@ -283,9 +312,9 @@
             acc[:, here, :] = first[:, m * LANES : (m + 1) * LANES, :]
         else:
             acc[:, here, :] = jnp.zeros((4, LANES, LANES), jnp.float32)
-    n_own = own_list.shape[0]
+    n_own = own_lists.shape[0]
     for n in range(n_own):
-        listed[n] = own_list[n]
+        lists[n] = own_lists[n]
     filled, full, many = is_full(cells, count_ref)
     copy.wait()
     work = Groups(tables)
@@ -297,8 +326,9 @@
                 place = (x, y, z % size_z)
                 tile = other[place] + shift_tile(cells, (x, y, z))
                 sources.append((tile, count_s[COUNT_ROW, bins.index(place)]))
-        first_tile = n_own + bz * LIST_Z
-        n_tiles = up_to(compact(listed, first_tile, sources), LANES)
+        n_tiles = up_to(compact(listed, bz * LIST_Z, sources), LANES)
+        first_tile = n_own + bz * (LIST_Z - 1)
+        spread_rows(lists, first_tile, listed, bz * LIST_Z, n_tiles, LIST_Z - 1)
         for n, at in enumerate(bins):
             if at[2] == bz:
                 work.add(up_to(count_ref[at], CHUNK), n_tiles, first_tile, n * LANES, n * LANES)
@@ -307,10 +337,10 @@
         if n < EARLY or n in FIRST:
             n_chunks = jnp.where(full if n < EARLY else many, 0, n_chunks)
         work.add(n_chunks, up_to(filled, LANES), 0, n * LANES, n * LANES)
-    work.run(listed, spread, coefs, acc)
-
-
-def middle_kernel(cells, count_ref, wide, spread, second, acc, listed, coefs, *refs):
+    work.run(lists, spread, coefs, acc)
+
+
+def middle_kernel(cells, count_ref, wide, spread, second, acc, listed, lists, coefs, *refs):
     tables, (count_v, count_s, sem) = refs[:5], refs[5:]
     size_x, size_y, size_z = cells
     n_z = 2 * size_z
@@ -329,16 +359,18 @@
                     place = (x + 1, y, z % n_z)
                     tile = wide[place] + shift_tile(cells, (x, y, z))
                     sources.append((tile, count_s[COUNT_ROW, places.index(place)]))
-            first_tile = (bx * size_z + bz) * LIST_X
-            n_tiles = up_to(compact(listed, first_tile, sources), LANES)
+            n_list = bx * size_z + bz
+            n_tiles = up_to(compact(listed, n_list * LIST_X, sources), LANES)
+            first_tile = n_list * (LIST_X - 1)
+            spread_rows(lists, first_tile, listed, n_list * LIST_X, n_tiles, LIST_X - 1)
             for n, at in enumerate(bins):
                 if (at[0], at[2]) == (bx, bz):
                     work.add(up_to(count_ref[at], CHUNK), n_tiles, first_tile, n * LANES, n * LANES)
-    work.run(listed, spread, coefs, acc)
+    work.run(lists, spread, coefs, acc)
 
 
 def last_kernel(cells, count_ref, own_ref, y_lo, y_hi, spread, *refs):
-    (middle, early, out_ref, acc, listed, coefs), refs = refs[:6], refs[6:]
+    (middle, early, out_ref, acc, listed, lists, coefs), refs = refs[:7], refs[7:]
     tables, (count_v, count_s, sem) = refs[:5], refs[5:]
     size_x, size_y, size_z = cells
     n_z = 2 * size_z
@@ -357,8 +389,10 @@
                 tile = tiles[cell] + shift_tile(cells, (x, (-1, size_y)[by], z))
                 sources.append((tile, count_s[COUNT_ROW, cell]))
         n_tiles = up_to(compact(listed, n * LIST_Y, sources), LANES)
-        work.add(up_to(count_ref[bx, by, bz], CHUNK), n_tiles, n * LIST_Y, n * LANES, n * LANES)
-    work.run(listed, spread, coefs, acc)
+        first_tile = n * (LIST_Y - 1)
+        spread_rows(lists, first_tile, listed, n * LIST_Y, n_tiles, LIST_Y - 1)
+        work.add(up_to(count_ref[bx, by, bz], CHUNK), n_tiles, first_tile, n * LANES, n * LANES)
+    work.run(lists, spread, coefs, acc)
 
     slot = lax.broadcasted_iota(jnp.int32, (1, LANES), 1)
     merged = lane_sums([acc[i, : len(bins) * LANES, :] for i in range(4)])
@@ -406,10 +440,13 @@
     ]
     cost = pl.CostEstimate(flops=1 << 28, bytes_accessed=1 << 16, transcendentals=1 << 20)
 
-    def list_scratch(n_tiles):
-        return [pltpu.VMEM((n_tiles, ROWS, LANES), jnp.float32)]
-
-    own_list, all_targets = floats(n_bins + 1, ROWS, slots), floats(3, n_targets, slots)
+    def list_scratch(n_lists, n_tiles, more=0):
+        return [
+            pltpu.VMEM((n_lists * n_tiles, ROWS, LANES), jnp.float32),
+            pltpu.VMEM((n_lists * (n_tiles - 1) + more, 6, ROWS, LANES), jnp.float32),
+        ]
+
+    own_lists, all_targets = floats(n_bins, 6, ROWS, slots), floats(3, n_targets, slots)
     arguments = [pltpu.with_memory_space_constraint(x, pltpu.HBM) for x in (counts, offsets, forces)]
     sent, early = pl.pallas_call(
         functools.partial(pack_kernel, cells),
@@ -421,7 +458,8 @@
             pltpu.VMEM(offsets.shape, jnp.float32),
             pltpu.VMEM(forces.shape, jnp.float32),
             pltpu.SemaphoreType.DMA((3,)),
-            pltpu.VMEM(own_list.shape, jnp.float32),
+            pltpu.VMEM((n_bins + 1, ROWS, LANES), jnp.float32),
+            pltpu.VMEM(own_lists.shape, jnp.float32),
             pltpu.VMEM((3, EARLY * slots, slots), jnp.float32),
             loop_scratch[0],
             pltpu.VMEM((4, EARLY * slots + CHUNK, slots), jnp.float32),
@@ -436,10 +474,12 @@
     other = lax.ppermute(sent, "ha", [(i, (i + 1) % size) for i in range(size)])
     own, listed, spread, first = pl.pallas_call(
         functools.partial(first_kernel, cells),
-        out_shape=[sent, own_list, all_targets, floats(4, len(FIRST) * slots + CHUNK, slots)],
+        out_shape=[sent, own_lists, all_targets, floats(4, len(FIRST) * slots + CHUNK, slots)],
         in_specs=[whole],
         out_specs=[whole] * 4,
-        scratch_shapes=loop_scratch + count_scratch,
+        scratch_shapes=[pltpu.VMEM((n_bins + 1, ROWS, LANES), jnp.float32)]
+        + loop_scratch
+        + count_scratch,
         compiler_params=params(8),
         cost_estimate=cost,
         name="first",
@@ -452,9 +492,7 @@
         out_shape=floats(4, n_targets + CHUNK, slots),
         in_specs=[scalars] + [whole] * 4,
         out_specs=whole,
-        scratch_shapes=[
-            pltpu.VMEM((own_list.shape[0] + cells[2] * LIST_Z, ROWS, LANES), jnp.float32)
-        ]
+        scratch_shapes=list_scratch(cells[2], LIST_Z, n_bins)
         + loop_scratch
         + count_scratch,
         compiler_params=params(8),
@@ -469,7 +507,7 @@
         out_shape=floats(4, n_targets + CHUNK, slots),
         in_specs=[scalars] + [whole] * 3,
         out_specs=whole,
-        scratch_shapes=list_scratch(cells[0] * cells[2] * LIST_X) + loop_scratch + count_scratch,
+        scratch_shapes=list_scratch(cells[0] * cells[2], LIST_X) + loop_scratch + count_scratch,
         compiler_params=params(8),
         cost_estimate=cost,
         name="middle",
@@ -481,7 +519,7 @@
         in_specs=[scalars] + [whole] * 6,
         out_specs=whole,
         scratch_shapes=[pltpu.VMEM((4, n_targets + CHUNK, slots), jnp.float32)]
-        + list_scratch(n_bins * LIST_Y)
+        + list_scratch(n_bins, LIST_Y)
         + loop_scratch
         + count_scratch,
         compiler_params=params(12),

time: 27 us -> 27.8 us (1.030); the launches traced: 26.8 us -> 28.2 us
  Pallas kernels: 22 us -> 24.1 us
  starting transfers between devices: 3.15 us -> 2.7 us
  waiting for transfers between devices: 1.58 us -> 1.24 us
    pallas_call x1, Pallas kernels: 6.32 us -> 7.64 us  [on_device(): pl.pallas_call(functools.partial(last_kernel, cells), out_shape=floats(3,...]
    ppermute x2, starting transfers between devices: 2.39 us -> 1.82 us  [shifted(): after = lax.ppermute(lax.slice_in_dim(array, 0, 1, axis=dim), axis, down)]
    pallas_call x1, Pallas kernels: 3.65 us -> 4.21 us  [on_device(): pl.pallas_call(functools.partial(pack_kernel, cells), out_shape=[floats(*...]
    ppermute x2, waiting for transfers between devices: 0.47 us -> 0.01 us  [shifted(): lax.ppermute(lax.slice_in_dim(array, length - 1, length, axis=dim), axis,...]
    ppermute x2, starting transfers between devices: 0.5 us -> 0.81 us  [shifted(): lax.ppermute(lax.slice_in_dim(array, length - 1, length, axis=dim), axis,...]
    pallas_call x1, Pallas kernels: 5.22 us -> 5.52 us  [on_device(): pl.pallas_call(functools.partial(second_kernel, cells), out_shape=floats(...]
  transfers between devices with their start and end apart: 5 -> 5, of which waited for: 2 -> 1; matrix products, arithmetic and copies ran while one was open for 0% -> 0% of each run, Pallas kernels for 45% -> 44%
where the time goes in v2:
time: 27.8 us; the launch traced here: 28.2 us
  Pallas kernels  24.1 us (87%)
  starting transfers between devices  2.7 us (10%)
  waiting for transfers between devices  1.24 us (4%)
    pallas_call x1, Pallas kernels, on_device(): pl.pallas_call(functools.partial(last_kernel, cells), out_shape=floats(3,...  7.64 us
    pallas_call x1, Pallas kernels, on_device(): pl.pallas_call(functools.partial(second_kernel, cells), out_shape=floats(...  5.52 us
    pallas_call x1, Pallas kernels, on_device(): pl.pallas_call(functools.partial(pack_kernel, cells), out_shape=[floats(*...  4.21 us
    pallas_call x1, Pallas kernels, on_device(): pl.pallas_call(functools.partial(middle_kernel, cells), out_shape=floats(...  4.09 us
    pallas_call x1, Pallas kernels, on_device(): pl.pallas_call(functools.partial(first_kernel, cells), out_shape=[sent, o...  2.67 us
    ppermute x2, starting transfers between devices, shifted(): after = lax.ppermute(lax.slice_in_dim(array, 0, 1, axis=dim), axis, down)  1.82 us
    ppermute x1, waiting for transfers between devices, on_device(): other = lax.ppermute(sent, 'ha', [(i, (i + 1) % size) for i in range(size)])  1.23 us
    ppermute x2, starting transfers between devices, shifted(): lax.ppermute(lax.slice_in_dim(array, length - 1, length, axis=dim), axis,...  0.81 us
  transfers between devices with their start and end apart: 5, of which 1 were waited for; matrix products, arithmetic and copies ran while one was open for 0% of the time, Pallas kernels for 44%

profile of v2, /device:TPU:0, one launch (start us, length us, event | category | flops | bytes accessed | tf_op | source)
XLA Modules:
  0.0 28.2 jit_solution(4331788361226778830)
XLA Ops:
  0.0 0.0 copy-start
  0.0 4.2 %pack.1 = (f32[2,2,2,8,128]{4,3,2,1,0:T(8,128)S(1)}, f32[3,8,128]{2,1,0:T(8,128)S(1)}) custom-call(s32[2,2,2]{2,1,0:T(2,128)} %count_ref.5, f32[3,2,2,2,128]{4,3,2,1,0:T(2,128)} %offset_hbm.1, f32[3,2,2,2,128]{4,3,2,1,0:T(2,128)} %force_hbm.1), custom_call_target="tpu_custom_call" | custom-call | tf_op jit(solution)/shard_map/pack/pallas_call | solution.py:451
  4.2 0.1 collective-permute-start
  4.3 2.7 %first.1 = (f32[2,2,2,8,128]{4,3,2,1,0:T(8,128)S(1)}, f32[8,6,8,128]{3,2,1,0:T(8,128)S(1)}, f32[3,1024,128]{2,1,0:T(8,128)S(1)}, f32[4,288,128]{2,1,0:T(8,128)S(1)}) custom-call(f32[2,2,2,8,128]{4,3,2,1,0:T(8,128)S(1)} %get-tuple-element.21.sent_ref), custom_call_target="tpu_custom_call" | custom-call | flops 268435456 | bytes 65536 | tf_op jit(solution)/shard_map/first/pallas_call | solution.py:475
  7.0 1.2 %collective-permute-done.other = f32[2,2,2,8,128]{4,3,2,1,0:T(8,128)S(1)} collective-permute-done((f32[2,2,2,8,128]{4,3,2,1,0:T(8,128)S(1)}, f32[2,2,2,8,128]{4,3,2,1,0:T(8,128)S(1)}, u32[]{:S(2)}, u32[]{:S(2)}) %collective-permute-start) | collective-permute-done | bytes 32800 | tf_op jit(solution)/shard_map/ppermute | solution.py:474
  8.2 1.8 %collective-permute-start.2 = (f32[1,2,4,8,128]{4,3,2,1,0:T(8,128)S(1)}, f32[1,2,4,8,128]{4,3,2,1,0:T(8,128)S(1)}, u32[]{:S(2)}, u32[]{:S(2)}) collective-permute-start(f32[1,2,4,8,128]{4,3,2,1,0:T(8,128)S(1)} %get-tuple-element.39), channel_id=1, source_target_pairs={{8,0},{16,8},{24,16},{0,24},{9,1},{17,9},{25,17},{1,25},{10,2},{18... | collective-permute-start | bytes 98312 | tf_op jit(solution)/shard_map/ppermute | solution.py:415
  10.0 0.3 %collective-permute-start.1 = (f32[1,2,4,8,128]{4,3,2,1,0:T(8,128)S(1)}, f32[1,2,4,8,128]{4,3,2,1,0:T(8,128)S(1)}, u32[]{:S(2)}, u32[]{:S(2)}) collective-permute-start(f32[1,2,4,8,128]{4,3,2,1,0:T(8,128)S(1)} %get-tuple-element.40), channel_id=1, source_target_pairs={{0,8},{8,16},{16,24},{24,0},{1,9},{9,17},{17,25},{25,1},{2,10},{10... | collective-permute-start | bytes 98312 | tf_op jit(solution)/shard_map/ppermute | solution.py:416
  10.3 0.0 copy-done
  10.3 5.5 %second.1 = f32[4,1056,128]{2,1,0:T(8,128)S(1)} custom-call(s32[2,2,2]{2,1,0:T(2,128)S(1)} %copy-done, f32[2,2,2,8,128]{4,3,2,1,0:T(8,128)S(1)} %collective-permute-done.other, f32[8,6,8,128]{3,2,1,0:T(8,128)S(1)} %get-tuple-element.27.own_lists, f32[3,1024,128]{2,1,0:T(8,128)S(1)} %get-tuple-element.28.spread, f32[4,288,128]{2,1,0:T(8,128)S(1)} %get-tuple-element.29.first), custom_call_target="tpu_custom_call" | custom-call | flops 268435456 | bytes 65536 | tf_op jit(solution)/shard_map/second/pallas_call | solution.py:490
  15.8 0.0 collective-permute-done.2
  15.9 0.0 collective-permute-done.1
  15.9 0.1 collective-permute-start.4
  16.0 0.5 %collective-permute-start.3 = (f32[4,1,4,8,128]{4,3,2,1,0:T(8,128)S(1)}, f32[4,1,4,8,128]{4,3,2,1,0:T(8,128)S(1)}, u32[]{:S(2)}, u32[]{:S(2)}) collective-permute-start(f32[4,1,4,8,128]{4,3,2,1,0:T(8,128)S(1)} %get-tuple-element.38), channel_id=1, source_target_pairs={{0,2},{2,4},{4,6},{6,0},{1,3},{3,5},{5,7},{7,1},{8,10},{10,12},{12... | collective-permute-start | bytes 196616 | tf_op jit(solution)/shard_map/ppermute | solution.py:416
  16.5 4.1 %middle.1.refs_0_ = f32[4,1056,128]{2,1,0:T(8,128)S(1)} custom-call(s32[2,2,2]{2,1,0:T(2,128)S(1)} %copy-done, f32[4,2,4,8,128]{4,3,2,1,0:T(8,128)S(1)} %pad_maximum_fusion.wide, f32[3,1024,128]{2,1,0:T(8,128)S(1)} %get-tuple-element.28.spread, f32[4,1056,128]{2,1,0:T(8,128)S(1)} %second.1), custom_call_target="tpu_custom_call" | custom-call | flops 268435456 | bytes 65536 | tf_op jit(solution)/shard_map/middle/pallas_call | solution.py:505
  20.6 0.0 collective-permute-done.4.y_hi
  20.6 0.0 collective-permute-done.3.y_lo
  20.6 7.6 %last.1 = f32[3,2,2,2,128]{4,3,2,1,0:T(2,128)} custom-call(s32[2,2,2]{2,1,0:T(2,128)S(1)} %copy-done, f32[2,2,2,8,128]{4,3,2,1,0:T(8,128)S(1)} %get-tuple-element.25.own_ref, f32[4,1,4,8,128]{4,3,2,1,0:T(8,128)S(1)} %collective-permute-done.3.y_lo, f32[4,1,4,8,128]{4,3,2,1,0:T(8,128)S(1)} %collective-permute-done.4.y_hi, ...), custom_call_target="tpu_custom_call" | custom-call | flops 268435456 | bytes 65536 | tf_op jit(solution)/shard_map/last/pallas_call | solution.py:516
  (5 shorter events, 0.0 us)
Async XLA Ops:
  0.0 10.3 %copy-start = (s32[2,2,2]{2,1,0:T(2,128)S(1)}, s32[2,2,2]{2,1,0:T(2,128)}, u32[]{:S(2)}) copy-start(s32[2,2,2]{2,1,0:T(2,128)} %count_ref.5) | copy-start | bytes 100
  4.2 4.0 %collective-permute-start = (f32[2,2,2,8,128]{4,3,2,1,0:T(8,128)S(1)}, f32[2,2,2,8,128]{4,3,2,1,0:T(8,128)S(1)}, u32[]{:S(2)}, u32[]{:S(2)}) collective-permute-start(f32[2,2,2,8,128]{4,3,2,1,0:T(8,128)S(1)} %get-tuple-element.21.sent_ref), channel_id=1, source_target_pairs={{0,1},{1,0},{2,3},{3,2},{4,5},{5,4},{6,7},{7,6},{8,9},{9,8},{10,11... | collective-permute-start | bytes 98312 | tf_op jit(solution)/shard_map/ppermute | solution.py:474
  8.2 7.6 %collective-permute-start.2 = (f32[1,2,4,8,128]{4,3,2,1,0:T(8,128)S(1)}, f32[1,2,4,8,128]{4,3,2,1,0:T(8,128)S(1)}, u32[]{:S(2)}, u32[]{:S(2)}) collective-permute-start(f32[1,2,4,8,128]{4,3,2,1,0:T(8,128)S(1)} %get-tuple-element.39), channel_id=1, source_target_pairs={{8,0},{16,8},{24,16},{0,24},{9,1},{17,9},{25,17},{1,25},{10,2},{18... | collective-permute-start | bytes 98312 | tf_op jit(solution)/shard_map/ppermute | solution.py:415
  10.0 5.9 %collective-permute-start.1 = (f32[1,2,4,8,128]{4,3,2,1,0:T(8,128)S(1)}, f32[1,2,4,8,128]{4,3,2,1,0:T(8,128)S(1)}, u32[]{:S(2)}, u32[]{:S(2)}) collective-permute-start(f32[1,2,4,8,128]{4,3,2,1,0:T(8,128)S(1)} %get-tuple-element.40), channel_id=1, source_target_pairs={{0,8},{8,16},{16,24},{24,0},{1,9},{9,17},{17,25},{25,1},{2,10},{10... | collective-permute-start | bytes 98312 | tf_op jit(solution)/shard_map/ppermute | solution.py:416
  15.9 4.7 %collective-permute-start.4 = (f32[4,1,4,8,128]{4,3,2,1,0:T(8,128)S(1)}, f32[4,1,4,8,128]{4,3,2,1,0:T(8,128)S(1)}, u32[]{:S(2)}, u32[]{:S(2)}) collective-permute-start(f32[4,1,4,8,128]{4,3,2,1,0:T(8,128)S(1)} %get-tuple-element.37), channel_id=1, source_target_pairs={{2,0},{4,2},{6,4},{0,6},{3,1},{5,3},{7,5},{1,7},{10,8},{12,10},{14... | collective-permute-start | bytes 196616 | tf_op jit(solution)/shard_map/ppermute | solution.py:415
  16.0 4.6 %collective-permute-start.3 = (f32[4,1,4,8,128]{4,3,2,1,0:T(8,128)S(1)}, f32[4,1,4,8,128]{4,3,2,1,0:T(8,128)S(1)}, u32[]{:S(2)}, u32[]{:S(2)}) collective-permute-start(f32[4,1,4,8,128]{4,3,2,1,0:T(8,128)S(1)} %get-tuple-element.38), channel_id=1, source_target_pairs={{0,2},{2,4},{4,6},{6,0},{1,3},{3,5},{5,7},{7,1},{8,10},{10,12},{12... | collective-permute-start | bytes 196616 | tf_op jit(solution)/shard_map/ppermute | solution.py:416

commit v3 on v2

--- a/solution.py
+++ b/solution.py
@@ -28,8 +28,9 @@
 FULL = 640
 MANY = 440
 EARLY = 3
-FIRST = (3, 4)
-SECOND = (5, 6, 7, 0, 1, 2, 3, 4)
+FIRST = (3, 4, 5)
+SECOND = (6, 7, 5, 0, 1, 2, 3, 4)
+FIRST_IF_MANY = (3, 4)
 LIST_Z, LIST_X, LIST_Y = 5, 7, 10
 FORCE_ROW = 4
 
@@ -117,7 +118,7 @@
     tail = (1.0 - lax.erf(u * inv)) * inv
     gauss = jnp.exp2(LOG2_G - u * LOG2_E)
     rest = gauss * (u - 1.5)
-    coef_d = ((tail - rest) - gauss) * (inv * inv)
+    coef_d = ((tail - rest) - gauss) * pl.reciprocal(u, approx=True)
     along = coef_d * (delta[0] * force[0] + delta[1] * force[1] + delta[2] * force[2])
     return tail + rest, along
 
@@ -211,16 +212,21 @@
     return (2.0 * STOKES_NORM) * (by_row + position * jnp.broadcast_to(by_row[3:4], (ROWS, LANES)))
 
 
-def lane_sums(totals):
-    _, lane = rows_and_lanes((2 * LANES, LANES))
-    merged = jnp.zeros(totals[0].shape, jnp.float32)
-    for i, total in enumerate(totals):
+def lane_sums(sums, n_bins):
+    row, lane = rows_and_lanes((2 * LANES, LANES))
+    merged = jnp.zeros(sums[0].shape, jnp.float32)
+    for i, part in enumerate(sums):
         merged = merged + jnp.dot(
-            jnp.concatenate(parts_of(total, 2), axis=1),
-            jnp.where(lane == i, 1.0, 0.0).astype(jnp.bfloat16),
+            jnp.concatenate(parts_of(part, 2), axis=1),
+            jnp.where(lax.bitwise_and(lane, ROWS - 1) == i, 1.0, 0.0).astype(jnp.bfloat16),
             preferred_element_type=jnp.float32,
         )
-    return merged
+    _, lane = rows_and_lanes((LANES, LANES))
+    chosen = merged[:LANES]
+    for n in range(1, n_bins):
+        chosen = jnp.where(lane >= n * ROWS, merged[n * LANES : (n + 1) * LANES], chosen)
+    turned = jnp.transpose(chosen)
+    return [turned[n * ROWS : (n + 1) * ROWS] for n in range(n_bins)]
 
 
 def pack_kernel(cells, count_hbm, offset_hbm, force_hbm, own_ref, early_ref, *refs):
@@ -263,9 +269,8 @@
             spread_targets(spread, n * LANES, tiles[n] + shift_tile(cells, at))
             work.add(up_to(count_ref[at], CHUNK), up_to(filled, LANES), 0, n * LANES, n * LANES)
         work.run(lists, spread, coefs, acc)
-        merged = lane_sums([acc[i, : EARLY * LANES, :] for i in range(4)])
-        for n in groups:
-            by_row = jnp.transpose(merged[n * LANES : (n + 1) * LANES])[:ROWS]
+        by_rows = lane_sums([acc[i, : EARLY * LANES, :] for i in range(4)], EARLY)
+        for n, by_row in enumerate(by_rows):
             early_ref[n] = velocity_rows(cells, n, by_row, tiles[n])
 
 
@@ -291,11 +296,11 @@
     copy.wait()
     count_ref = {at: count_s[COUNT_ROW, n] for n, at in enumerate(bins)}
     list_own(cells, count_ref, own_ref, listed)
-    filled, _, many = is_full(cells, count_ref)
+    filled, full, many = is_full(cells, count_ref)
     spread_rows(lists, 0, listed, 0, up_to(filled, LANES), len(bins))
     work = Groups(tables)
     for m, n in enumerate(FIRST):
-        n_chunks = jnp.where(many, up_to(count_ref[bins[n]], CHUNK), 0)
+        n_chunks = jnp.where(many if n in FIRST_IF_MANY else full, up_to(count_ref[bins[n]], CHUNK), 0)
         work.add(n_chunks, up_to(filled, LANES), 0, n * LANES, m * LANES)
     work.run(lists, spread, coefs, acc)
 
@@ -335,7 +340,7 @@
     for n in SECOND:
         n_chunks = up_to(count_ref[bins[n]], CHUNK)
         if n < EARLY or n in FIRST:
-            n_chunks = jnp.where(full if n < EARLY else many, 0, n_chunks)
+            n_chunks = jnp.where(many if n in FIRST_IF_MANY else full, 0, n_chunks)
         work.add(n_chunks, up_to(filled, LANES), 0, n * LANES, n * LANES)
     work.run(lists, spread, coefs, acc)
 
@@ -395,9 +400,8 @@
     work.run(lists, spread, coefs, acc)
 
     slot = lax.broadcasted_iota(jnp.int32, (1, LANES), 1)
-    merged = lane_sums([acc[i, : len(bins) * LANES, :] for i in range(4)])
-    for n, at in enumerate(bins):
-        by_row = jnp.transpose(merged[n * LANES : (n + 1) * LANES])[:ROWS]
+    by_rows = lane_sums([acc[i, : len(bins) * LANES, :] for i in range(4)], len(bins))
+    for n, (at, by_row) in enumerate(zip(bins, by_rows)):
         tile = own_ref[at]
         total = velocity_rows(cells, n, by_row, tile)
         total = total - (STOKES_NORM * SELF_C) * pltpu.roll(tile, ROWS - FORCE_ROW, 0)
@@ -408,13 +412,18 @@
             out_ref[i, at[0], at[1], at[2] : at[2] + 1, :] = total[i : i + 1]
 
 
-def shifted(array, axis, dim):
-    size, length = lax.axis_size(axis), array.shape[dim]
+def shifted(first, last, axis):
+    size = lax.axis_size(axis)
     up = [(i, (i + 1) % size) for i in range(size)]
-    down = [(j, i) for i, j in up]
-    after = lax.ppermute(lax.slice_in_dim(array, 0, 1, axis=dim), axis, down)
-    before = lax.ppermute(lax.slice_in_dim(array, length - 1, length, axis=dim), axis, up)
-    return before, after
+    if size % 2:
+        down = [(j, i) for i, j in up]
+        return lax.ppermute(last, axis, up), lax.ppermute(first, axis, down)
+    odd = lax.rem(lax.axis_index(axis), 2) == 1
+    got = []
+    for parity in (0, 1):
+        pairs = [pair for i, j in up if i % 2 == parity for pair in ((i, j), (j, i))]
+        got.append(lax.ppermute(jnp.where(odd == bool(parity), last, first), axis, pairs))
+    return jnp.where(odd, got[0], got[1]), jnp.where(odd, got[1], got[0])
 
 
 def on_device(offsets, forces, counts):
@@ -486,7 +495,7 @@
     )(sent)
     other, own, listed, first = together((other, own, listed, first))
     column = jnp.concatenate([own, other], axis=2)
-    x_lo, x_hi = shifted(column, "gx", 0)
+    x_lo, x_hi = shifted(column[:1], column[cells[0] - 1 :], "gx")
     second = pl.pallas_call(
         functools.partial(second_kernel, cells),
         out_shape=floats(4, n_targets + CHUNK, slots),
@@ -499,9 +508,9 @@
         cost_estimate=cost,
         name="second",
     )(counts, other, listed, spread, first)
-    x_lo, x_hi, second = together((x_lo, x_hi, second))
+    x_hi, x_lo, second = together((x_hi, x_lo, second))
     wide = jnp.concatenate([x_lo, column, x_hi], axis=0)
-    y_lo, y_hi = shifted(wide, "gy", 1)
+    y_lo, y_hi = shifted(wide[:, :1], wide[:, cells[1] - 1 :], "gy")
     middle = pl.pallas_call(
         functools.partial(middle_kernel, cells),
         out_shape=floats(4, n_targets + CHUNK, slots),

time: 27.8 us -> 27.4 us (0.986); the launches traced: 28.2 us -> 27.2 us
  waiting for transfers between devices: 1.24 us -> 0.49 us
  Pallas kernels: 24.1 us -> 23.4 us
  starting transfers between devices: 2.7 us -> 3.12 us
    ppermute x1, waiting for transfers between devices: 1.23 us -> 0.48 us  [on_device(): other = lax.ppermute(sent, 'ha', [(i, (i + 1) % size) for i in range(size)])]
    pallas_call x1, Pallas kernels: 5.52 us -> 4.83 us  [on_device(): pl.pallas_call(functools.partial(second_kernel, cells), out_shape=floats(...]
    pallas_call x1, Pallas kernels: 2.67 us -> 3.32 us  [on_device(): pl.pallas_call(functools.partial(first_kernel, cells), out_shape=[sent, o...]
    pallas_call x1, Pallas kernels: 4.21 us -> 3.74 us  [on_device(): pl.pallas_call(functools.partial(pack_kernel, cells), out_shape=[floats(*...]
    ppermute x4, starting transfers between devices: 2.63 us -> 2.96 us  [shifted(): lax.ppermute(jnp.where(odd == bool(parity), last, first), axis, pairs)]
where the time goes in v3:
time: 27.4 us; the launch traced here: 27.2 us
  Pallas kernels  23.4 us (85%)
  starting transfers between devices  3.12 us (11%)
  waiting for transfers between devices  0.49 us (2%)
    pallas_call x1, Pallas kernels, on_device(): pl.pallas_call(functools.partial(last_kernel, cells), out_shape=floats(3,...  7.63 us
    pallas_call x1, Pallas kernels, on_device(): pl.pallas_call(functools.partial(second_kernel, cells), out_shape=floats(...  4.83 us
    pallas_call x1, Pallas kernels, on_device(): pl.pallas_call(functools.partial(middle_kernel, cells), out_shape=floats(...  3.87 us
    pallas_call x1, Pallas kernels, on_device(): pl.pallas_call(functools.partial(pack_kernel, cells), out_shape=[floats(*...  3.74 us
    pallas_call x1, Pallas kernels, on_device(): pl.pallas_call(functools.partial(first_kernel, cells), out_shape=[sent, o...  3.32 us
    ppermute x4, starting transfers between devices, shifted(): lax.ppermute(jnp.where(odd == bool(parity), last, first), axis, pairs)  2.96 us
  transfers between devices with their start and end apart: 5, of which 1 were waited for; matrix products, arithmetic and copies ran while one was open for 0% of the time, Pallas kernels for 44%

profile of v3, /device:TPU:0, one launch (start us, length us, event | category | flops | bytes accessed | tf_op | source)
XLA Modules:
  0.0 27.2 jit_solution(1210269341416778908)
XLA Ops:
  0.0 0.0 copy-start
  0.0 3.7 %pack.1 = (f32[2,2,2,8,128]{4,3,2,1,0:T(8,128)S(1)}, f32[3,8,128]{2,1,0:T(8,128)S(1)}) custom-call(s32[2,2,2]{2,1,0:T(2,128)} %count_ref.5, f32[3,2,2,2,128]{4,3,2,1,0:T(2,128)} %offset_hbm.1, f32[3,2,2,2,128]{4,3,2,1,0:T(2,128)} %force_hbm.1), custom_call_target="tpu_custom_call" | custom-call | tf_op jit(solution)/shard_map/pack/pallas_call | solution.py:460
  3.8 0.2 collective-permute-start
  3.9 3.3 %first.1 = (f32[2,2,2,8,128]{4,3,2,1,0:T(8,128)S(1)}, f32[8,6,8,128]{3,2,1,0:T(8,128)S(1)}, f32[3,1024,128]{2,1,0:T(8,128)S(1)}, f32[4,416,128]{2,1,0:T(8,128)S(1)}) custom-call(f32[2,2,2,8,128]{4,3,2,1,0:T(8,128)S(1)} %get-tuple-element.21.sent_ref), custom_call_target="tpu_custom_call" | custom-call | flops 268435456 | bytes 65536 | tf_op jit(solution)/shard_map/first/pallas_call | solution.py:484
  7.3 0.5 %collective-permute-done.other = f32[2,2,2,8,128]{4,3,2,1,0:T(8,128)S(1)} collective-permute-done((f32[2,2,2,8,128]{4,3,2,1,0:T(8,128)S(1)}, f32[2,2,2,8,128]{4,3,2,1,0:T(8,128)S(1)}, u32[]{:S(2)}, u32[]{:S(2)}) %collective-permute-start) | collective-permute-done | bytes 32800 | tf_op jit(solution)/shard_map/ppermute | solution.py:483
  7.8 2.2 %collective-permute-start.1 = (f32[1,2,4,8,128]{4,3,2,1,0:T(8,128)S(1)}, f32[1,2,4,8,128]{4,3,2,1,0:T(8,128)S(1)}, u32[]{:S(2)}, u32[]{:S(2)}) collective-permute-start(f32[1,2,4,8,128]{4,3,2,1,0:T(8,128)S(1)} %get-tuple-element.44), channel_id=1, source_target_pairs={{8,16},{16,8},{24,0},{0,24},{9,17},{17,9},{25,1},{1,25},{10,18},{1... | collective-permute-start | bytes 98312 | tf_op jit(solution)/shard_map/ppermute | solution.py:425
  10.0 0.0 collective-permute-start.2
  10.0 0.0 copy-done
  10.0 4.8 %second.1 = f32[4,1056,128]{2,1,0:T(8,128)S(1)} custom-call(s32[2,2,2]{2,1,0:T(2,128)S(1)} %copy-done, f32[2,2,2,8,128]{4,3,2,1,0:T(8,128)S(1)} %collective-permute-done.other, f32[8,6,8,128]{3,2,1,0:T(8,128)S(1)} %get-tuple-element.27.own_lists, f32[3,1024,128]{2,1,0:T(8,128)S(1)} %get-tuple-element.28.spread, f32[4,416,128]{2,1,0:T(8,128)S(1)} %get-tuple-element.29.first), custom_call_target="tpu_custom_call" | custom-call | flops 268435456 | bytes 65536 | tf_op jit(solution)/shard_map/second/pallas_call | solution.py:499
  14.9 0.0 collective-permute-done.1
  14.9 0.0 collective-permute-done.2
  14.9 0.1 collective-permute-start.3
  15.0 0.6 %collective-permute-start.4 = (f32[4,1,4,8,128]{4,3,2,1,0:T(8,128)S(1)}, f32[4,1,4,8,128]{4,3,2,1,0:T(8,128)S(1)}, u32[]{:S(2)}, u32[]{:S(2)}) collective-permute-start(f32[4,1,4,8,128]{4,3,2,1,0:T(8,128)S(1)} %get-tuple-element.39), channel_id=1, source_target_pairs={{2,4},{4,2},{6,0},{0,6},{3,5},{5,3},{7,1},{1,7},{10,12},{12,10},{1... | collective-permute-start | bytes 196616 | tf_op jit(solution)/shard_map/ppermute | solution.py:425
  15.7 3.9 %middle.1.refs_0_ = f32[4,1056,128]{2,1,0:T(8,128)S(1)} custom-call(s32[2,2,2]{2,1,0:T(2,128)S(1)} %copy-done, f32[4,2,4,8,128]{4,3,2,1,0:T(8,128)S(1)} %pad_maximum_fusion.wide, f32[3,1024,128]{2,1,0:T(8,128)S(1)} %get-tuple-element.28.spread, f32[4,1056,128]{2,1,0:T(8,128)S(1)} %second.1), custom_call_target="tpu_custom_call" | custom-call | flops 268435456 | bytes 65536 | tf_op jit(solution)/shard_map/middle/pallas_call | solution.py:514
  19.5 0.0 collective-permute-done.3
  19.5 0.0 collective-permute-done.4
  19.6 7.6 %last.1 = f32[3,2,2,2,128]{4,3,2,1,0:T(2,128)} custom-call(s32[2,2,2]{2,1,0:T(2,128)S(1)} %copy-done, f32[2,2,2,8,128]{4,3,2,1,0:T(8,128)S(1)} %get-tuple-element.25.own_ref, f32[4,1,4,8,128]{4,3,2,1,0:T(8,128)S(1)} %get-tuple-element.33.y_lo, f32[4,1,4,8,128]{4,3,2,1,0:T(8,128)S(1)} %get-tuple-element.34.y_hi, ...), custom_call_target="tpu_custom_call" | custom-call | flops 268435456 | bytes 65536 | tf_op jit(solution)/shard_map/last/pallas_call | solution.py:525
  (7 shorter events, 0.1 us)
Async XLA Ops:
  0.0 10.0 %copy-start = (s32[2,2,2]{2,1,0:T(2,128)S(1)}, s32[2,2,2]{2,1,0:T(2,128)}, u32[]{:S(2)}) copy-start(s32[2,2,2]{2,1,0:T(2,128)} %count_ref.5) | copy-start | bytes 100
  3.8 4.0 %collective-permute-start = (f32[2,2,2,8,128]{4,3,2,1,0:T(8,128)S(1)}, f32[2,2,2,8,128]{4,3,2,1,0:T(8,128)S(1)}, u32[]{:S(2)}, u32[]{:S(2)}) collective-permute-start(f32[2,2,2,8,128]{4,3,2,1,0:T(8,128)S(1)} %get-tuple-element.21.sent_ref), channel_id=1, source_target_pairs={{0,1},{1,0},{2,3},{3,2},{4,5},{5,4},{6,7},{7,6},{8,9},{9,8},{10,11... | collective-permute-start | bytes 98312 | tf_op jit(solution)/shard_map/ppermute | solution.py:483
  7.8 7.1 %collective-permute-start.1 = (f32[1,2,4,8,128]{4,3,2,1,0:T(8,128)S(1)}, f32[1,2,4,8,128]{4,3,2,1,0:T(8,128)S(1)}, u32[]{:S(2)}, u32[]{:S(2)}) collective-permute-start(f32[1,2,4,8,128]{4,3,2,1,0:T(8,128)S(1)} %get-tuple-element.44), channel_id=1, source_target_pairs={{8,16},{16,8},{24,0},{0,24},{9,17},{17,9},{25,1},{1,25},{10,18},{1... | collective-permute-start | bytes 98312 | tf_op jit(solution)/shard_map/ppermute | solution.py:425
  10.0 4.9 %collective-permute-start.2 = (f32[1,2,4,8,128]{4,3,2,1,0:T(8,128)S(1)}, f32[1,2,4,8,128]{4,3,2,1,0:T(8,128)S(1)}, u32[]{:S(2)}, u32[]{:S(2)}) collective-permute-start(f32[1,2,4,8,128]{4,3,2,1,0:T(8,128)S(1)} %get-tuple-element.43), channel_id=1, source_target_pairs={{0,8},{8,0},{16,24},{24,16},{1,9},{9,1},{17,25},{25,17},{2,10},{10... | collective-permute-start | bytes 98312 | tf_op jit(solution)/shard_map/ppermute | solution.py:425
  14.9 4.6 %collective-permute-start.3 = (f32[4,1,4,8,128]{4,3,2,1,0:T(8,128)S(1)}, f32[4,1,4,8,128]{4,3,2,1,0:T(8,128)S(1)}, u32[]{:S(2)}, u32[]{:S(2)}) collective-permute-start(f32[4,1,4,8,128]{4,3,2,1,0:T(8,128)S(1)} %get-tuple-element.40), channel_id=1, source_target_pairs={{0,2},{2,0},{4,6},{6,4},{1,3},{3,1},{5,7},{7,5},{8,10},{10,8},{12,... | collective-permute-start | bytes 196616 | tf_op jit(solution)/shard_map/ppermute | solution.py:425
  15.0 4.5 %collective-permute-start.4 = (f32[4,1,4,8,128]{4,3,2,1,0:T(8,128)S(1)}, f32[4,1,4,8,128]{4,3,2,1,0:T(8,128)S(1)}, u32[]{:S(2)}, u32[]{:S(2)}) collective-permute-start(f32[4,1,4,8,128]{4,3,2,1,0:T(8,128)S(1)} %get-tuple-element.39), channel_id=1, source_target_pairs={{2,4},{4,2},{6,0},{0,6},{3,5},{5,3},{7,1},{1,7},{10,12},{12,10},{1... | collective-permute-start | bytes 196616 | tf_op jit(solution)/shard_map/ppermute | solution.py:425

commit v4 on v3

--- a/solution.py
+++ b/solution.py
@@ -25,7 +25,7 @@
 CHUNK = 32
 UNITS = 8
 COUNT_ROW = 3
-FULL = 640
+FULL = 700
 MANY = 440
 EARLY = 3
 FIRST = (3, 4, 5)
@@ -70,20 +70,6 @@
     return filled
 
 
-def spread_rows(lists, to, listed, base, n_tiles, most):
-    def some(tiles):
-        for n in tiles:
-            for i, row in enumerate((0, 1, 2, 4, 5, 6)):
-                lists[to + n, i] = jnp.broadcast_to(listed[base + n, row : row + 1, :], (ROWS, LANES))
-
-    likely = min(5, most)
-    some(range(likely))
-
-    @pl.when(n_tiles > likely)
-    def _():
-        some(range(likely, most))
-
-
 def up_to(count, size):
     return lax.shift_right_logical(count + (size - 1), size.bit_length() - 1)
 
@@ -135,13 +121,13 @@
         self.size += 1
         self.total = self.total + n_chunks * n_tiles
 
-    def run(self, lists, spread, coefs, acc):
+    def run(self, listed, spread, coefs, acc):
         chunks_of, tiles_of, list_of, spread_of, acc_of = self.tables
         trash = acc.shape[1] - CHUNK
 
         def rows(tile_id):
-            wide = [jnp.concatenate([lists[tile_id, i]] * (CHUNK // ROWS), axis=0) for i in range(6)]
-            return wide[:3], wide[3:]
+            single = [listed[tile_id, i : i + 1, :] for i in (0, 1, 2, 4, 5, 6)]
+            return single[:3], single[3:]
 
         def advance(group, chunk, tile):
             end_tile = tile + 1 == tiles_of[group]
@@ -230,7 +216,7 @@
 
 
 def pack_kernel(cells, count_hbm, offset_hbm, force_hbm, own_ref, early_ref, *refs):
-    (count_ref, offset_v, force_v, sems, listed, lists, spread, coefs, acc), tables = refs[:9], refs[9:]
+    (count_ref, offset_v, force_v, sems, listed, spread, coefs, acc), tables = refs[:8], refs[8:]
     copies = [
         pltpu.make_async_copy(source, target, sems.at[n])
         for n, (source, target) in enumerate(
@@ -259,7 +245,6 @@
     @pl.when(full)
     def _():
         list_own(cells, count_ref, own_ref, listed)
-        spread_rows(lists, 0, listed, 0, up_to(filled, LANES), len(bins_of(cells)))
         acc[...] = jnp.zeros_like(acc)
         groups = range(EARLY)
         tiles = [own_ref[bins_of(cells)[n]] for n in groups]
@@ -268,48 +253,37 @@
             at = bins_of(cells)[n]
             spread_targets(spread, n * LANES, tiles[n] + shift_tile(cells, at))
             work.add(up_to(count_ref[at], CHUNK), up_to(filled, LANES), 0, n * LANES, n * LANES)
-        work.run(lists, spread, coefs, acc)
+        work.run(listed, spread, coefs, acc)
         by_rows = lane_sums([acc[i, : EARLY * LANES, :] for i in range(4)], EARLY)
         for n, by_row in enumerate(by_rows):
             early_ref[n] = velocity_rows(cells, n, by_row, tiles[n])
 
 
-def counts_of(tiles, count_v, count_s, sem):
-    _, lane = rows_and_lanes()
-    held = jnp.zeros((ROWS, LANES), jnp.float32)
-    for cell, tile in enumerate(tiles):
-        held = jnp.where(lane == cell, tile, held)
-    count_v[...] = held.astype(jnp.int32)
-    copy = pltpu.make_async_copy(count_v, count_s, sem)
-    copy.start()
-    return copy
-
-
-def first_kernel(cells, sent_ref, own_ref, lists, spread, acc, listed, coefs, *refs):
-    tables, (count_v, count_s, sem) = refs[:5], refs[5:]
+def counts_of(tiles):
+    return [tile[COUNT_ROW, 0].astype(jnp.int32) for tile in tiles]
+
+
+def first_kernel(cells, sent_ref, own_ref, listed, spread, acc, coefs, *tables):
     bins = bins_of(cells)
-    copy = counts_of([sent_ref[at] for at in bins], count_v, count_s, sem)
+    count_s = counts_of([sent_ref[at] for at in bins])
     own_ref[...] = sent_ref[...]
     for n, at in enumerate(bins):
         spread_targets(spread, n * LANES, own_ref[at] + shift_tile(cells, at))
     acc[...] = jnp.zeros_like(acc)
-    copy.wait()
-    count_ref = {at: count_s[COUNT_ROW, n] for n, at in enumerate(bins)}
+    count_ref = {at: count_s[n] for n, at in enumerate(bins)}
     list_own(cells, count_ref, own_ref, listed)
     filled, full, many = is_full(cells, count_ref)
-    spread_rows(lists, 0, listed, 0, up_to(filled, LANES), len(bins))
     work = Groups(tables)
     for m, n in enumerate(FIRST):
         n_chunks = jnp.where(many if n in FIRST_IF_MANY else full, up_to(count_ref[bins[n]], CHUNK), 0)
         work.add(n_chunks, up_to(filled, LANES), 0, n * LANES, m * LANES)
-    work.run(lists, spread, coefs, acc)
-
-
-def second_kernel(cells, count_ref, other, own_lists, spread, first, acc, listed, lists, coefs, *refs):
-    tables, (count_v, count_s, sem) = refs[:5], refs[5:]
+    work.run(listed, spread, coefs, acc)
+
+
+def second_kernel(cells, count_ref, other, own_list, spread, first, acc, listed, coefs, *tables):
     bins = bins_of(cells)
     size_x, size_y, size_z = cells
-    copy = counts_of([other[at] for at in bins], count_v, count_s, sem)
+    count_s = counts_of([other[at] for at in bins])
     for n in range(len(bins)):
         here = slice(n * LANES, (n + 1) * LANES)
         if n in FIRST:
@@ -317,11 +291,10 @@
             acc[:, here, :] = first[:, m * LANES : (m + 1) * LANES, :]
         else:
             acc[:, here, :] = jnp.zeros((4, LANES, LANES), jnp.float32)
-    n_own = own_lists.shape[0]
+    n_own = own_list.shape[0]
     for n in range(n_own):
-        lists[n] = own_lists[n]
+        listed[n] = own_list[n]
     filled, full, many = is_full(cells, count_ref)
-    copy.wait()
     work = Groups(tables)
     for bz in range(size_z):
         z = (-1, size_z)[bz]
@@ -330,10 +303,9 @@
             for y in range(size_y):
                 place = (x, y, z % size_z)
                 tile = other[place] + shift_tile(cells, (x, y, z))
-                sources.append((tile, count_s[COUNT_ROW, bins.index(place)]))
-        n_tiles = up_to(compact(listed, bz * LIST_Z, sources), LANES)
-        first_tile = n_own + bz * (LIST_Z - 1)
-        spread_rows(lists, first_tile, listed, bz * LIST_Z, n_tiles, LIST_Z - 1)
+                sources.append((tile, count_s[bins.index(place)]))
+        first_tile = n_own + bz * LIST_Z
+        n_tiles = up_to(compact(listed, first_tile, sources), LANES)
         for n, at in enumerate(bins):
             if at[2] == bz:
                 work.add(up_to(count_ref[at], CHUNK), n_tiles, first_tile, n * LANES, n * LANES)
@@ -342,18 +314,16 @@
         if n < EARLY or n in FIRST:
             n_chunks = jnp.where(many if n in FIRST_IF_MANY else full, 0, n_chunks)
         work.add(n_chunks, up_to(filled, LANES), 0, n * LANES, n * LANES)
-    work.run(lists, spread, coefs, acc)
-
-
-def middle_kernel(cells, count_ref, wide, spread, second, acc, listed, lists, coefs, *refs):
-    tables, (count_v, count_s, sem) = refs[:5], refs[5:]
+    work.run(listed, spread, coefs, acc)
+
+
+def middle_kernel(cells, count_ref, wide, spread, second, acc, listed, coefs, *tables):
     size_x, size_y, size_z = cells
     n_z = 2 * size_z
     bins = bins_of(cells)
     places = [(i, j, k) for i in (0, size_x + 1) for j in range(size_y) for k in range(n_z)]
-    copy = counts_of([wide[at] for at in places], count_v, count_s, sem)
+    count_s = counts_of([wide[at] for at in places])
     acc[...] = second[...]
-    copy.wait()
     work = Groups(tables)
     for bx in range(size_x):
         for bz in range(size_z):
@@ -363,28 +333,24 @@
                 for z in (bz - 1, bz, bz + 1):
                     place = (x + 1, y, z % n_z)
                     tile = wide[place] + shift_tile(cells, (x, y, z))
-                    sources.append((tile, count_s[COUNT_ROW, places.index(place)]))
-            n_list = bx * size_z + bz
-            n_tiles = up_to(compact(listed, n_list * LIST_X, sources), LANES)
-            first_tile = n_list * (LIST_X - 1)
-            spread_rows(lists, first_tile, listed, n_list * LIST_X, n_tiles, LIST_X - 1)
+                    sources.append((tile, count_s[places.index(place)]))
+            first_tile = (bx * size_z + bz) * LIST_X
+            n_tiles = up_to(compact(listed, first_tile, sources), LANES)
             for n, at in enumerate(bins):
                 if (at[0], at[2]) == (bx, bz):
                     work.add(up_to(count_ref[at], CHUNK), n_tiles, first_tile, n * LANES, n * LANES)
-    work.run(lists, spread, coefs, acc)
+    work.run(listed, spread, coefs, acc)
 
 
 def last_kernel(cells, count_ref, own_ref, y_lo, y_hi, spread, *refs):
-    (middle, early, out_ref, acc, listed, lists, coefs), refs = refs[:7], refs[7:]
-    tables, (count_v, count_s, sem) = refs[:5], refs[5:]
+    (middle, early, out_ref, acc, listed, coefs), tables = refs[:6], refs[6:]
     size_x, size_y, size_z = cells
     n_z = 2 * size_z
     bins = bins_of(cells)
     places = [(i, j, k) for i in range(size_x + 2) for j in range(2) for k in range(n_z)]
     tiles = [(y_lo, y_hi)[j][i, 0, k] for i, j, k in places]
-    copy = counts_of(tiles, count_v, count_s, sem)
+    count_s = counts_of(tiles)
     acc[...] = middle[...]
-    copy.wait()
     work = Groups(tables)
     for n, (bx, by, bz) in enumerate(bins):
         sources = []
@@ -392,12 +358,11 @@
             for z in (bz - 1, bz, bz + 1):
                 cell = places.index((x + 1, by, z % n_z))
                 tile = tiles[cell] + shift_tile(cells, (x, (-1, size_y)[by], z))
-                sources.append((tile, count_s[COUNT_ROW, cell]))
+                sources.append((tile, count_s[cell]))
         n_tiles = up_to(compact(listed, n * LIST_Y, sources), LANES)
-        first_tile = n * (LIST_Y - 1)
-        spread_rows(lists, first_tile, listed, n * LIST_Y, n_tiles, LIST_Y - 1)
+        first_tile = n * LIST_Y
         work.add(up_to(count_ref[bx, by, bz], CHUNK), n_tiles, first_tile, n * LANES, n * LANES)
-    work.run(lists, spread, coefs, acc)
+    work.run(listed, spread, coefs, acc)
 
     slot = lax.broadcasted_iota(jnp.int32, (1, LANES), 1)
     by_rows = lane_sums([acc[i, : len(bins) * LANES, :] for i in range(4)], len(bins))
@@ -442,20 +407,12 @@
 
     loop_scratch = [pltpu.VMEM((UNITS, 2, CHUNK, LANES), jnp.float32)]
     loop_scratch += [pltpu.SMEM((2 * n_bins,), jnp.int32)] * 5
-    count_scratch = [
-        pltpu.VMEM((ROWS, LANES), jnp.int32),
-        pltpu.SMEM((ROWS, LANES), jnp.int32),
-        pltpu.SemaphoreType.DMA,
-    ]
     cost = pl.CostEstimate(flops=1 << 28, bytes_accessed=1 << 16, transcendentals=1 << 20)
 
-    def list_scratch(n_lists, n_tiles, more=0):
-        return [
-            pltpu.VMEM((n_lists * n_tiles, ROWS, LANES), jnp.float32),
-            pltpu.VMEM((n_lists * (n_tiles - 1) + more, 6, ROWS, LANES), jnp.float32),
-        ]
-
-    own_lists, all_targets = floats(n_bins, 6, ROWS, slots), floats(3, n_targets, slots)
+    def list_scratch(n_tiles):
+        return [pltpu.VMEM((n_tiles, ROWS, LANES), jnp.float32)]
+
+    own_list, all_targets = floats(n_bins + 1, ROWS, slots), floats(3, n_targets, slots)
     arguments = [pltpu.with_memory_space_constraint(x, pltpu.HBM) for x in (counts, offsets, forces)]
     sent, early = pl.pallas_call(
         functools.partial(pack_kernel, cells),
@@ -467,8 +424,7 @@
             pltpu.VMEM(offsets.shape, jnp.float32),
             pltpu.VMEM(forces.shape, jnp.float32),
             pltpu.SemaphoreType.DMA((3,)),
-            pltpu.VMEM((n_bins + 1, ROWS, LANES), jnp.float32),
-            pltpu.VMEM(own_lists.shape, jnp.float32),
+            pltpu.VMEM(own_list.shape, jnp.float32),
             pltpu.VMEM((3, EARLY * slots, slots), jnp.float32),
             loop_scratch[0],
             pltpu.VMEM((4, EARLY * slots + CHUNK, slots), jnp.float32),
@@ -483,12 +439,10 @@
     other = lax.ppermute(sent, "ha", [(i, (i + 1) % size) for i in range(size)])
     own, listed, spread, first = pl.pallas_call(
         functools.partial(first_kernel, cells),
-        out_shape=[sent, own_lists, all_targets, floats(4, len(FIRST) * slots + CHUNK, slots)],
+        out_shape=[sent, own_list, all_targets, floats(4, len(FIRST) * slots + CHUNK, slots)],
         in_specs=[whole],
         out_specs=[whole] * 4,
-        scratch_shapes=[pltpu.VMEM((n_bins + 1, ROWS, LANES), jnp.float32)]
-        + loop_scratch
-        + count_scratch,
+        scratch_shapes=loop_scratch,
         compiler_params=params(8),
         cost_estimate=cost,
         name="first",
@@ -501,9 +455,8 @@
         out_shape=floats(4, n_targets + CHUNK, slots),
         in_specs=[scalars] + [whole] * 4,
         out_specs=whole,
-        scratch_shapes=list_scratch(cells[2], LIST_Z, n_bins)
-        + loop_scratch
-        + count_scratch,
+        scratch_shapes=list_scratch(cells[2] * LIST_Z + n_bins + 1)
+        + loop_scratch,
         compiler_params=params(8),
         cost_estimate=cost,
         name="second",
@@ -516,7 +469,7 @@
         out_shape=floats(4, n_targets + CHUNK, slots),
         in_specs=[scalars] + [whole] * 3,
         out_specs=whole,
-        scratch_shapes=list_scratch(cells[0] * cells[2], LIST_X) + loop_scratch + count_scratch,
+        scratch_shapes=list_scratch(cells[0] * cells[2] * LIST_X) + loop_scratch,
         compiler_params=params(8),
         cost_estimate=cost,
         name="middle",
@@ -528,9 +481,8 @@
         in_specs=[scalars] + [whole] * 6,
         out_specs=whole,
         scratch_shapes=[pltpu.VMEM((4, n_targets + CHUNK, slots), jnp.float32)]
-        + list_scratch(n_bins, LIST_Y)
-        + loop_scratch
-        + count_scratch,
+        + list_scratch(n_bins * LIST_Y)
+        + loop_scratch,
         compiler_params=params(12),
         cost_estimate=cost,
         name="last",

time: 27.4 us -> 25.8 us (0.942); the launches traced: 27.2 us -> 25.9 us
  Pallas kernels: 23.4 us -> 20.5 us
  waiting for transfers between devices: 0.49 us -> 1.88 us
    pallas_call x1, Pallas kernels: 7.63 us -> 6 us  [on_device(): pl.pallas_call(functools.partial(last_kernel, cells), out_shape=floats(3,...]
    pallas_call x1, Pallas kernels: 4.83 us -> 3.45 us  [on_device(): pl.pallas_call(functools.partial(second_kernel, cells), out_shape=floats(...]
    ppermute x4, waiting for transfers between devices: 0.01 us -> 0.78 us  [shifted(): lax.ppermute(jnp.where(odd == bool(parity), last, first), axis, pairs)]
    ppermute x1, waiting for transfers between devices: 0.48 us -> 1.1 us  [on_device(): other = lax.ppermute(sent, 'ha', [(i, (i + 1) % size) for i in range(size)])]
    pallas_call x1, Pallas kernels: 3.32 us -> 2.79 us  [on_device(): pl.pallas_call(functools.partial(first_kernel, cells), out_shape=[sent, o...]
    pallas_call x1, Pallas kernels: 3.74 us -> 4.1 us  [on_device(): pl.pallas_call(functools.partial(pack_kernel, cells), out_shape=[floats(*...]
    pallas_call x1, Pallas kernels: 3.87 us -> 4.17 us  [on_device(): pl.pallas_call(functools.partial(middle_kernel, cells), out_shape=floats(...]
    ppermute x4, starting transfers between devices: 2.96 us -> 3.25 us  [shifted(): lax.ppermute(jnp.where(odd == bool(parity), last, first), axis, pairs)]
  transfers between devices with their start and end apart: 5 -> 5, of which waited for: 1 -> 3; matrix products, arithmetic and copies ran while one was open for 0% -> 0% of each run, Pallas kernels for 44% -> 40%
where the time goes in v4:
time: 25.8 us; the launch traced here: 25.9 us
  Pallas kernels  20.5 us (79%)
  starting transfers between devices  3.32 us (13%)
  waiting for transfers between devices  1.88 us (7%)
    pallas_call x1, Pallas kernels, on_device(): pl.pallas_call(functools.partial(last_kernel, cells), out_shape=floats(3,...  6 us
    pallas_call x1, Pallas kernels, on_device(): pl.pallas_call(functools.partial(middle_kernel, cells), out_shape=floats(...  4.17 us
    pallas_call x1, Pallas kernels, on_device(): pl.pallas_call(functools.partial(pack_kernel, cells), out_shape=[floats(*...  4.1 us
    pallas_call x1, Pallas kernels, on_device(): pl.pallas_call(functools.partial(second_kernel, cells), out_shape=floats(...  3.45 us
    ppermute x4, starting transfers between devices, shifted(): lax.ppermute(jnp.where(odd == bool(parity), last, first), axis, pairs)  3.25 us
    pallas_call x1, Pallas kernels, on_device(): pl.pallas_call(functools.partial(first_kernel, cells), out_shape=[sent, o...  2.79 us
    ppermute x1, waiting for transfers between devices, on_device(): other = lax.ppermute(sent, 'ha', [(i, (i + 1) % size) for i in range(size)])  1.1 us
    ppermute x4, waiting for transfers between devices, shifted(): lax.ppermute(jnp.where(odd == bool(parity), last, first), axis, pairs)  0.78 us
  transfers between devices with their start and end apart: 5, of which 3 were waited for; matrix products, arithmetic and copies ran while one was open for 0% of the time, Pallas kernels for 40%

profile of v4, /device:TPU:0, one launch (start us, length us, event | category | flops | bytes accessed | tf_op | source)
XLA Modules:
  0.0 25.9 jit_solution(13964248315366879483)
XLA Ops:
  0.0 0.0 copy-start
  0.0 4.1 %pack.1 = (f32[2,2,2,8,128]{4,3,2,1,0:T(8,128)S(1)}, f32[3,8,128]{2,1,0:T(8,128)S(1)}) custom-call(s32[2,2,2]{2,1,0:T(2,128)} %count_ref.5, f32[3,2,2,2,128]{4,3,2,1,0:T(2,128)} %offset_hbm.1, f32[3,2,2,2,128]{4,3,2,1,0:T(2,128)} %force_hbm.1), custom_call_target="tpu_custom_call" | custom-call | tf_op jit(solution)/shard_map/pack/pallas_call | solution.py:417
  4.1 0.1 collective-permute-start
  4.2 2.8 %first.1 = (f32[2,2,2,8,128]{4,3,2,1,0:T(8,128)S(1)}, f32[9,8,128]{2,1,0:T(8,128)S(1)}, f32[3,1024,128]{2,1,0:T(8,128)S(1)}, f32[4,416,128]{2,1,0:T(8,128)S(1)}) custom-call(f32[2,2,2,8,128]{4,3,2,1,0:T(8,128)S(1)} %get-tuple-element.21.sent_ref), custom_call_target="tpu_custom_call" | custom-call | flops 268435456 | bytes 65536 | tf_op jit(solution)/shard_map/first/pallas_call | solution.py:440
  7.0 1.1 %collective-permute-done.other = f32[2,2,2,8,128]{4,3,2,1,0:T(8,128)S(1)} collective-permute-done((f32[2,2,2,8,128]{4,3,2,1,0:T(8,128)S(1)}, f32[2,2,2,8,128]{4,3,2,1,0:T(8,128)S(1)}, u32[]{:S(2)}, u32[]{:S(2)}) %collective-permute-start) | collective-permute-done | bytes 32800 | tf_op jit(solution)/shard_map/ppermute | solution.py:439
  8.1 1.9 %collective-permute-start.1 = (f32[1,2,4,8,128]{4,3,2,1,0:T(8,128)S(1)}, f32[1,2,4,8,128]{4,3,2,1,0:T(8,128)S(1)}, u32[]{:S(2)}, u32[]{:S(2)}) collective-permute-start(f32[1,2,4,8,128]{4,3,2,1,0:T(8,128)S(1)} %get-tuple-element.44), channel_id=1, source_target_pairs={{8,16},{16,8},{24,0},{0,24},{9,17},{17,9},{25,1},{1,25},{10,18},{1... | collective-permute-start | bytes 98312 | tf_op jit(solution)/shard_map/ppermute | solution.py:390
  10.0 0.0 collective-permute-start.2
  10.0 0.0 copy-done
  10.0 3.5 %second.1 = f32[4,1056,128]{2,1,0:T(8,128)S(1)} custom-call(s32[2,2,2]{2,1,0:T(2,128)S(1)} %copy-done, f32[2,2,2,8,128]{4,3,2,1,0:T(8,128)S(1)} %collective-permute-done.other, f32[9,8,128]{2,1,0:T(8,128)S(1)} %get-tuple-element.27.own_list, f32[3,1024,128]{2,1,0:T(8,128)S(1)} %get-tuple-element.28.spread, f32[4,416,128]{2,1,0:T(8,128)S(1)} %get-tuple-element.29.first), custom_call_target="tpu_custom_call" | custom-call | flops 268435456 | bytes 65536 | tf_op jit(solution)/shard_map/second/pallas_call | solution.py:453
  13.5 0.5 %collective-permute-done.1 = f32[1,2,4,8,128]{4,3,2,1,0:T(8,128)S(1)} collective-permute-done((f32[1,2,4,8,128]{4,3,2,1,0:T(8,128)S(1)}, f32[1,2,4,8,128]{4,3,2,1,0:T(8,128)S(1)}, u32[]{:S(2)}, u32[]{:S(2)}) %collective-permute-start.1) | collective-permute-done | bytes 32800 | tf_op jit(solution)/shard_map/ppermute | solution.py:390
  13.9 0.3 %collective-permute-done.2 = f32[1,2,4,8,128]{4,3,2,1,0:T(8,128)S(1)} collective-permute-done((f32[1,2,4,8,128]{4,3,2,1,0:T(8,128)S(1)}, f32[1,2,4,8,128]{4,3,2,1,0:T(8,128)S(1)}, u32[]{:S(2)}, u32[]{:S(2)}) %collective-permute-start.2) | collective-permute-done | bytes 32800 | tf_op jit(solution)/shard_map/ppermute | solution.py:390
  14.3 0.1 collective-permute-start.3
  14.4 1.3 %collective-permute-start.4 = (f32[4,1,4,8,128]{4,3,2,1,0:T(8,128)S(1)}, f32[4,1,4,8,128]{4,3,2,1,0:T(8,128)S(1)}, u32[]{:S(2)}, u32[]{:S(2)}) collective-permute-start(f32[4,1,4,8,128]{4,3,2,1,0:T(8,128)S(1)} %get-tuple-element.39), channel_id=1, source_target_pairs={{2,4},{4,2},{6,0},{0,6},{3,5},{5,3},{7,1},{1,7},{10,12},{12,10},{1... | collective-permute-start | bytes 196616 | tf_op jit(solution)/shard_map/ppermute | solution.py:390
  15.7 4.2 %middle.1.refs_0_ = f32[4,1056,128]{2,1,0:T(8,128)S(1)} custom-call(s32[2,2,2]{2,1,0:T(2,128)S(1)} %copy-done, f32[4,2,4,8,128]{4,3,2,1,0:T(8,128)S(1)} %pad_maximum_fusion.wide, f32[3,1024,128]{2,1,0:T(8,128)S(1)} %get-tuple-element.28.spread, f32[4,1056,128]{2,1,0:T(8,128)S(1)} %second.1), custom_call_target="tpu_custom_call" | custom-call | flops 268435456 | bytes 65536 | tf_op jit(solution)/shard_map/middle/pallas_call | solution.py:467
  19.8 0.0 collective-permute-done.3
  19.9 0.0 collective-permute-done.4
  19.9 6.0 %last.1 = f32[3,2,2,2,128]{4,3,2,1,0:T(2,128)} custom-call(s32[2,2,2]{2,1,0:T(2,128)S(1)} %copy-done, f32[2,2,2,8,128]{4,3,2,1,0:T(8,128)S(1)} %get-tuple-element.25.own_ref, f32[4,1,4,8,128]{4,3,2,1,0:T(8,128)S(1)} %get-tuple-element.33.y_lo, f32[4,1,4,8,128]{4,3,2,1,0:T(8,128)S(1)} %get-tuple-element.34.y_hi, ...), custom_call_target="tpu_custom_call" | custom-call | flops 268435456 | bytes 65536 | tf_op jit(solution)/shard_map/last/pallas_call | solution.py:478
  (7 shorter events, 0.1 us)
Async XLA Ops:
  0.0 10.0 %copy-start = (s32[2,2,2]{2,1,0:T(2,128)S(1)}, s32[2,2,2]{2,1,0:T(2,128)}, u32[]{:S(2)}) copy-start(s32[2,2,2]{2,1,0:T(2,128)} %count_ref.5) | copy-start | bytes 100
  4.1 4.0 %collective-permute-start = (f32[2,2,2,8,128]{4,3,2,1,0:T(8,128)S(1)}, f32[2,2,2,8,128]{4,3,2,1,0:T(8,128)S(1)}, u32[]{:S(2)}, u32[]{:S(2)}) collective-permute-start(f32[2,2,2,8,128]{4,3,2,1,0:T(8,128)S(1)} %get-tuple-element.21.sent_ref), channel_id=1, source_target_pairs={{0,1},{1,0},{2,3},{3,2},{4,5},{5,4},{6,7},{7,6},{8,9},{9,8},{10,11... | collective-permute-start | bytes 98312 | tf_op jit(solution)/shard_map/ppermute | solution.py:439
  8.1 5.8 %collective-permute-start.1 = (f32[1,2,4,8,128]{4,3,2,1,0:T(8,128)S(1)}, f32[1,2,4,8,128]{4,3,2,1,0:T(8,128)S(1)}, u32[]{:S(2)}, u32[]{:S(2)}) collective-permute-start(f32[1,2,4,8,128]{4,3,2,1,0:T(8,128)S(1)} %get-tuple-element.44), channel_id=1, source_target_pairs={{8,16},{16,8},{24,0},{0,24},{9,17},{17,9},{25,1},{1,25},{10,18},{1... | collective-permute-start | bytes 98312 | tf_op jit(solution)/shard_map/ppermute | solution.py:390
  10.0 4.2 %collective-permute-start.2 = (f32[1,2,4,8,128]{4,3,2,1,0:T(8,128)S(1)}, f32[1,2,4,8,128]{4,3,2,1,0:T(8,128)S(1)}, u32[]{:S(2)}, u32[]{:S(2)}) collective-permute-start(f32[1,2,4,8,128]{4,3,2,1,0:T(8,128)S(1)} %get-tuple-element.43), channel_id=1, source_target_pairs={{0,8},{8,0},{16,24},{24,16},{1,9},{9,1},{17,25},{25,17},{2,10},{10... | collective-permute-start | bytes 98312 | tf_op jit(solution)/shard_map/ppermute | solution.py:390
  14.3 5.5 %collective-permute-start.3 = (f32[4,1,4,8,128]{4,3,2,1,0:T(8,128)S(1)}, f32[4,1,4,8,128]{4,3,2,1,0:T(8,128)S(1)}, u32[]{:S(2)}, u32[]{:S(2)}) collective-permute-start(f32[4,1,4,8,128]{4,3,2,1,0:T(8,128)S(1)} %get-tuple-element.40), channel_id=1, source_target_pairs={{0,2},{2,0},{4,6},{6,4},{1,3},{3,1},{5,7},{7,5},{8,10},{10,8},{12,... | collective-permute-start | bytes 196616 | tf_op jit(solution)/shard_map/ppermute | solution.py:390
  14.4 5.5 %collective-permute-start.4 = (f32[4,1,4,8,128]{4,3,2,1,0:T(8,128)S(1)}, f32[4,1,4,8,128]{4,3,2,1,0:T(8,128)S(1)}, u32[]{:S(2)}, u32[]{:S(2)}) collective-permute-start(f32[4,1,4,8,128]{4,3,2,1,0:T(8,128)S(1)} %get-tuple-element.39), channel_id=1, source_target_pairs={{2,4},{4,2},{6,0},{0,6},{3,5},{5,3},{7,1},{1,7},{10,12},{12,10},{1... | collective-permute-start | bytes 196616 | tf_op jit(solution)/shard_map/ppermute | solution.py:390

commit v5 on v4

--- a/solution.py
+++ b/solution.py
@@ -97,16 +97,19 @@
         spread[i, first : first + LANES, :] = wide[:, i * LANES : (i + 1) * LANES]
 
 
-def coefficients(target, source, force):
+def separations(target, source, force):
     delta = [t - s for t, s in zip(target, source)]
     u = (delta[0] * delta[0] + SOFT_U) + delta[1] * delta[1] + delta[2] * delta[2]
+    return u, delta[0] * force[0] + delta[1] * force[1] + delta[2] * force[2]
+
+
+def coefficients(u, dot):
     inv = lax.rsqrt(u)
     tail = (1.0 - lax.erf(u * inv)) * inv
     gauss = jnp.exp2(LOG2_G - u * LOG2_E)
     rest = gauss * (u - 1.5)
     coef_d = ((tail - rest) - gauss) * pl.reciprocal(u, approx=True)
-    along = coef_d * (delta[0] * force[0] + delta[1] * force[1] + delta[2] * force[2])
-    return tail + rest, along
+    return tail + rest, coef_d * dot
 
 
 class Groups:
@@ -144,21 +147,24 @@
                 units += [jnp.where(valid, acc_of[group] + chunk, trash), list_of[group] + tile]
                 at = pl.ds(pl.multiple_of(spread_of[group] + chunk, CHUNK), CHUNK)
                 target = [spread[i, at, :] for i in range(3)]
-                found.append(coefficients(target, *rows(units[-1])))
+                found.append(separations(target, *rows(units[-1])))
                 place = advance(*place)
             return found, tuple(units), place
+
+        def weigh():
+            return [coefficients(coefs[n, 0], coefs[n, 1]) for n in range(UNITS)]
 
         def use(units):
             terms = []
             for n, tile in enumerate(units[1::2]):
-                coef_c, along = coefs[n, 0], coefs[n, 1]
+                coef_c, along = coefs[n, 2], coefs[n, 3]
                 source, force = rows(tile)
                 terms.append([coef_c * force[i] - along * source[i] for i in range(3)] + [along])
             return terms
 
-        def keep(found):
-            for n, pair in enumerate(found):
-                coefs[n, 0], coefs[n, 1] = pair
+        def keep(pairs, at):
+            for n, pair in enumerate(pairs):
+                coefs[n, at], coefs[n, at + 1] = pair
 
         def add(units, terms):
             for first, unit in zip(units[::2], terms):
@@ -167,18 +173,30 @@
                     acc[i, at, :] = acc[i, at, :] + unit[i]
 
         def body(step, state):
-            place, olds = state[:3], state[3:]
-            terms = use(olds)
-            found, news, place = find(step, place)
-            add(olds, terms)
-            keep(found)
-            return place + news
+            place, middle, old = state[:3], state[3 : 3 + 2 * UNITS], state[3 + 2 * UNITS :]
+            terms = use(old)
+            weighed = weigh()
+            found, new, place = find(step, place)
+            add(old, terms)
+            keep(weighed, 2)
+            keep(found, 0)
+            return place + new + middle
 
         zero = jnp.int32(0)
-        found, units, place = find(0, (zero, zero, zero))
-        keep(found)
-        state = lax.fori_loop(1, lax.div(self.total + UNITS - 1, UNITS), body, place + units)
-        add(state[3:], use(state[3:]))
+        found, old, place = find(0, (zero, zero, zero))
+        keep(found, 0)
+        weighed = weigh()
+        found, new, place = find(1, place)
+        keep(weighed, 2)
+        keep(found, 0)
+        steps = lax.shift_right_logical(self.total + (UNITS - 1), UNITS.bit_length() - 1)
+        state = lax.fori_loop(2, steps, body, place + new + old)
+        middle, old = state[3 : 3 + 2 * UNITS], state[3 + 2 * UNITS :]
+        terms = use(old)
+        weighed = weigh()
+        add(old, terms)
+        keep(weighed, 2)
+        add(middle, use(middle))
 
 
 def is_full(cells, count_ref):
@@ -405,7 +423,7 @@
     def params(mib):
         return pltpu.CompilerParams(vmem_limit_bytes=mib << 20)
 
-    loop_scratch = [pltpu.VMEM((UNITS, 2, CHUNK, LANES), jnp.float32)]
+    loop_scratch = [pltpu.VMEM((UNITS, 4, CHUNK, LANES), jnp.float32)]
     loop_scratch += [pltpu.SMEM((2 * n_bins,), jnp.int32)] * 5
     cost = pl.CostEstimate(flops=1 << 28, bytes_accessed=1 << 16, transcendentals=1 << 20)
 

time: 25.8 us -> 26.2 us (1.016); the launches traced: 25.9 us -> 26 us
  starting transfers between devices: 3.32 us -> 3.81 us
  waiting for transfers between devices: 1.88 us -> 1.49 us
    ppermute x4, waiting for transfers between devices: 0.78 us -> 0.26 us  [shifted(): lax.ppermute(jnp.where(odd == bool(parity), last, first), axis, pairs)]
    ppermute x4, starting transfers between devices: 3.25 us -> 3.74 us  [shifted(): lax.ppermute(jnp.where(odd == bool(parity), last, first), axis, pairs)]
    pallas_call x1, Pallas kernels: 3.45 us -> 3.72 us  [on_device(): pl.pallas_call(functools.partial(second_kernel, cells), out_shape=floats(...]
  transfers between devices with their start and end apart: 5 -> 5, of which waited for: 3 -> 2; matrix products, arithmetic and copies ran while one was open for 0% -> 0% of each run, Pallas kernels for 40% -> 40%
where the time goes in v5:
time: 26.2 us; the launch traced here: 26 us
  Pallas kernels  20.5 us (78%)
  starting transfers between devices  3.81 us (15%)
  waiting for transfers between devices  1.49 us (6%)
    pallas_call x1, Pallas kernels, on_device(): pl.pallas_call(functools.partial(last_kernel, cells), out_shape=floats(3,...  6.15 us
    pallas_call x1, Pallas kernels, on_device(): pl.pallas_call(functools.partial(middle_kernel, cells), out_shape=floats(...  4.1 us
    pallas_call x1, Pallas kernels, on_device(): pl.pallas_call(functools.partial(pack_kernel, cells), out_shape=[floats(*...  3.85 us
    ppermute x4, starting transfers between devices, shifted(): lax.ppermute(jnp.where(odd == bool(parity), last, first), axis, pairs)  3.74 us
    pallas_call x1, Pallas kernels, on_device(): pl.pallas_call(functools.partial(second_kernel, cells), out_shape=floats(...  3.72 us
    pallas_call x1, Pallas kernels, on_device(): pl.pallas_call(functools.partial(first_kernel, cells), out_shape=[sent, o...  2.65 us
    ppermute x1, waiting for transfers between devices, on_device(): other = lax.ppermute(sent, 'ha', [(i, (i + 1) % size) for i in range(size)])  1.24 us
  transfers between devices with their start and end apart: 5, of which 2 were waited for; matrix products, arithmetic and copies ran while one was open for 0% of the time, Pallas kernels for 40%

profile of v5, /device:TPU:0, one launch (start us, length us, event | category | flops | bytes accessed | tf_op | source)
XLA Modules:
  0.0 26.0 jit_solution(12399396464397430845)
XLA Ops:
  0.0 0.0 copy-start
  0.0 3.9 %pack.1 = (f32[2,2,2,8,128]{4,3,2,1,0:T(8,128)S(1)}, f32[3,8,128]{2,1,0:T(8,128)S(1)}) custom-call(s32[2,2,2]{2,1,0:T(2,128)} %count_ref.5, f32[3,2,2,2,128]{4,3,2,1,0:T(2,128)} %offset_hbm.1, f32[3,2,2,2,128]{4,3,2,1,0:T(2,128)} %force_hbm.1), custom_call_target="tpu_custom_call" | custom-call | tf_op jit(solution)/shard_map/pack/pallas_call | solution.py:435
  3.9 0.1 collective-permute-start
  4.0 2.7 %first.1 = (f32[2,2,2,8,128]{4,3,2,1,0:T(8,128)S(1)}, f32[9,8,128]{2,1,0:T(8,128)S(1)}, f32[3,1024,128]{2,1,0:T(8,128)S(1)}, f32[4,416,128]{2,1,0:T(8,128)S(1)}) custom-call(f32[2,2,2,8,128]{4,3,2,1,0:T(8,128)S(1)} %get-tuple-element.21.sent_ref), custom_call_target="tpu_custom_call" | custom-call | flops 268435456 | bytes 65536 | tf_op jit(solution)/shard_map/first/pallas_call | solution.py:458
  6.6 1.2 %collective-permute-done.other = f32[2,2,2,8,128]{4,3,2,1,0:T(8,128)S(1)} collective-permute-done((f32[2,2,2,8,128]{4,3,2,1,0:T(8,128)S(1)}, f32[2,2,2,8,128]{4,3,2,1,0:T(8,128)S(1)}, u32[]{:S(2)}, u32[]{:S(2)}) %collective-permute-start) | collective-permute-done | bytes 32800 | tf_op jit(solution)/shard_map/ppermute | solution.py:457
  7.9 2.1 %collective-permute-start.1 = (f32[1,2,4,8,128]{4,3,2,1,0:T(8,128)S(1)}, f32[1,2,4,8,128]{4,3,2,1,0:T(8,128)S(1)}, u32[]{:S(2)}, u32[]{:S(2)}) collective-permute-start(f32[1,2,4,8,128]{4,3,2,1,0:T(8,128)S(1)} %get-tuple-element.44), channel_id=1, source_target_pairs={{8,16},{16,8},{24,0},{0,24},{9,17},{17,9},{25,1},{1,25},{10,18},{1... | collective-permute-start | bytes 98312 | tf_op jit(solution)/shard_map/ppermute | solution.py:408
  10.0 0.0 collective-permute-start.2
  10.0 0.0 copy-done
  10.0 3.7 %second.1 = f32[4,1056,128]{2,1,0:T(8,128)S(1)} custom-call(s32[2,2,2]{2,1,0:T(2,128)S(1)} %copy-done, f32[2,2,2,8,128]{4,3,2,1,0:T(8,128)S(1)} %collective-permute-done.other, f32[9,8,128]{2,1,0:T(8,128)S(1)} %get-tuple-element.27.own_list, f32[3,1024,128]{2,1,0:T(8,128)S(1)} %get-tuple-element.28.spread, f32[4,416,128]{2,1,0:T(8,128)S(1)} %get-tuple-element.29.first), custom_call_target="tpu_custom_call" | custom-call | flops 268435456 | bytes 65536 | tf_op jit(solution)/shard_map/second/pallas_call | solution.py:471
  13.7 0.0 collective-permute-done.1
  13.8 0.2 collective-permute-done.2
  14.1 0.1 collective-permute-start.3
  14.1 1.5 %collective-permute-start.4 = (f32[4,1,4,8,128]{4,3,2,1,0:T(8,128)S(1)}, f32[4,1,4,8,128]{4,3,2,1,0:T(8,128)S(1)}, u32[]{:S(2)}, u32[]{:S(2)}) collective-permute-start(f32[4,1,4,8,128]{4,3,2,1,0:T(8,128)S(1)} %get-tuple-element.39), channel_id=1, source_target_pairs={{2,4},{4,2},{6,0},{0,6},{3,5},{5,3},{7,1},{1,7},{10,12},{12,10},{1... | collective-permute-start | bytes 196616 | tf_op jit(solution)/shard_map/ppermute | solution.py:408
  15.7 4.1 %middle.1.refs_0_ = f32[4,1056,128]{2,1,0:T(8,128)S(1)} custom-call(s32[2,2,2]{2,1,0:T(2,128)S(1)} %copy-done, f32[4,2,4,8,128]{4,3,2,1,0:T(8,128)S(1)} %pad_maximum_fusion.wide, f32[3,1024,128]{2,1,0:T(8,128)S(1)} %get-tuple-element.28.spread, f32[4,1056,128]{2,1,0:T(8,128)S(1)} %second.1), custom_call_target="tpu_custom_call" | custom-call | flops 268435456 | bytes 65536 | tf_op jit(solution)/shard_map/middle/pallas_call | solution.py:485
  19.8 0.0 collective-permute-done.3
  19.8 0.0 collective-permute-done.4
  19.8 6.2 %last.1 = f32[3,2,2,2,128]{4,3,2,1,0:T(2,128)} custom-call(s32[2,2,2]{2,1,0:T(2,128)S(1)} %copy-done, f32[2,2,2,8,128]{4,3,2,1,0:T(8,128)S(1)} %get-tuple-element.25.own_ref, f32[4,1,4,8,128]{4,3,2,1,0:T(8,128)S(1)} %get-tuple-element.33.y_lo, f32[4,1,4,8,128]{4,3,2,1,0:T(8,128)S(1)} %get-tuple-element.34.y_hi, ...), custom_call_target="tpu_custom_call" | custom-call | flops 268435456 | bytes 65536 | tf_op jit(solution)/shard_map/last/pallas_call | solution.py:496
  (7 shorter events, 0.1 us)
Async XLA Ops:
  0.0 10.0 %copy-start = (s32[2,2,2]{2,1,0:T(2,128)S(1)}, s32[2,2,2]{2,1,0:T(2,128)}, u32[]{:S(2)}) copy-start(s32[2,2,2]{2,1,0:T(2,128)} %count_ref.5) | copy-start | bytes 100
  3.9 4.0 %collective-permute-start = (f32[2,2,2,8,128]{4,3,2,1,0:T(8,128)S(1)}, f32[2,2,2,8,128]{4,3,2,1,0:T(8,128)S(1)}, u32[]{:S(2)}, u32[]{:S(2)}) collective-permute-start(f32[2,2,2,8,128]{4,3,2,1,0:T(8,128)S(1)} %get-tuple-element.21.sent_ref), channel_id=1, source_target_pairs={{0,1},{1,0},{2,3},{3,2},{4,5},{5,4},{6,7},{7,6},{8,9},{9,8},{10,11... | collective-permute-start | bytes 98312 | tf_op jit(solution)/shard_map/ppermute | solution.py:457
  7.9 5.9 %collective-permute-start.1 = (f32[1,2,4,8,128]{4,3,2,1,0:T(8,128)S(1)}, f32[1,2,4,8,128]{4,3,2,1,0:T(8,128)S(1)}, u32[]{:S(2)}, u32[]{:S(2)}) collective-permute-start(f32[1,2,4,8,128]{4,3,2,1,0:T(8,128)S(1)} %get-tuple-element.44), channel_id=1, source_target_pairs={{8,16},{16,8},{24,0},{0,24},{9,17},{17,9},{25,1},{1,25},{10,18},{1... | collective-permute-start | bytes 98312 | tf_op jit(solution)/shard_map/ppermute | solution.py:408
  10.0 4.0 %collective-permute-start.2 = (f32[1,2,4,8,128]{4,3,2,1,0:T(8,128)S(1)}, f32[1,2,4,8,128]{4,3,2,1,0:T(8,128)S(1)}, u32[]{:S(2)}, u32[]{:S(2)}) collective-permute-start(f32[1,2,4,8,128]{4,3,2,1,0:T(8,128)S(1)} %get-tuple-element.43), channel_id=1, source_target_pairs={{0,8},{8,0},{16,24},{24,16},{1,9},{9,1},{17,25},{25,17},{2,10},{10... | collective-permute-start | bytes 98312 | tf_op jit(solution)/shard_map/ppermute | solution.py:408
  14.1 5.7 %collective-permute-start.3 = (f32[4,1,4,8,128]{4,3,2,1,0:T(8,128)S(1)}, f32[4,1,4,8,128]{4,3,2,1,0:T(8,128)S(1)}, u32[]{:S(2)}, u32[]{:S(2)}) collective-permute-start(f32[4,1,4,8,128]{4,3,2,1,0:T(8,128)S(1)} %get-tuple-element.40), channel_id=1, source_target_pairs={{0,2},{2,0},{4,6},{6,4},{1,3},{3,1},{5,7},{7,5},{8,10},{10,8},{12,... | collective-permute-start | bytes 196616 | tf_op jit(solution)/shard_map/ppermute | solution.py:408
  14.1 5.7 %collective-permute-start.4 = (f32[4,1,4,8,128]{4,3,2,1,0:T(8,128)S(1)}, f32[4,1,4,8,128]{4,3,2,1,0:T(8,128)S(1)}, u32[]{:S(2)}, u32[]{:S(2)}) collective-permute-start(f32[4,1,4,8,128]{4,3,2,1,0:T(8,128)S(1)} %get-tuple-element.39), channel_id=1, source_target_pairs={{2,4},{4,2},{6,0},{0,6},{3,5},{5,3},{7,1},{1,7},{10,12},{12,10},{1... | collective-permute-start | bytes 196616 | tf_op jit(solution)/shard_map/ppermute | solution.py:408

commit v6 on v4

--- a/solution.py
+++ b/solution.py
@@ -317,13 +317,12 @@
     work.run(listed, spread, coefs, acc)
 
 
-def middle_kernel(cells, count_ref, wide, spread, second, acc, listed, coefs, *tables):
+def middle_kernel(cells, count_ref, wide, spread, _, acc, listed, coefs, *tables):
     size_x, size_y, size_z = cells
     n_z = 2 * size_z
     bins = bins_of(cells)
     places = [(i, j, k) for i in (0, size_x + 1) for j in range(size_y) for k in range(n_z)]
     count_s = counts_of([wide[at] for at in places])
-    acc[...] = second[...]
     work = Groups(tables)
     for bx in range(size_x):
         for bz in range(size_z):
@@ -343,14 +342,13 @@
 
 
 def last_kernel(cells, count_ref, own_ref, y_lo, y_hi, spread, *refs):
-    (middle, early, out_ref, acc, listed, coefs), tables = refs[:6], refs[6:]
+    (_, early, out_ref, acc, listed, coefs), tables = refs[:6], refs[6:]
     size_x, size_y, size_z = cells
     n_z = 2 * size_z
     bins = bins_of(cells)
     places = [(i, j, k) for i in range(size_x + 2) for j in range(2) for k in range(n_z)]
     tiles = [(y_lo, y_hi)[j][i, 0, k] for i, j, k in places]
     count_s = counts_of(tiles)
-    acc[...] = middle[...]
     work = Groups(tables)
     for n, (bx, by, bz) in enumerate(bins):
         sources = []
@@ -408,6 +406,9 @@
     loop_scratch = [pltpu.VMEM((UNITS, 2, CHUNK, LANES), jnp.float32)]
     loop_scratch += [pltpu.SMEM((2 * n_bins,), jnp.int32)] * 5
     cost = pl.CostEstimate(flops=1 << 28, bytes_accessed=1 << 16, transcendentals=1 << 20)
+
+    def in_place(sums):
+        return pltpu.with_memory_space_constraint(sums, pltpu.VMEM)
 
     def list_scratch(n_tiles):
         return [pltpu.VMEM((n_tiles, ROWS, LANES), jnp.float32)]
@@ -470,23 +471,24 @@
         in_specs=[scalars] + [whole] * 3,
         out_specs=whole,
         scratch_shapes=list_scratch(cells[0] * cells[2] * LIST_X) + loop_scratch,
+        input_output_aliases={3: 0},
         compiler_params=params(8),
         cost_estimate=cost,
         name="middle",
-    )(counts, wide, spread, second)
+    )(counts, wide, spread, in_place(second))
     y_lo, y_hi, middle = together((y_lo, y_hi, middle))
     return pl.pallas_call(
         functools.partial(last_kernel, cells),
-        out_shape=floats(3, *cells, slots),
+        out_shape=[floats(3, *cells, slots), floats(4, n_targets + CHUNK, slots)],
         in_specs=[scalars] + [whole] * 6,
-        out_specs=whole,
-        scratch_shapes=[pltpu.VMEM((4, n_targets + CHUNK, slots), jnp.float32)]
-        + list_scratch(n_bins * LIST_Y)
+        out_specs=[whole, whole],
+        scratch_shapes=list_scratch(n_bins * LIST_Y)
         + loop_scratch,
+        input_output_aliases={5: 1},
         compiler_params=params(12),
         cost_estimate=cost,
         name="last",
-    )(counts, own, y_lo, y_hi, spread, middle, early)
+    )(counts, own, y_lo, y_hi, spread, in_place(middle), early)[0]
 
 
 def solution(mesh):

time: 25.8 us -> 25.8 us (level)
  Pallas kernels: 20.5 us -> 18.2 us
  starting transfers between devices: 3.32 us -> 5.6 us
    ppermute x4, starting transfers between devices: 3.25 us -> 5.32 us  [shifted(): lax.ppermute(jnp.where(odd == bool(parity), last, first), axis, pairs)]
    pallas_call x1, Pallas kernels: 4.17 us -> 3.15 us  [on_device(): pl.pallas_call(functools.partial(middle_kernel, cells), out_shape=floats(...]
    pallas_call x1, Pallas kernels: 2.79 us -> 1.92 us  [on_device(): pl.pallas_call(functools.partial(first_kernel, cells), out_shape=[sent, o...]
    ppermute x4, waiting for transfers between devices: 0.78 us -> 0.06 us  [shifted(): lax.ppermute(jnp.where(odd == bool(parity), last, first), axis, pairs)]
    ppermute x1, waiting for transfers between devices: 1.1 us -> 1.77 us  [on_device(): other = lax.ppermute(sent, 'ha', [(i, (i + 1) % size) for i in range(size)])]
    pallas_call x1, Pallas kernels: 4.1 us -> 3.63 us  [on_device(): pl.pallas_call(functools.partial(pack_kernel, cells), out_shape=[floats(*...]
    pallas_call x1, Pallas kernels: 6 us -> 6.32 us  [on_device(): pl.pallas_call(functools.partial(last_kernel, cells), out_shape=[floats(3...]
    pallas_call x1, Pallas kernels: 3.45 us -> 3.17 us  [on_device(): pl.pallas_call(functools.partial(second_kernel, cells), out_shape=floats(...]
  transfers between devices with their start and end apart: 5 -> 5, of which waited for: 3 -> 1; matrix products, arithmetic and copies ran while one was open for 0% -> 0% of each run, Pallas kernels for 40% -> 32%
where the time goes in v6:
time: 25.8 us
  Pallas kernels  18.2 us (71%)
  starting transfers between devices  5.6 us (22%)
  waiting for transfers between devices  1.82 us (7%)
    pallas_call x1, Pallas kernels, on_device(): pl.pallas_call(functools.partial(last_kernel, cells), out_shape=[floats(3...  6.32 us
    ppermute x4, starting transfers between devices, shifted(): lax.ppermute(jnp.where(odd == bool(parity), last, first), axis, pairs)  5.32 us
    pallas_call x1, Pallas kernels, on_device(): pl.pallas_call(functools.partial(pack_kernel, cells), out_shape=[floats(*...  3.63 us
    pallas_call x1, Pallas kernels, on_device(): pl.pallas_call(functools.partial(second_kernel, cells), out_shape=floats(...  3.17 us
    pallas_call x1, Pallas kernels, on_device(): pl.pallas_call(functools.partial(middle_kernel, cells), out_shape=floats(...  3.15 us
    pallas_call x1, Pallas kernels, on_device(): pl.pallas_call(functools.partial(first_kernel, cells), out_shape=[sent, o...  1.92 us
    ppermute x1, waiting for transfers between devices, on_device(): other = lax.ppermute(sent, 'ha', [(i, (i + 1) % size) for i in range(size)])  1.77 us
  transfers between devices with their start and end apart: 5, of which 1 were waited for; matrix products, arithmetic and copies ran while one was open for 0% of the time, Pallas kernels for 32%

profile of v6, /device:TPU:0, one launch (start us, length us, event | category | flops | bytes accessed | tf_op | source)
XLA Modules:
  0.0 25.8 jit_solution(8159588869171879570)
XLA Ops:
  0.0 0.0 copy-start
  0.0 3.6 %pack.1 = (f32[2,2,2,8,128]{4,3,2,1,0:T(8,128)S(1)}, f32[3,8,128]{2,1,0:T(8,128)S(1)}) custom-call(s32[2,2,2]{2,1,0:T(2,128)} %count_ref.5, f32[3,2,2,2,128]{4,3,2,1,0:T(2,128)} %offset_hbm.1, f32[3,2,2,2,128]{4,3,2,1,0:T(2,128)} %force_hbm.1), custom_call_target="tpu_custom_call" | custom-call | tf_op jit(solution)/shard_map/pack/pallas_call | solution.py:418
  3.6 0.3 %collective-permute-start = (f32[2,2,2,8,128]{4,3,2,1,0:T(8,128)S(1)}, f32[2,2,2,8,128]{4,3,2,1,0:T(8,128)S(1)}, u32[]{:S(2)}, u32[]{:S(2)}) collective-permute-start(f32[2,2,2,8,128]{4,3,2,1,0:T(8,128)S(1)} %get-tuple-element.22.sent_ref), channel_id=1, source_target_pairs={{0,1},{1,0},{2,3},{3,2},{4,5},{5,4},{6,7},{7,6},{8,9},{9,8},{10,11... | collective-permute-start | bytes 98312 | tf_op jit(solution)/shard_map/ppermute | solution.py:440
  3.9 1.9 %first.1 = (f32[2,2,2,8,128]{4,3,2,1,0:T(8,128)S(1)}, f32[9,8,128]{2,1,0:T(8,128)S(1)}, f32[3,1024,128]{2,1,0:T(8,128)S(1)}, f32[4,416,128]{2,1,0:T(8,128)S(1)}) custom-call(f32[2,2,2,8,128]{4,3,2,1,0:T(8,128)S(1)} %get-tuple-element.22.sent_ref), custom_call_target="tpu_custom_call" | custom-call | flops 268435456 | bytes 65536 | tf_op jit(solution)/shard_map/first/pallas_call | solution.py:441
  5.8 1.8 %collective-permute-done.other = f32[2,2,2,8,128]{4,3,2,1,0:T(8,128)S(1)} collective-permute-done((f32[2,2,2,8,128]{4,3,2,1,0:T(8,128)S(1)}, f32[2,2,2,8,128]{4,3,2,1,0:T(8,128)S(1)}, u32[]{:S(2)}, u32[]{:S(2)}) %collective-permute-start) | collective-permute-done | bytes 32800 | tf_op jit(solution)/shard_map/ppermute | solution.py:440
  7.7 0.3 %collective-permute-start.2 = (f32[1,2,4,8,128]{4,3,2,1,0:T(8,128)S(1)}, f32[1,2,4,8,128]{4,3,2,1,0:T(8,128)S(1)}, u32[]{:S(2)}, u32[]{:S(2)}) collective-permute-start(f32[1,2,4,8,128]{4,3,2,1,0:T(8,128)S(1)} %get-tuple-element.45), channel_id=1, source_target_pairs={{0,8},{8,0},{16,24},{24,16},{1,9},{9,1},{17,25},{25,17},{2,10},{10... | collective-permute-start | bytes 98312 | tf_op jit(solution)/shard_map/ppermute | solution.py:388
  8.0 2.5 %collective-permute-start.1 = (f32[1,2,4,8,128]{4,3,2,1,0:T(8,128)S(1)}, f32[1,2,4,8,128]{4,3,2,1,0:T(8,128)S(1)}, u32[]{:S(2)}, u32[]{:S(2)}) collective-permute-start(f32[1,2,4,8,128]{4,3,2,1,0:T(8,128)S(1)} %get-tuple-element.46), channel_id=1, source_target_pairs={{8,16},{16,8},{24,0},{0,24},{9,17},{17,9},{25,1},{1,25},{10,18},{1... | collective-permute-start | bytes 98312 | tf_op jit(solution)/shard_map/ppermute | solution.py:388
  10.5 0.0 copy-done
  10.5 3.2 %second.1._ = f32[4,1056,128]{2,1,0:T(8,128)S(1)} custom-call(s32[2,2,2]{2,1,0:T(2,128)S(1)} %copy-done, f32[2,2,2,8,128]{4,3,2,1,0:T(8,128)S(1)} %collective-permute-done.other, f32[9,8,128]{2,1,0:T(8,128)S(1)} %get-tuple-element.28.own_list, f32[3,1024,128]{2,1,0:T(8,128)S(1)} %get-tuple-element.29.spread, f32[4,416,128]{2,1,0:T(8,128)S(1)} %get-tuple-element.30.first), custom_call_target="tpu_custom_call" | custom-call | flops 268435456 | bytes 65536 | tf_op jit(solution)/shard_map/second/pallas_call | solution.py:454
  13.6 0.0 collective-permute-done.2
  13.7 0.0 collective-permute-done.1
  13.8 0.1 collective-permute-start.4
  13.8 2.4 %collective-permute-start.3 = (f32[4,1,4,8,128]{4,3,2,1,0:T(8,128)S(1)}, f32[4,1,4,8,128]{4,3,2,1,0:T(8,128)S(1)}, u32[]{:S(2)}, u32[]{:S(2)}) collective-permute-start(f32[4,1,4,8,128]{4,3,2,1,0:T(8,128)S(1)} %get-tuple-element.42), channel_id=1, source_target_pairs={{0,2},{2,0},{4,6},{6,4},{1,3},{3,1},{5,7},{7,5},{8,10},{10,8},{12,... | collective-permute-start | bytes 196616 | tf_op jit(solution)/shard_map/ppermute | solution.py:388
  16.3 3.1 %middle.1.refs_0_ = f32[4,1056,128]{2,1,0:T(8,128)S(1)} custom-call(s32[2,2,2]{2,1,0:T(2,128)S(1)} %copy-done, f32[4,2,4,8,128]{4,3,2,1,0:T(8,128)S(1)} %pad_maximum_fusion.wide, f32[3,1024,128]{2,1,0:T(8,128)S(1)} %get-tuple-element.29.spread, f32[4,1056,128]{2,1,0:T(8,128)S(1)} %second.1._), custom_call_target="tpu_custom_call", output_to_operand_aliasing={{}: (3, {})} | custom-call | flops 268435456 | bytes 65536 | tf_op jit(solution)/shard_map/middle/pallas_call | solution.py:468
  19.4 0.0 collective-permute-done.4
  19.4 0.0 collective-permute-done.3
  19.5 6.3 %last.1 = (f32[3,2,2,2,128]{4,3,2,1,0:T(2,128)}, f32[4,1056,128]{2,1,0:T(8,128)S(1)}) custom-call(s32[2,2,2]{2,1,0:T(2,128)S(1)} %copy-done, f32[2,2,2,8,128]{4,3,2,1,0:T(8,128)S(1)} %get-tuple-element.26.own_ref, f32[4,1,4,8,128]{4,3,2,1,0:T(8,128)S(1)} %get-tuple-element.34.y_lo, ...), custom_call_target="tpu_custom_call", output_to_operand_aliasing={{1}: (5, {})} | custom-call | flops 268435456 | bytes 65536 | tf_op jit(solution)/shard_map/last/pallas_call | solution.py:480
  (7 shorter events, 0.1 us)
Async XLA Ops:
  0.0 10.5 %copy-start = (s32[2,2,2]{2,1,0:T(2,128)S(1)}, s32[2,2,2]{2,1,0:T(2,128)}, u32[]{:S(2)}) copy-start(s32[2,2,2]{2,1,0:T(2,128)} %count_ref.5) | copy-start | bytes 100
  3.6 4.0 %collective-permute-start = (f32[2,2,2,8,128]{4,3,2,1,0:T(8,128)S(1)}, f32[2,2,2,8,128]{4,3,2,1,0:T(8,128)S(1)}, u32[]{:S(2)}, u32[]{:S(2)}) collective-permute-start(f32[2,2,2,8,128]{4,3,2,1,0:T(8,128)S(1)} %get-tuple-element.22.sent_ref), channel_id=1, source_target_pairs={{0,1},{1,0},{2,3},{3,2},{4,5},{5,4},{6,7},{7,6},{8,9},{9,8},{10,11... | collective-permute-start | bytes 98312 | tf_op jit(solution)/shard_map/ppermute | solution.py:440
  7.7 6.0 %collective-permute-start.2 = (f32[1,2,4,8,128]{4,3,2,1,0:T(8,128)S(1)}, f32[1,2,4,8,128]{4,3,2,1,0:T(8,128)S(1)}, u32[]{:S(2)}, u32[]{:S(2)}) collective-permute-start(f32[1,2,4,8,128]{4,3,2,1,0:T(8,128)S(1)} %get-tuple-element.45), channel_id=1, source_target_pairs={{0,8},{8,0},{16,24},{24,16},{1,9},{9,1},{17,25},{25,17},{2,10},{10... | collective-permute-start | bytes 98312 | tf_op jit(solution)/shard_map/ppermute | solution.py:388
  8.0 5.7 %collective-permute-start.1 = (f32[1,2,4,8,128]{4,3,2,1,0:T(8,128)S(1)}, f32[1,2,4,8,128]{4,3,2,1,0:T(8,128)S(1)}, u32[]{:S(2)}, u32[]{:S(2)}) collective-permute-start(f32[1,2,4,8,128]{4,3,2,1,0:T(8,128)S(1)} %get-tuple-element.46), channel_id=1, source_target_pairs={{8,16},{16,8},{24,0},{0,24},{9,17},{17,9},{25,1},{1,25},{10,18},{1... | collective-permute-start | bytes 98312 | tf_op jit(solution)/shard_map/ppermute | solution.py:388
  13.8 5.7 %collective-permute-start.4 = (f32[4,1,4,8,128]{4,3,2,1,0:T(8,128)S(1)}, f32[4,1,4,8,128]{4,3,2,1,0:T(8,128)S(1)}, u32[]{:S(2)}, u32[]{:S(2)}) collective-permute-start(f32[4,1,4,8,128]{4,3,2,1,0:T(8,128)S(1)} %get-tuple-element.41), channel_id=1, source_target_pairs={{2,4},{4,2},{6,0},{0,6},{3,5},{5,3},{7,1},{1,7},{10,12},{12,10},{1... | collective-permute-start | bytes 196616 | tf_op jit(solution)/shard_map/ppermute | solution.py:388
  13.8 5.6 %collective-permute-start.3 = (f32[4,1,4,8,128]{4,3,2,1,0:T(8,128)S(1)}, f32[4,1,4,8,128]{4,3,2,1,0:T(8,128)S(1)}, u32[]{:S(2)}, u32[]{:S(2)}) collective-permute-start(f32[4,1,4,8,128]{4,3,2,1,0:T(8,128)S(1)} %get-tuple-element.42), channel_id=1, source_target_pairs={{0,2},{2,0},{4,6},{6,4},{1,3},{3,1},{5,7},{7,5},{8,10},{10,8},{12,... | collective-permute-start | bytes 196616 | tf_op jit(solution)/shard_map/ppermute | solution.py:388

commit v7 on v6

--- a/solution.py
+++ b/solution.py
@@ -199,14 +199,13 @@
 
 
 def lane_sums(sums, n_bins):
-    row, lane = rows_and_lanes((2 * LANES, LANES))
-    merged = jnp.zeros(sums[0].shape, jnp.float32)
-    for i, part in enumerate(sums):
-        merged = merged + jnp.dot(
-            jnp.concatenate(parts_of(part, 2), axis=1),
-            jnp.where(lax.bitwise_and(lane, ROWS - 1) == i, 1.0, 0.0).astype(jnp.bfloat16),
-            preferred_element_type=jnp.float32,
-        )
+    row, lane = rows_and_lanes((2 * LANES * len(sums), LANES))
+    pick = lax.bitwise_and(lane, ROWS - 1) == lax.shift_right_logical(row, (2 * LANES).bit_length() - 1)
+    merged = jnp.dot(
+        jnp.concatenate([p for part in sums for p in parts_of(part, 2)], axis=1),
+        jnp.where(pick, 1.0, 0.0).astype(jnp.bfloat16),
+        preferred_element_type=jnp.float32,
+    )
     _, lane = rows_and_lanes((LANES, LANES))
     chosen = merged[:LANES]
     for n in range(1, n_bins):
@@ -462,7 +461,7 @@
         cost_estimate=cost,
         name="second",
     )(counts, other, listed, spread, first)
-    x_hi, x_lo, second = together((x_hi, x_lo, second))
+    x_lo, x_hi, second = together((x_lo, x_hi, second))
     wide = jnp.concatenate([x_lo, column, x_hi], axis=0)
     y_lo, y_hi = shifted(wide[:, :1], wide[:, cells[1] - 1 :], "gy")
     middle = pl.pallas_call(

time: 25.8 us -> 25.6 us (level); the launches traced: 25.8 us -> 25.9 us
  Pallas kernels: 18.2 us -> 19.3 us
  starting transfers between devices: 5.6 us -> 4.9 us
  waiting for transfers between devices: 1.82 us -> 1.47 us
    pallas_call x1, Pallas kernels: 3.17 us -> 3.83 us  [on_device(): pl.pallas_call(functools.partial(second_kernel, cells), out_shape=floats(...]
    pallas_call x1, Pallas kernels: 1.92 us -> 2.58 us  [on_device(): pl.pallas_call(functools.partial(first_kernel, cells), out_shape=[sent, o...]
    ppermute x4, starting transfers between devices: 5.32 us -> 4.82 us  [shifted(): lax.ppermute(jnp.where(odd == bool(parity), last, first), axis, pairs)]
    ppermute x1, waiting for transfers between devices: 1.77 us -> 1.31 us  [on_device(): other = lax.ppermute(sent, 'ha', [(i, (i + 1) % size) for i in range(size)])]
  transfers between devices with their start and end apart: 5 -> 5, of which waited for: 1 -> 2; matrix products, arithmetic and copies ran while one was open for 0% -> 0% of each run, Pallas kernels for 32% -> 36%
where the time goes in v7:
time: 25.6 us; the launch traced here: 25.9 us
  Pallas kernels  19.3 us (75%)
  starting transfers between devices  4.9 us (19%)
  waiting for transfers between devices  1.47 us (6%)
    pallas_call x1, Pallas kernels, on_device(): pl.pallas_call(functools.partial(last_kernel, cells), out_shape=[floats(3...  6.13 us
    ppermute x4, starting transfers between devices, shifted(): lax.ppermute(jnp.where(odd == bool(parity), last, first), axis, pairs)  4.82 us
    pallas_call x1, Pallas kernels, on_device(): pl.pallas_call(functools.partial(pack_kernel, cells), out_shape=[floats(*...  3.86 us
    pallas_call x1, Pallas kernels, on_device(): pl.pallas_call(functools.partial(second_kernel, cells), out_shape=floats(...  3.83 us
    pallas_call x1, Pallas kernels, on_device(): pl.pallas_call(functools.partial(middle_kernel, cells), out_shape=floats(...  2.94 us
    pallas_call x1, Pallas kernels, on_device(): pl.pallas_call(functools.partial(first_kernel, cells), out_shape=[sent, o...  2.58 us
    ppermute x1, waiting for transfers between devices, on_device(): other = lax.ppermute(sent, 'ha', [(i, (i + 1) % size) for i in range(size)])  1.31 us
  transfers between devices with their start and end apart: 5, of which 2 were waited for; matrix products, arithmetic and copies ran while one was open for 0% of the time, Pallas kernels for 36%

profile of v7, /device:TPU:0, one launch (start us, length us, event | category | flops | bytes accessed | tf_op | source)
XLA Modules:
  0.0 25.9 jit_solution(2608538480787161362)
XLA Ops:
  0.0 0.0 copy-start
  0.0 3.9 %pack.1 = (f32[2,2,2,8,128]{4,3,2,1,0:T(8,128)S(1)}, f32[3,8,128]{2,1,0:T(8,128)S(1)}) custom-call(s32[2,2,2]{2,1,0:T(2,128)} %count_ref.5, f32[3,2,2,2,128]{4,3,2,1,0:T(2,128)} %offset_hbm.1, f32[3,2,2,2,128]{4,3,2,1,0:T(2,128)} %force_hbm.1), custom_call_target="tpu_custom_call" | custom-call | tf_op jit(solution)/shard_map/pack/pallas_call | solution.py:417
  3.9 0.1 collective-permute-start
  4.0 2.6 %first.1 = (f32[2,2,2,8,128]{4,3,2,1,0:T(8,128)S(1)}, f32[9,8,128]{2,1,0:T(8,128)S(1)}, f32[3,1024,128]{2,1,0:T(8,128)S(1)}, f32[4,416,128]{2,1,0:T(8,128)S(1)}) custom-call(f32[2,2,2,8,128]{4,3,2,1,0:T(8,128)S(1)} %get-tuple-element.22.sent_ref), custom_call_target="tpu_custom_call" | custom-call | flops 268435456 | bytes 65536 | tf_op jit(solution)/shard_map/first/pallas_call | solution.py:440
  6.5 1.3 %collective-permute-done.other = f32[2,2,2,8,128]{4,3,2,1,0:T(8,128)S(1)} collective-permute-done((f32[2,2,2,8,128]{4,3,2,1,0:T(8,128)S(1)}, f32[2,2,2,8,128]{4,3,2,1,0:T(8,128)S(1)}, u32[]{:S(2)}, u32[]{:S(2)}) %collective-permute-start) | collective-permute-done | bytes 32800 | tf_op jit(solution)/shard_map/ppermute | solution.py:439
  7.9 2.1 %collective-permute-start.2 = (f32[1,2,4,8,128]{4,3,2,1,0:T(8,128)S(1)}, f32[1,2,4,8,128]{4,3,2,1,0:T(8,128)S(1)}, u32[]{:S(2)}, u32[]{:S(2)}) collective-permute-start(f32[1,2,4,8,128]{4,3,2,1,0:T(8,128)S(1)} %get-tuple-element.45), channel_id=1, source_target_pairs={{8,16},{16,8},{24,0},{0,24},{9,17},{17,9},{25,1},{1,25},{10,18},{1... | collective-permute-start | bytes 98312 | tf_op jit(solution)/shard_map/ppermute | solution.py:387
  10.0 0.0 collective-permute-start.1
  10.0 0.0 copy-done
  10.0 3.8 %second.1._ = f32[4,1056,128]{2,1,0:T(8,128)S(1)} custom-call(s32[2,2,2]{2,1,0:T(2,128)S(1)} %copy-done, f32[2,2,2,8,128]{4,3,2,1,0:T(8,128)S(1)} %collective-permute-done.other, f32[9,8,128]{2,1,0:T(8,128)S(1)} %get-tuple-element.28.own_list, f32[3,1024,128]{2,1,0:T(8,128)S(1)} %get-tuple-element.29.spread, f32[4,416,128]{2,1,0:T(8,128)S(1)} %get-tuple-element.30.first), custom_call_target="tpu_custom_call" | custom-call | flops 268435456 | bytes 65536 | tf_op jit(solution)/shard_map/second/pallas_call | solution.py:453
  13.9 0.0 collective-permute-done.2
  13.9 0.1 collective-permute-done.1
  14.1 0.1 collective-permute-start.4
  14.1 2.6 %collective-permute-start.3 = (f32[4,1,4,8,128]{4,3,2,1,0:T(8,128)S(1)}, f32[4,1,4,8,128]{4,3,2,1,0:T(8,128)S(1)}, u32[]{:S(2)}, u32[]{:S(2)}) collective-permute-start(f32[4,1,4,8,128]{4,3,2,1,0:T(8,128)S(1)} %get-tuple-element.42), channel_id=1, source_target_pairs={{0,2},{2,0},{4,6},{6,4},{1,3},{3,1},{5,7},{7,5},{8,10},{10,8},{12,... | collective-permute-start | bytes 196616 | tf_op jit(solution)/shard_map/ppermute | solution.py:387
  16.8 2.9 %middle.1.refs_0_ = f32[4,1056,128]{2,1,0:T(8,128)S(1)} custom-call(s32[2,2,2]{2,1,0:T(2,128)S(1)} %copy-done, f32[4,2,4,8,128]{4,3,2,1,0:T(8,128)S(1)} %pad_maximum_fusion.wide, f32[3,1024,128]{2,1,0:T(8,128)S(1)} %get-tuple-element.29.spread, f32[4,1056,128]{2,1,0:T(8,128)S(1)} %second.1._), custom_call_target="tpu_custom_call", output_to_operand_aliasing={{}: (3, {})} | custom-call | flops 268435456 | bytes 65536 | tf_op jit(solution)/shard_map/middle/pallas_call | solution.py:467
  19.7 0.0 collective-permute-done.4
  19.7 0.0 collective-permute-done.3
  19.8 6.1 %last.1 = (f32[3,2,2,2,128]{4,3,2,1,0:T(2,128)}, f32[4,1056,128]{2,1,0:T(8,128)S(1)}) custom-call(s32[2,2,2]{2,1,0:T(2,128)S(1)} %copy-done, f32[2,2,2,8,128]{4,3,2,1,0:T(8,128)S(1)} %get-tuple-element.26.own_ref, f32[4,1,4,8,128]{4,3,2,1,0:T(8,128)S(1)} %get-tuple-element.34.y_lo, ...), custom_call_target="tpu_custom_call", output_to_operand_aliasing={{1}: (5, {})} | custom-call | flops 268435456 | bytes 65536 | tf_op jit(solution)/shard_map/last/pallas_call | solution.py:479
  (7 shorter events, 0.1 us)
Async XLA Ops:
  0.0 10.0 %copy-start = (s32[2,2,2]{2,1,0:T(2,128)S(1)}, s32[2,2,2]{2,1,0:T(2,128)}, u32[]{:S(2)}) copy-start(s32[2,2,2]{2,1,0:T(2,128)} %count_ref.5) | copy-start | bytes 100
  3.9 4.0 %collective-permute-start = (f32[2,2,2,8,128]{4,3,2,1,0:T(8,128)S(1)}, f32[2,2,2,8,128]{4,3,2,1,0:T(8,128)S(1)}, u32[]{:S(2)}, u32[]{:S(2)}) collective-permute-start(f32[2,2,2,8,128]{4,3,2,1,0:T(8,128)S(1)} %get-tuple-element.22.sent_ref), channel_id=1, source_target_pairs={{0,1},{1,0},{2,3},{3,2},{4,5},{5,4},{6,7},{7,6},{8,9},{9,8},{10,11... | collective-permute-start | bytes 98312 | tf_op jit(solution)/shard_map/ppermute | solution.py:439
  7.9 6.0 %collective-permute-start.2 = (f32[1,2,4,8,128]{4,3,2,1,0:T(8,128)S(1)}, f32[1,2,4,8,128]{4,3,2,1,0:T(8,128)S(1)}, u32[]{:S(2)}, u32[]{:S(2)}) collective-permute-start(f32[1,2,4,8,128]{4,3,2,1,0:T(8,128)S(1)} %get-tuple-element.45), channel_id=1, source_target_pairs={{8,16},{16,8},{24,0},{0,24},{9,17},{17,9},{25,1},{1,25},{10,18},{1... | collective-permute-start | bytes 98312 | tf_op jit(solution)/shard_map/ppermute | solution.py:387
  10.0 4.0 %collective-permute-start.1 = (f32[1,2,4,8,128]{4,3,2,1,0:T(8,128)S(1)}, f32[1,2,4,8,128]{4,3,2,1,0:T(8,128)S(1)}, u32[]{:S(2)}, u32[]{:S(2)}) collective-permute-start(f32[1,2,4,8,128]{4,3,2,1,0:T(8,128)S(1)} %get-tuple-element.46), channel_id=1, source_target_pairs={{0,8},{8,0},{16,24},{24,16},{1,9},{9,1},{17,25},{25,17},{2,10},{10... | collective-permute-start | bytes 98312 | tf_op jit(solution)/shard_map/ppermute | solution.py:387
  14.1 5.6 %collective-permute-start.4 = (f32[4,1,4,8,128]{4,3,2,1,0:T(8,128)S(1)}, f32[4,1,4,8,128]{4,3,2,1,0:T(8,128)S(1)}, u32[]{:S(2)}, u32[]{:S(2)}) collective-permute-start(f32[4,1,4,8,128]{4,3,2,1,0:T(8,128)S(1)} %get-tuple-element.41), channel_id=1, source_target_pairs={{2,4},{4,2},{6,0},{0,6},{3,5},{5,3},{7,1},{1,7},{10,12},{12,10},{1... | collective-permute-start | bytes 196616 | tf_op jit(solution)/shard_map/ppermute | solution.py:387
  14.1 5.6 %collective-permute-start.3 = (f32[4,1,4,8,128]{4,3,2,1,0:T(8,128)S(1)}, f32[4,1,4,8,128]{4,3,2,1,0:T(8,128)S(1)}, u32[]{:S(2)}, u32[]{:S(2)}) collective-permute-start(f32[4,1,4,8,128]{4,3,2,1,0:T(8,128)S(1)} %get-tuple-element.42), channel_id=1, source_target_pairs={{0,2},{2,0},{4,6},{6,4},{1,3},{3,1},{5,7},{7,5},{8,10},{10,8},{12,... | collective-permute-start | bytes 196616 | tf_op jit(solution)/shard_map/ppermute | solution.py:387

commit v8 on v7

--- a/solution.py
+++ b/solution.py
@@ -25,7 +25,6 @@
 CHUNK = 32
 UNITS = 8
 COUNT_ROW = 3
-FULL = 700
 MANY = 440
 EARLY = 3
 FIRST = (3, 4, 5)
@@ -183,9 +182,12 @@
 
 def is_full(cells, count_ref):
     filled = jnp.int32(0)
+    heavy = jnp.int32(0)
     for at in bins_of(cells):
-        filled = filled + count_ref[at]
-    return filled, filled > FULL, filled > MANY
+        count = count_ref[at]
+        filled = filled + count
+        heavy = heavy + jnp.where(count > LANES // 2, 1, 0)
+    return filled, heavy == len(bins_of(cells)), filled > MANY
 
 
 def list_own(cells, count_ref, own_ref, listed):

time: 25.6 us -> 24.3 us (0.949); the launches traced: 25.9 us -> 24.1 us
  Pallas kernels: 19.3 us -> 17.6 us
  starting transfers between devices: 4.9 us -> 5.23 us
  waiting for transfers between devices: 1.47 us -> 1.17 us
    pallas_call x1, Pallas kernels: 6.13 us -> 4.83 us  [on_device(): pl.pallas_call(functools.partial(last_kernel, cells), out_shape=[floats(3...]
    pallas_call x1, Pallas kernels: 3.86 us -> 3.17 us  [on_device(): pl.pallas_call(functools.partial(pack_kernel, cells), out_shape=[floats(*...]
    ppermute x1, starting transfers between devices: 0.07 us -> 0.74 us  [on_device(): other = lax.ppermute(sent, 'ha', [(i, (i + 1) % size) for i in range(size)])]
    pallas_call x1, Pallas kernels: 2.94 us -> 3.58 us  [on_device(): pl.pallas_call(functools.partial(middle_kernel, cells), out_shape=floats(...]
    ppermute x1, waiting for transfers between devices: 1.31 us -> 0.88 us  [on_device(): other = lax.ppermute(sent, 'ha', [(i, (i + 1) % size) for i in range(size)])]
    ppermute x4, starting transfers between devices: 4.82 us -> 4.49 us  [shifted(): lax.ppermute(jnp.where(odd == bool(parity), last, first), axis, pairs)]
  transfers between devices with their start and end apart: 5 -> 5, of which waited for: 2 -> 2; matrix products, arithmetic and copies ran while one was open for 0% -> 0% of each run, Pallas kernels for 36% -> 40%
where the time goes in v8:
time: 24.3 us; the launch traced here: 24.1 us
  Pallas kernels  17.6 us (72%)
  starting transfers between devices  5.23 us (22%)
  waiting for transfers between devices  1.17 us (5%)
    pallas_call x1, Pallas kernels, on_device(): pl.pallas_call(functools.partial(last_kernel, cells), out_shape=[floats(3...  4.83 us
    ppermute x4, starting transfers between devices, shifted(): lax.ppermute(jnp.where(odd == bool(parity), last, first), axis, pairs)  4.49 us
    pallas_call x1, Pallas kernels, on_device(): pl.pallas_call(functools.partial(second_kernel, cells), out_shape=floats(...  3.61 us
    pallas_call x1, Pallas kernels, on_device(): pl.pallas_call(functools.partial(middle_kernel, cells), out_shape=floats(...  3.58 us
    pallas_call x1, Pallas kernels, on_device(): pl.pallas_call(functools.partial(pack_kernel, cells), out_shape=[floats(*...  3.17 us
    pallas_call x1, Pallas kernels, on_device(): pl.pallas_call(functools.partial(first_kernel, cells), out_shape=[sent, o...  2.35 us
    ppermute x1, waiting for transfers between devices, on_device(): other = lax.ppermute(sent, 'ha', [(i, (i + 1) % size) for i in range(size)])  0.88 us
    ppermute x1, starting transfers between devices, on_device(): other = lax.ppermute(sent, 'ha', [(i, (i + 1) % size) for i in range(size)])  0.74 us
  transfers between devices with their start and end apart: 5, of which 2 were waited for; matrix products, arithmetic and copies ran while one was open for 0% of the time, Pallas kernels for 40%

profile of v8, /device:TPU:0, one launch (start us, length us, event | category | flops | bytes accessed | tf_op | source)
XLA Modules:
  0.0 24.1 jit_solution(11696870449762733621)
XLA Ops:
  0.0 0.0 copy-start
  0.0 3.2 %pack.1 = (f32[2,2,2,8,128]{4,3,2,1,0:T(8,128)S(1)}, f32[3,8,128]{2,1,0:T(8,128)S(1)}) custom-call(s32[2,2,2]{2,1,0:T(2,128)} %count_ref.5, f32[3,2,2,2,128]{4,3,2,1,0:T(2,128)} %offset_hbm.1, f32[3,2,2,2,128]{4,3,2,1,0:T(2,128)} %force_hbm.1), custom_call_target="tpu_custom_call" | custom-call | tf_op jit(solution)/shard_map/pack/pallas_call | solution.py:419
  3.2 0.7 %collective-permute-start = (f32[2,2,2,8,128]{4,3,2,1,0:T(8,128)S(1)}, f32[2,2,2,8,128]{4,3,2,1,0:T(8,128)S(1)}, u32[]{:S(2)}, u32[]{:S(2)}) collective-permute-start(f32[2,2,2,8,128]{4,3,2,1,0:T(8,128)S(1)} %get-tuple-element.22.sent_ref), channel_id=1, source_target_pairs={{0,1},{1,0},{2,3},{3,2},{4,5},{5,4},{6,7},{7,6},{8,9},{9,8},{10,11... | collective-permute-start | bytes 98312 | tf_op jit(solution)/shard_map/ppermute | solution.py:441
  3.9 2.4 %first.1 = (f32[2,2,2,8,128]{4,3,2,1,0:T(8,128)S(1)}, f32[9,8,128]{2,1,0:T(8,128)S(1)}, f32[3,1024,128]{2,1,0:T(8,128)S(1)}, f32[4,416,128]{2,1,0:T(8,128)S(1)}) custom-call(f32[2,2,2,8,128]{4,3,2,1,0:T(8,128)S(1)} %get-tuple-element.22.sent_ref), custom_call_target="tpu_custom_call" | custom-call | flops 268435456 | bytes 65536 | tf_op jit(solution)/shard_map/first/pallas_call | solution.py:442
  6.3 0.9 %collective-permute-done.other = f32[2,2,2,8,128]{4,3,2,1,0:T(8,128)S(1)} collective-permute-done((f32[2,2,2,8,128]{4,3,2,1,0:T(8,128)S(1)}, f32[2,2,2,8,128]{4,3,2,1,0:T(8,128)S(1)}, u32[]{:S(2)}, u32[]{:S(2)}) %collective-permute-start) | collective-permute-done | bytes 32800 | tf_op jit(solution)/shard_map/ppermute | solution.py:441
  7.2 2.8 %collective-permute-start.2 = (f32[1,2,4,8,128]{4,3,2,1,0:T(8,128)S(1)}, f32[1,2,4,8,128]{4,3,2,1,0:T(8,128)S(1)}, u32[]{:S(2)}, u32[]{:S(2)}) collective-permute-start(f32[1,2,4,8,128]{4,3,2,1,0:T(8,128)S(1)} %get-tuple-element.45), channel_id=1, source_target_pairs={{8,16},{16,8},{24,0},{0,24},{9,17},{17,9},{25,1},{1,25},{10,18},{1... | collective-permute-start | bytes 98312 | tf_op jit(solution)/shard_map/ppermute | solution.py:389
  10.0 0.0 collective-permute-start.1
  10.0 0.0 copy-done
  10.0 3.6 %second.1._ = f32[4,1056,128]{2,1,0:T(8,128)S(1)} custom-call(s32[2,2,2]{2,1,0:T(2,128)S(1)} %copy-done, f32[2,2,2,8,128]{4,3,2,1,0:T(8,128)S(1)} %collective-permute-done.other, f32[9,8,128]{2,1,0:T(8,128)S(1)} %get-tuple-element.28.own_list, f32[3,1024,128]{2,1,0:T(8,128)S(1)} %get-tuple-element.29.spread, f32[4,416,128]{2,1,0:T(8,128)S(1)} %get-tuple-element.30.first), custom_call_target="tpu_custom_call" | custom-call | flops 268435456 | bytes 65536 | tf_op jit(solution)/shard_map/second/pallas_call | solution.py:455
  13.6 0.0 collective-permute-done.2
  13.6 0.3 %collective-permute-done.1 = f32[1,2,4,8,128]{4,3,2,1,0:T(8,128)S(1)} collective-permute-done((f32[1,2,4,8,128]{4,3,2,1,0:T(8,128)S(1)}, f32[1,2,4,8,128]{4,3,2,1,0:T(8,128)S(1)}, u32[]{:S(2)}, u32[]{:S(2)}) %collective-permute-start.1) | collective-permute-done | bytes 32800 | tf_op jit(solution)/shard_map/ppermute | solution.py:389
  14.0 0.1 collective-permute-start.4
  14.1 1.6 %collective-permute-start.3 = (f32[4,1,4,8,128]{4,3,2,1,0:T(8,128)S(1)}, f32[4,1,4,8,128]{4,3,2,1,0:T(8,128)S(1)}, u32[]{:S(2)}, u32[]{:S(2)}) collective-permute-start(f32[4,1,4,8,128]{4,3,2,1,0:T(8,128)S(1)} %get-tuple-element.42), channel_id=1, source_target_pairs={{0,2},{2,0},{4,6},{6,4},{1,3},{3,1},{5,7},{7,5},{8,10},{10,8},{12,... | collective-permute-start | bytes 196616 | tf_op jit(solution)/shard_map/ppermute | solution.py:389
  15.7 3.6 %middle.1.refs_0_ = f32[4,1056,128]{2,1,0:T(8,128)S(1)} custom-call(s32[2,2,2]{2,1,0:T(2,128)S(1)} %copy-done, f32[4,2,4,8,128]{4,3,2,1,0:T(8,128)S(1)} %pad_maximum_fusion.wide, f32[3,1024,128]{2,1,0:T(8,128)S(1)} %get-tuple-element.29.spread, f32[4,1056,128]{2,1,0:T(8,128)S(1)} %second.1._), custom_call_target="tpu_custom_call", output_to_operand_aliasing={{}: (3, {})} | custom-call | flops 268435456 | bytes 65536 | tf_op jit(solution)/shard_map/middle/pallas_call | solution.py:469
  19.2 0.0 collective-permute-done.4
  19.3 0.0 collective-permute-done.3
  19.3 4.8 %last.1 = (f32[3,2,2,2,128]{4,3,2,1,0:T(2,128)}, f32[4,1056,128]{2,1,0:T(8,128)S(1)}) custom-call(s32[2,2,2]{2,1,0:T(2,128)S(1)} %copy-done, f32[2,2,2,8,128]{4,3,2,1,0:T(8,128)S(1)} %get-tuple-element.26.own_ref, f32[4,1,4,8,128]{4,3,2,1,0:T(8,128)S(1)} %get-tuple-element.34.y_lo, ...), custom_call_target="tpu_custom_call", output_to_operand_aliasing={{1}: (5, {})} | custom-call | flops 268435456 | bytes 65536 | tf_op jit(solution)/shard_map/last/pallas_call | solution.py:481
  (7 shorter events, 0.1 us)
Async XLA Ops:
  0.0 10.0 %copy-start = (s32[2,2,2]{2,1,0:T(2,128)S(1)}, s32[2,2,2]{2,1,0:T(2,128)}, u32[]{:S(2)}) copy-start(s32[2,2,2]{2,1,0:T(2,128)} %count_ref.5) | copy-start | bytes 100
  3.2 4.0 %collective-permute-start = (f32[2,2,2,8,128]{4,3,2,1,0:T(8,128)S(1)}, f32[2,2,2,8,128]{4,3,2,1,0:T(8,128)S(1)}, u32[]{:S(2)}, u32[]{:S(2)}) collective-permute-start(f32[2,2,2,8,128]{4,3,2,1,0:T(8,128)S(1)} %get-tuple-element.22.sent_ref), channel_id=1, source_target_pairs={{0,1},{1,0},{2,3},{3,2},{4,5},{5,4},{6,7},{7,6},{8,9},{9,8},{10,11... | collective-permute-start | bytes 98312 | tf_op jit(solution)/shard_map/ppermute | solution.py:441
  7.2 6.4 %collective-permute-start.2 = (f32[1,2,4,8,128]{4,3,2,1,0:T(8,128)S(1)}, f32[1,2,4,8,128]{4,3,2,1,0:T(8,128)S(1)}, u32[]{:S(2)}, u32[]{:S(2)}) collective-permute-start(f32[1,2,4,8,128]{4,3,2,1,0:T(8,128)S(1)} %get-tuple-element.45), channel_id=1, source_target_pairs={{8,16},{16,8},{24,0},{0,24},{9,17},{17,9},{25,1},{1,25},{10,18},{1... | collective-permute-start | bytes 98312 | tf_op jit(solution)/shard_map/ppermute | solution.py:389
  10.0 3.9 %collective-permute-start.1 = (f32[1,2,4,8,128]{4,3,2,1,0:T(8,128)S(1)}, f32[1,2,4,8,128]{4,3,2,1,0:T(8,128)S(1)}, u32[]{:S(2)}, u32[]{:S(2)}) collective-permute-start(f32[1,2,4,8,128]{4,3,2,1,0:T(8,128)S(1)} %get-tuple-element.46), channel_id=1, source_target_pairs={{0,8},{8,0},{16,24},{24,16},{1,9},{9,1},{17,25},{25,17},{2,10},{10... | collective-permute-start | bytes 98312 | tf_op jit(solution)/shard_map/ppermute | solution.py:389
  14.0 5.3 %collective-permute-start.4 = (f32[4,1,4,8,128]{4,3,2,1,0:T(8,128)S(1)}, f32[4,1,4,8,128]{4,3,2,1,0:T(8,128)S(1)}, u32[]{:S(2)}, u32[]{:S(2)}) collective-permute-start(f32[4,1,4,8,128]{4,3,2,1,0:T(8,128)S(1)} %get-tuple-element.41), channel_id=1, source_target_pairs={{2,4},{4,2},{6,0},{0,6},{3,5},{5,3},{7,1},{1,7},{10,12},{12,10},{1... | collective-permute-start | bytes 196616 | tf_op jit(solution)/shard_map/ppermute | solution.py:389
  14.1 5.2 %collective-permute-start.3 = (f32[4,1,4,8,128]{4,3,2,1,0:T(8,128)S(1)}, f32[4,1,4,8,128]{4,3,2,1,0:T(8,128)S(1)}, u32[]{:S(2)}, u32[]{:S(2)}) collective-permute-start(f32[4,1,4,8,128]{4,3,2,1,0:T(8,128)S(1)} %get-tuple-element.42), channel_id=1, source_target_pairs={{0,2},{2,0},{4,6},{6,4},{1,3},{3,1},{5,7},{7,5},{8,10},{10,8},{12,... | collective-permute-start | bytes 196616 | tf_op jit(solution)/shard_map/ppermute | solution.py:389

commit v9 on v8

--- a/solution.py
+++ b/solution.py
@@ -23,7 +23,7 @@
 LANES = 128
 ROWS = 8
 CHUNK = 32
-UNITS = 8
+UNITS = 4
 COUNT_ROW = 3
 MANY = 440
 EARLY = 3
@@ -203,15 +203,17 @@
 def lane_sums(sums, n_bins):
     row, lane = rows_and_lanes((2 * LANES * len(sums), LANES))
     pick = lax.bitwise_and(lane, ROWS - 1) == lax.shift_right_logical(row, (2 * LANES).bit_length() - 1)
-    merged = jnp.dot(
-        jnp.concatenate([p for part in sums for p in parts_of(part, 2)], axis=1),
-        jnp.where(pick, 1.0, 0.0).astype(jnp.bfloat16),
-        preferred_element_type=jnp.float32,
-    )
+    pick = jnp.where(pick, 1.0, 0.0).astype(jnp.bfloat16)
+    middle = n_bins // 2 * LANES
+    merged = []
+    for rows in (slice(0, middle), slice(middle, n_bins * LANES)):
+        parts = [p for part in sums for p in parts_of(part[rows], 2)]
+        product = jnp.dot(jnp.concatenate(parts, axis=1), pick, preferred_element_type=jnp.float32)
+        merged += [product[n : n + LANES] for n in range(0, product.shape[0], LANES)]
     _, lane = rows_and_lanes((LANES, LANES))
-    chosen = merged[:LANES]
+    chosen = merged[0]
     for n in range(1, n_bins):
-        chosen = jnp.where(lane >= n * ROWS, merged[n * LANES : (n + 1) * LANES], chosen)
+        chosen = jnp.where(lane >= n * ROWS, merged[n], chosen)
     turned = jnp.transpose(chosen)
     return [turned[n * ROWS : (n + 1) * ROWS] for n in range(n_bins)]
 

time: 24.3 us -> 24.1 us (level)
  waiting for transfers between devices: 1.17 us -> 1.74 us
  Pallas kernels: 17.6 us -> 17.2 us
  starting transfers between devices: 5.23 us -> 4.84 us
    pallas_call x1, Pallas kernels: 3.58 us -> 2.94 us  [on_device(): pl.pallas_call(functools.partial(middle_kernel, cells), out_shape=floats(...]
    pallas_call x1, Pallas kernels: 4.83 us -> 5.34 us  [on_device(): pl.pallas_call(functools.partial(last_kernel, cells), out_shape=[floats(3...]
    ppermute x1, waiting for transfers between devices: 0.88 us -> 1.27 us  [on_device(): other = lax.ppermute(sent, 'ha', [(i, (i + 1) % size) for i in range(size)])]
  transfers between devices with their start and end apart: 5 -> 5, of which waited for: 2 -> 2; matrix products, arithmetic and copies ran while one was open for 0% -> 0% of each run, Pallas kernels for 40% -> 35%
where the time goes in v9:
time: 24.1 us; the launch traced here: 24 us
  Pallas kernels  17.2 us (71%)
  starting transfers between devices  4.84 us (20%)
  waiting for transfers between devices  1.74 us (7%)
    pallas_call x1, Pallas kernels, on_device(): pl.pallas_call(functools.partial(last_kernel, cells), out_shape=[floats(3...  5.34 us
    ppermute x4, starting transfers between devices, shifted(): lax.ppermute(jnp.where(odd == bool(parity), last, first), axis, pairs)  4.3 us
    pallas_call x1, Pallas kernels, on_device(): pl.pallas_call(functools.partial(second_kernel, cells), out_shape=floats(...  3.43 us
    pallas_call x1, Pallas kernels, on_device(): pl.pallas_call(functools.partial(pack_kernel, cells), out_shape=[floats(*...  3.36 us
    pallas_call x1, Pallas kernels, on_device(): pl.pallas_call(functools.partial(middle_kernel, cells), out_shape=floats(...  2.94 us
    pallas_call x1, Pallas kernels, on_device(): pl.pallas_call(functools.partial(first_kernel, cells), out_shape=[sent, o...  2.15 us
    ppermute x1, waiting for transfers between devices, on_device(): other = lax.ppermute(sent, 'ha', [(i, (i + 1) % size) for i in range(size)])  1.27 us
    ppermute x1, starting transfers between devices, on_device(): other = lax.ppermute(sent, 'ha', [(i, (i + 1) % size) for i in range(size)])  0.55 us
  transfers between devices with their start and end apart: 5, of which 2 were waited for; matrix products, arithmetic and copies ran while one was open for 0% of the time, Pallas kernels for 35%

profile of v9, /device:TPU:0, one launch (start us, length us, event | category | flops | bytes accessed | tf_op | source)
XLA Modules:
  0.0 24.0 jit_solution(3819224023018943426)
XLA Ops:
  0.0 0.0 copy-start
  0.0 3.4 %pack.1 = (f32[2,2,2,8,128]{4,3,2,1,0:T(8,128)S(1)}, f32[3,8,128]{2,1,0:T(8,128)S(1)}) custom-call(s32[2,2,2]{2,1,0:T(2,128)} %count_ref.5, f32[3,2,2,2,128]{4,3,2,1,0:T(2,128)} %offset_hbm.1, f32[3,2,2,2,128]{4,3,2,1,0:T(2,128)} %force_hbm.1), custom_call_target="tpu_custom_call" | custom-call | tf_op jit(solution)/shard_map/pack/pallas_call | solution.py:421
  3.4 0.5 %collective-permute-start = (f32[2,2,2,8,128]{4,3,2,1,0:T(8,128)S(1)}, f32[2,2,2,8,128]{4,3,2,1,0:T(8,128)S(1)}, u32[]{:S(2)}, u32[]{:S(2)}) collective-permute-start(f32[2,2,2,8,128]{4,3,2,1,0:T(8,128)S(1)} %get-tuple-element.22.sent_ref), channel_id=1, source_target_pairs={{0,1},{1,0},{2,3},{3,2},{4,5},{5,4},{6,7},{7,6},{8,9},{9,8},{10,11... | collective-permute-start | bytes 98312 | tf_op jit(solution)/shard_map/ppermute | solution.py:443
  3.9 2.2 %first.1 = (f32[2,2,2,8,128]{4,3,2,1,0:T(8,128)S(1)}, f32[9,8,128]{2,1,0:T(8,128)S(1)}, f32[3,1024,128]{2,1,0:T(8,128)S(1)}, f32[4,416,128]{2,1,0:T(8,128)S(1)}) custom-call(f32[2,2,2,8,128]{4,3,2,1,0:T(8,128)S(1)} %get-tuple-element.22.sent_ref), custom_call_target="tpu_custom_call" | custom-call | flops 268435456 | bytes 65536 | tf_op jit(solution)/shard_map/first/pallas_call | solution.py:444
  6.1 1.3 %collective-permute-done.other = f32[2,2,2,8,128]{4,3,2,1,0:T(8,128)S(1)} collective-permute-done((f32[2,2,2,8,128]{4,3,2,1,0:T(8,128)S(1)}, f32[2,2,2,8,128]{4,3,2,1,0:T(8,128)S(1)}, u32[]{:S(2)}, u32[]{:S(2)}) %collective-permute-start) | collective-permute-done | bytes 32800 | tf_op jit(solution)/shard_map/ppermute | solution.py:443
  7.4 2.6 %collective-permute-start.2 = (f32[1,2,4,8,128]{4,3,2,1,0:T(8,128)S(1)}, f32[1,2,4,8,128]{4,3,2,1,0:T(8,128)S(1)}, u32[]{:S(2)}, u32[]{:S(2)}) collective-permute-start(f32[1,2,4,8,128]{4,3,2,1,0:T(8,128)S(1)} %get-tuple-element.45), channel_id=1, source_target_pairs={{8,16},{16,8},{24,0},{0,24},{9,17},{17,9},{25,1},{1,25},{10,18},{1... | collective-permute-start | bytes 98312 | tf_op jit(solution)/shard_map/ppermute | solution.py:391
  10.0 0.0 collective-permute-start.1
  10.0 0.0 copy-done
  10.0 3.4 %second.1._ = f32[4,1056,128]{2,1,0:T(8,128)S(1)} custom-call(s32[2,2,2]{2,1,0:T(2,128)S(1)} %copy-done, f32[2,2,2,8,128]{4,3,2,1,0:T(8,128)S(1)} %collective-permute-done.other, f32[9,8,128]{2,1,0:T(8,128)S(1)} %get-tuple-element.28.own_list, f32[3,1024,128]{2,1,0:T(8,128)S(1)} %get-tuple-element.29.spread, f32[4,416,128]{2,1,0:T(8,128)S(1)} %get-tuple-element.30.first), custom_call_target="tpu_custom_call" | custom-call | flops 268435456 | bytes 65536 | tf_op jit(solution)/shard_map/second/pallas_call | solution.py:457
  13.5 0.0 collective-permute-done.2
  13.5 0.5 %collective-permute-done.1 = f32[1,2,4,8,128]{4,3,2,1,0:T(8,128)S(1)} collective-permute-done((f32[1,2,4,8,128]{4,3,2,1,0:T(8,128)S(1)}, f32[1,2,4,8,128]{4,3,2,1,0:T(8,128)S(1)}, u32[]{:S(2)}, u32[]{:S(2)}) %collective-permute-start.1) | collective-permute-done | bytes 32800 | tf_op jit(solution)/shard_map/ppermute | solution.py:391
  14.0 0.1 collective-permute-start.4
  14.1 1.6 %collective-permute-start.3 = (f32[4,1,4,8,128]{4,3,2,1,0:T(8,128)S(1)}, f32[4,1,4,8,128]{4,3,2,1,0:T(8,128)S(1)}, u32[]{:S(2)}, u32[]{:S(2)}) collective-permute-start(f32[4,1,4,8,128]{4,3,2,1,0:T(8,128)S(1)} %get-tuple-element.42), channel_id=1, source_target_pairs={{0,2},{2,0},{4,6},{6,4},{1,3},{3,1},{5,7},{7,5},{8,10},{10,8},{12,... | collective-permute-start | bytes 196616 | tf_op jit(solution)/shard_map/ppermute | solution.py:391
  15.7 2.9 %middle.1.refs_0_ = f32[4,1056,128]{2,1,0:T(8,128)S(1)} custom-call(s32[2,2,2]{2,1,0:T(2,128)S(1)} %copy-done, f32[4,2,4,8,128]{4,3,2,1,0:T(8,128)S(1)} %pad_maximum_fusion.wide, f32[3,1024,128]{2,1,0:T(8,128)S(1)} %get-tuple-element.29.spread, f32[4,1056,128]{2,1,0:T(8,128)S(1)} %second.1._), custom_call_target="tpu_custom_call", output_to_operand_aliasing={{}: (3, {})} | custom-call | flops 268435456 | bytes 65536 | tf_op jit(solution)/shard_map/middle/pallas_call | solution.py:471
  18.6 0.0 collective-permute-done.4
  18.6 0.0 collective-permute-done.3
  18.6 5.3 %last.1 = (f32[3,2,2,2,128]{4,3,2,1,0:T(2,128)}, f32[4,1056,128]{2,1,0:T(8,128)S(1)}) custom-call(s32[2,2,2]{2,1,0:T(2,128)S(1)} %copy-done, f32[2,2,2,8,128]{4,3,2,1,0:T(8,128)S(1)} %get-tuple-element.26.own_ref, f32[4,1,4,8,128]{4,3,2,1,0:T(8,128)S(1)} %get-tuple-element.34.y_lo, ...), custom_call_target="tpu_custom_call", output_to_operand_aliasing={{1}: (5, {})} | custom-call | flops 268435456 | bytes 65536 | tf_op jit(solution)/shard_map/last/pallas_call | solution.py:483
  (7 shorter events, 0.1 us)
Async XLA Ops:
  0.0 10.0 %copy-start = (s32[2,2,2]{2,1,0:T(2,128)S(1)}, s32[2,2,2]{2,1,0:T(2,128)}, u32[]{:S(2)}) copy-start(s32[2,2,2]{2,1,0:T(2,128)} %count_ref.5) | copy-start | bytes 100
  3.4 4.0 %collective-permute-start = (f32[2,2,2,8,128]{4,3,2,1,0:T(8,128)S(1)}, f32[2,2,2,8,128]{4,3,2,1,0:T(8,128)S(1)}, u32[]{:S(2)}, u32[]{:S(2)}) collective-permute-start(f32[2,2,2,8,128]{4,3,2,1,0:T(8,128)S(1)} %get-tuple-element.22.sent_ref), channel_id=1, source_target_pairs={{0,1},{1,0},{2,3},{3,2},{4,5},{5,4},{6,7},{7,6},{8,9},{9,8},{10,11... | collective-permute-start | bytes 98312 | tf_op jit(solution)/shard_map/ppermute | solution.py:443
  7.4 6.1 %collective-permute-start.2 = (f32[1,2,4,8,128]{4,3,2,1,0:T(8,128)S(1)}, f32[1,2,4,8,128]{4,3,2,1,0:T(8,128)S(1)}, u32[]{:S(2)}, u32[]{:S(2)}) collective-permute-start(f32[1,2,4,8,128]{4,3,2,1,0:T(8,128)S(1)} %get-tuple-element.45), channel_id=1, source_target_pairs={{8,16},{16,8},{24,0},{0,24},{9,17},{17,9},{25,1},{1,25},{10,18},{1... | collective-permute-start | bytes 98312 | tf_op jit(solution)/shard_map/ppermute | solution.py:391
  10.0 3.9 %collective-permute-start.1 = (f32[1,2,4,8,128]{4,3,2,1,0:T(8,128)S(1)}, f32[1,2,4,8,128]{4,3,2,1,0:T(8,128)S(1)}, u32[]{:S(2)}, u32[]{:S(2)}) collective-permute-start(f32[1,2,4,8,128]{4,3,2,1,0:T(8,128)S(1)} %get-tuple-element.46), channel_id=1, source_target_pairs={{0,8},{8,0},{16,24},{24,16},{1,9},{9,1},{17,25},{25,17},{2,10},{10... | collective-permute-start | bytes 98312 | tf_op jit(solution)/shard_map/ppermute | solution.py:391
  14.0 4.6 %collective-permute-start.4 = (f32[4,1,4,8,128]{4,3,2,1,0:T(8,128)S(1)}, f32[4,1,4,8,128]{4,3,2,1,0:T(8,128)S(1)}, u32[]{:S(2)}, u32[]{:S(2)}) collective-permute-start(f32[4,1,4,8,128]{4,3,2,1,0:T(8,128)S(1)} %get-tuple-element.41), channel_id=1, source_target_pairs={{2,4},{4,2},{6,0},{0,6},{3,5},{5,3},{7,1},{1,7},{10,12},{12,10},{1... | collective-permute-start | bytes 196616 | tf_op jit(solution)/shard_map/ppermute | solution.py:391
  14.1 4.5 %collective-permute-start.3 = (f32[4,1,4,8,128]{4,3,2,1,0:T(8,128)S(1)}, f32[4,1,4,8,128]{4,3,2,1,0:T(8,128)S(1)}, u32[]{:S(2)}, u32[]{:S(2)}) collective-permute-start(f32[4,1,4,8,128]{4,3,2,1,0:T(8,128)S(1)} %get-tuple-element.42), channel_id=1, source_target_pairs={{0,2},{2,0},{4,6},{6,4},{1,3},{3,1},{5,7},{7,5},{8,10},{10,8},{12,... | collective-permute-start | bytes 196616 | tf_op jit(solution)/shard_map/ppermute | solution.py:391
